TPU v7x, 128 devices: a whole 4x4x4 slice. The times are simulated.
128 devices in a mesh: pipe: 2 (over z_lo), dp: 16 (over z_hi, y, core), tensor: 4 (over x).
Axes of the slice: x: 4, y: 4, z: 4 (z_hi: 2, z_lo: 2; z = z_hi * 2 + z_lo), core: 2. Of those that a mesh axis runs over, the one named last changes fastest.
Arguments:
- inputs: bfloat16 [32, 1024, 1024], P('dp', 'tensor'), may hold values from -6 to 6
- out_grad: bfloat16 [32, 1024, 1024], P('dp', 'tensor'), may hold values from -6 to 6
- norm_gain: float32 [2, 1024], P('pipe'), may hold values from 0.5 to 1.5
- in_gate_x: bfloat16 [2, 1024, 2, 2048], P('pipe', 'dp', None, 'tensor'), may hold values from -0.1875 to 0.1875
- in_read_write: bfloat16 [2, 1024, 256], P('pipe', 'dp'), may hold values from -0.1875 to 0.1875
- in_step: bfloat16 [2, 1024, 32], P('pipe', 'dp', 'tensor'), may hold values from -0.1875 to 0.1875
- conv_main: float32 [2, 5, 2048], P('pipe', None, 'tensor'), may hold values from -3 to 3
- conv_state: float32 [2, 5, 256], P('pipe'), may hold values from -3 to 3
- step_bias: float32 [2, 32], P('pipe', 'tensor'), may hold values from -9 to -3
- log_rate: float32 [2, 32], P('pipe', 'tensor'), may hold values from 0 to 2.77
- skip_gain: float32 [2, 32], P('pipe', 'tensor'), may hold values from 0.5 to 1.5
- gate_gain: float32 [2, 2048], P('pipe', 'tensor'), may hold values from 0.5 to 1.5
- out_weight: bfloat16 [2, 1024, 2048], P('pipe', 'dp', 'tensor'), may hold values from -0.125 to 0.125
Outputs:
- activations: float32 [2, 32, 1024, 1024], P('pipe', 'dp', 'tensor')
- input_grads: float32 [2, 32, 1024, 1024], P('pipe', 'dp', 'tensor')
- grad_norm_gain: float32 [2, 1024], P('pipe')
- grad_in_gate_x: float32 [2, 1024, 2, 2048], P('pipe', 'dp', None, 'tensor')
- grad_in_read_write: float32 [2, 1024, 256], P('pipe', ('dp', 'tensor'))
- grad_in_step: float32 [2, 1024, 32], P('pipe', 'dp', 'tensor')
- grad_conv_main: float32 [2, 5, 2048], P('pipe', None, 'tensor')
- grad_conv_state: float32 [2, 5, 256], P('pipe')
- grad_step_bias: float32 [2, 32], P('pipe', 'tensor')
- grad_log_rate: float32 [2, 32], P('pipe', 'tensor')
- grad_skip_gain: float32 [2, 32], P('pipe', 'tensor')
- grad_gate_gain: float32 [2, 2048], P('pipe', 'tensor')
- grad_out_weight: float32 [2, 1024, 2048], P('pipe', 'dp', 'tensor')
All inputs are finite; a program needn't handle non-finite values.
Results may differ from a plain program's by a relative error of at most 0.02.
Values may be sent and summed in bfloat16 or wider, within the bound.
A program may use at most 256 MiB of HBM per device.

v0:
```python
from functools import partial

import jax
import jax.numpy as jnp
from jax import lax
from jax.sharding import PartitionSpec as P

BLOCK = 256
INNER = 2048


EPS = 1e-05
NEG_FILL = -1e30
HIGH = lax.Precision.HIGHEST


def as_sent(array):

    def short(part):
        return part.astype(jnp.bfloat16) if part.dtype == jnp.float32 else part

    return jax.tree.map(short, array)


def shifted(value, axis, steps):
    count = lax.axis_size(axis)
    leading, last = (max(0, -steps), min(count, count - steps))
    return lax.ppermute(value, axis, [(source, source + steps) for source in range(leading, last)])


def causal_conv(signal, taps):
    width = taps.shape[0] - 1
    padded = jnp.pad(signal, ((width - 1, 0), (0, 0)))
    total = taps[width][None, :] + jnp.zeros_like(signal)
    for index in range(width):
        total = total + taps[index][None, :] * padded[index : index + signal.shape[0]]
    return total


def ssd_block(decay, carry, block):
    block_x, block_b, block_c, block_dt = block
    width = block_dt.shape[0]
    log_decay = jnp.cumsum(block_dt * decay[None, :], axis=0)
    products = jnp.einsum("tn,sn->ts", block_c, block_b, precision=HIGH)
    spread_log = log_decay[:, None, :] - log_decay[None, :, :]
    causal = jnp.arange(width)[:, None] >= jnp.arange(width)[None, :]
    mixing = (
        products[:, :, None]
        * jnp.exp(jnp.where(causal[:, :, None], spread_log, NEG_FILL))
        * block_dt[None, :, :]
    )
    within = jnp.einsum("tsh,shp->thp", mixing, block_x, precision=HIGH)
    carried = (
        jnp.einsum("tn,hnp->thp", block_c, carry, precision=HIGH) * jnp.exp(log_decay)[:, :, None]
    )
    to_end = jnp.exp(log_decay[-1][None, :] - log_decay) * block_dt
    carry = jnp.exp(log_decay[-1])[:, None, None] * carry + jnp.einsum(
        "sn,shp->hnp", block_b, to_end[:, :, None] * block_x, precision=HIGH
    )
    return (carry, within + carried)


def scan_ssd(values, bmat, cmat, delta, decay, skip_gain):
    length, heads, head_width = values.shape
    count = length // BLOCK
    blocks = (
        values.reshape(count, BLOCK, heads, head_width),
        bmat.reshape(count, BLOCK, -1),
        cmat.reshape(count, BLOCK, -1),
        delta.reshape(count, BLOCK, heads),
    )
    start = jnp.zeros((heads, bmat.shape[1], head_width), values.dtype)
    stepper = jax.checkpoint(partial(ssd_block, decay))
    final, outputs = lax.scan(stepper, start, blocks)
    return outputs.reshape(length, heads, head_width) + skip_gain[None, :, None] * values


def mixer(projected, taps, step_bias, log_rate, skip_gain, inner_width, state_width, head_count):
    gate = projected[:, :inner_width]
    convolved = jax.nn.silu(
        causal_conv(projected[:, inner_width : 2 * inner_width + 2 * state_width], taps)
    )
    values = convolved[:, :inner_width].reshape(-1, head_count, inner_width // head_count)
    bmat = convolved[:, inner_width : inner_width + state_width]
    cmat = convolved[:, inner_width + state_width :]
    delta = jax.nn.softplus(projected[:, 2 * inner_width + 2 * state_width :] + step_bias[None, :])
    outputs = scan_ssd(values, bmat, cmat, delta, -jnp.exp(log_rate), skip_gain)
    return outputs.reshape(projected.shape[0], inner_width) * jax.nn.silu(gate)


def gather_weights(shards):
    gate_x_full, read_write_full, step_full, out_full = (
        lax.all_gather(shards[0], "dp", axis=0, tiled=True),
        lax.all_gather(shards[1], "dp", axis=0, tiled=True),
        lax.all_gather(shards[2], "dp", axis=0, tiled=True),
        lax.all_gather(shards[3], "dp", axis=0, tiled=True),
    )
    w_in = jnp.concatenate([gate_x_full[:, 0], gate_x_full[:, 1], read_write_full, step_full], 1)
    w_keep = jnp.concatenate([gate_x_full[:, 0], gate_x_full[:, 1], step_full], 1)
    return (w_in, w_keep, read_write_full, out_full)


def share(grads):
    return jax.tree.map(
        lambda part: part.astype(jnp.float32),
        lax.psum_scatter(as_sent(grads), "dp", scatter_dimension=0, tiled=True),
    )


def tree_add(left, right):
    return jax.tree.map(lambda first_term, second_term: first_term + second_term, left, right)


def body(
    inputs,
    out_grad,
    norm_gain,
    in_gate_x,
    in_read_write,
    in_step,
    conv_main,
    conv_state,
    step_bias,
    log_rate,
    skip_gain,
    gate_gain,
    out_weight,
):
    micro = inputs.shape[0]
    part = inputs.shape[1]
    width = inputs.shape[2]
    inner_local = out_weight.shape[2]
    state_pair = in_read_write.shape[2]
    heads_local = step_bias.shape[1]
    first_section = lax.axis_index("pipe") == 0
    offset = lax.axis_index("tensor") * part
    gain = norm_gain[0]
    gate_scale = gate_gain[0]
    taps = jnp.concatenate([conv_main[0], conv_state[0]], 1)
    shards = (in_gate_x[0], in_read_write[0], in_step[0], out_weight[0])
    split = 2 * inner_local

    def local_mix(projected, taps_in, bias_in, rate_in, skip_in):
        return mixer(
            projected, taps_in, bias_in, rate_in, skip_in, inner_local, state_pair // 2, heads_local
        )

    w_in, w_keep, w_read, w_out = gather_weights(shards)
    received = jnp.zeros((part, width), jnp.float32)
    history = []
    for tick in range(micro + 1):
        own = inputs[min(tick, micro - 1)].astype(jnp.float32)
        residual = jnp.where(first_section, own, received)
        forward_scale = lax.rsqrt(jnp.mean(residual * residual, -1, keepdims=True) + EPS)
        normed = (residual * forward_scale * gain).astype(jnp.bfloat16)
        forward_gathered = lax.all_gather(normed, "tensor", axis=0, tiled=True)
        forward_projected = jnp.dot(forward_gathered, w_in, preferred_element_type=jnp.float32)
        gated, forward_pullback = jax.vjp(
            local_mix, forward_projected, taps, step_bias[0], log_rate[0], skip_gain[0]
        )
        squares = lax.psum(jnp.sum(gated * gated, -1), "tensor")
        forward_inverse_rms = lax.rsqrt(squares / INNER + EPS)[:, None]
        forward_scaled = gated * forward_inverse_rms
        forward_mixed_low = (forward_scaled * gate_scale).astype(jnp.bfloat16)
        branch = lax.psum_scatter(
            jnp.einsum("ti,di->td", forward_mixed_low, w_out, preferred_element_type=jnp.float32),
            "tensor",
            scatter_dimension=0,
            tiled=True,
        )
        result = residual + branch
        kept = (
            residual,
            forward_gathered,
            forward_scaled,
            forward_inverse_rms,
            forward_mixed_low,
            forward_pullback,
        )
        history.append((result, kept))
        if tick < micro:
            received = shifted(result, "pipe", 1)
    w_in, w_keep, w_read, w_out = gather_weights(shards)
    back_in = jnp.zeros((part, width), jnp.float32)
    grads_in = []
    large_total = None
    small_total = None
    for tick in range(micro + 1):
        kept = history[micro - tick][1]
        mine = out_grad[max(micro - 1 - tick, 0)].astype(jnp.float32)
        grad_out = jnp.where(first_section, back_in, mine)
        valid = jnp.where(first_section, tick >= 1, tick <= micro - 1).astype(jnp.float32)
        backward_residual, gathered, scaled, inverse_rms, mixed_low, pullback = kept
        sent = grad_out.astype(jnp.bfloat16)
        piece = lax.all_gather(sent, "tensor", axis=0, tiled=True)
        back_rows = jnp.dot(piece, w_out, preferred_element_type=jnp.float32)
        grad_mixed = back_rows
        backward_grad_wout = jnp.einsum(
            "td,ti->di", piece, mixed_low, preferred_element_type=jnp.float32
        )
        grad_mixed, backward_grad_wout = (grad_mixed, backward_grad_wout)
        grad_scaled = grad_mixed * gate_scale
        backward_grad_gate = jnp.sum(grad_mixed * scaled, 0)
        inner_dot = lax.psum(jnp.sum(grad_scaled * scaled, -1), "tensor")
        grad_gated = inverse_rms * (grad_scaled - scaled * (inner_dot / INNER)[:, None])
        (
            grad_proj,
            backward_grad_taps,
            backward_grad_bias,
            backward_grad_rate,
            backward_grad_skip,
        ) = pullback(grad_gated)
        kept_low = jnp.concatenate(
            [grad_proj[:, :split], grad_proj[:, split + state_pair :]], 1
        ).astype(jnp.bfloat16)
        partial_rw = grad_proj[:, split : split + state_pair]
        in_back_rows = jnp.einsum("tc,dc->td", kept_low, w_keep, preferred_element_type=jnp.float32)
        summed = lax.psum_scatter(
            jnp.concatenate([in_back_rows, partial_rw], 1).astype(jnp.bfloat16),
            "tensor",
            scatter_dimension=0,
            tiled=True,
        ).astype(jnp.float32)
        rw_low = summed[:, width:].astype(jnp.bfloat16)
        grad_normed = summed[:, :width] + jnp.einsum(
            "tc,dc->td", rw_low, w_read, preferred_element_type=jnp.float32
        )
        own_rows = lax.dynamic_slice_in_dim(gathered, offset, part, 0)
        backward_grad_wrw = jnp.einsum(
            "td,tc->dc", own_rows, rw_low, preferred_element_type=jnp.float32
        )
        grad_win = jnp.einsum("td,tc->dc", gathered, kept_low, preferred_element_type=jnp.float32)
        scale = lax.rsqrt(jnp.mean(backward_residual * backward_residual, -1, keepdims=True) + EPS)
        unit = backward_residual * scale
        grad_unit = grad_normed * gain
        backward_grad_gain = jnp.sum(grad_normed * unit, 0)
        grad_residual = grad_out + scale * (
            grad_unit - unit * jnp.mean(grad_unit * unit, -1, keepdims=True)
        )
        large_terms = (
            grad_win[:, :split].reshape(width, 2, inner_local),
            grad_win[:, split:],
            backward_grad_wout,
        )
        small_terms = (
            backward_grad_taps,
            backward_grad_bias,
            backward_grad_rate,
            backward_grad_skip,
            backward_grad_gate,
            backward_grad_gain,
            backward_grad_wrw,
        )
        grad_residual, large_terms, small_terms = (grad_residual, large_terms, small_terms)
        grads_in.append(grad_residual)
        large_terms = jax.tree.map(lambda term_value: term_value * valid, large_terms)
        small_terms = jax.tree.map(lambda term_value: term_value * valid, small_terms)
        large_total = large_terms if large_total is None else tree_add(large_total, large_terms)
        small_total = small_terms if small_total is None else tree_add(small_total, small_terms)
        if tick < micro:
            back_in = shifted(grad_residual.astype(jnp.bfloat16), "pipe", -1).astype(
                grad_residual.dtype
            )
    large_total = share(large_total)
    grad_gate_x, grad_step, grad_wout = large_total
    grad_taps, grad_bias, grad_rate, grad_skip, grad_gate, grad_gain, grad_wrw = small_total
    conv_main_grad, grad_bias, grad_rate, grad_skip, grad_gate = lax.psum(
        (grad_taps[:, :inner_local], grad_bias, grad_rate, grad_skip, grad_gate), "dp"
    )
    grad_gain, conv_state_grad = lax.psum((grad_gain, grad_taps[:, inner_local:]), ("dp", "tensor"))
    grad_wrw = lax.psum_scatter(grad_wrw, ("dp", "tensor"), scatter_dimension=0, tiled=True)
    activations = jnp.stack(
        [
            jnp.where(first_section, history[index][0], history[index + 1][0])
            for index in range(micro)
        ]
    )
    input_grads = jnp.stack(
        [
            jnp.where(first_section, grads_in[micro - index], grads_in[micro - 1 - index])
            for index in range(micro)
        ]
    )
    return (
        activations[None],
        input_grads[None],
        grad_gain[None],
        grad_gate_x[None],
        grad_wrw[None],
        grad_step[None],
        conv_main_grad[None],
        conv_state_grad[None],
        grad_bias[None],
        grad_rate[None],
        grad_skip[None],
        grad_gate[None],
        grad_wout[None],
    )


def solution(mesh):
    in_specs = (
        P("dp", "tensor", None),
        P("dp", "tensor", None),
        P("pipe", None),
        P("pipe", "dp", None, "tensor"),
        P("pipe", "dp", None),
        P("pipe", "dp", "tensor"),
        P("pipe", None, "tensor"),
        P("pipe", None, None),
        P("pipe", "tensor"),
        P("pipe", "tensor"),
        P("pipe", "tensor"),
        P("pipe", "tensor"),
        P("pipe", "dp", "tensor"),
    )
    out_specs = (
        P("pipe", "dp", "tensor", None),
        P("pipe", "dp", "tensor", None),
        P("pipe", None),
        P("pipe", "dp", None, "tensor"),
        P("pipe", ("dp", "tensor"), None),
        P("pipe", "dp", "tensor"),
        P("pipe", None, "tensor"),
        P("pipe", None, None),
        P("pipe", "tensor"),
        P("pipe", "tensor"),
        P("pipe", "tensor"),
        P("pipe", "tensor"),
        P("pipe", "dp", "tensor"),
    )
    return jax.shard_map(body, mesh=mesh, in_specs=in_specs, out_specs=out_specs, check_vma=False)
```

profile of v0, /device:TPU:0, one launch (start us, length us, event | category | flops | bytes accessed | tf_op | source)
XLA Modules:
  0.0 2162.2 jit_solution(10661329916785299305)
XLA Ops:
  13.1 26.8 %all-gather.1 = bf16[1,1024,256]{2,1,0:T(8,128)(2,1)S(1)} all-gather(bf16[1,64,256]{2,1,0:T(8,128)(2,1)S(1)} %copy-done.115), channel_id=3, replica_groups=mesh['pipe'=2,'dp'=16,'tensor'=4] {'dp'}, dimensions={1}, use_global_device_ids=true | all-gather | bytes 557056 | tf_op jit(solution)/shard_map/all_gather | solution.py:94
  40.1 20.1 all-gather.2
  63.9 30.5 %all-gather.13.cloned.1.call-done = bf16[1024,1024]{1,0:T(8,128)(2,1)} async-done(((bf16[256,1024]{1,0:T(8,128)(2,1)}), bf16[1024,1024]{1,0:T(8,128)(2,1)}) %all-gather.13.cloned.1.call-update) | async-done | bytes 2097168 | tf_op jit(solution)/shard_map/all_gather | solution.py:156
  118.6 84.0 %while.123 = (s32[]{:T(128)}, f32[8,128,64]{1,2,0:T(8,128)S(1)}, f32[4,256,8,64]{1,0,3,2:T(4,128)}, f32[4,8,128,64]{2,3,1,0:T(8,128)S(1)}, f32[4,256,8]{1,2,0:T(...) while((s32[]{:T(128)}, f32[8,128,64]{1,2,0:T(8,128)S(1)}, ...), condition=%wide.region_4.6_spmd.clone, body=%wide.region_1.5_spmd.clone.sunk | while | flops 908924928 | bytes 7540543 | solution.py:74
  125.4 12.3 dynamic_update_slice.191
  146.4 12.3 dynamic_update_slice.191
  167.4 12.3 dynamic_update_slice.191
  188.4 12.3 dynamic_update_slice.191
  208.7 8.6 psum.91
  222.1 46.3 %reduce-scatter.12.cloned.1.call-done = f32[256,1024]{1,0:T(8,128)} async-done(((f32[1024,1024]{1,0:T(8,128)}), f32[256,1024]{1,0:T(8,128)}) %reduce-scatter.12.cloned.1.call-update) | async-done | bytes 1048592 | tf_op jit(solution)/shard_map/reduce_scatter | solution.py:165
  273.5 22.4 %collective-permute-done = f32[256,1024]{1,0:T(8,128)S(1)} collective-permute-done((f32[256,1024]{1,0:T(8,128)S(1)}, f32[256,1024]{1,0:T(8,128)S(1)}, u32[]{:S(2)}, u32[]{:S(2)}) %collective-permute-start) | collective-permute-done | bytes 1048608 | tf_op jit(solution)/shard_map/ppermute | solution.py:28
  297.3 31.4 %all-gather.15.cloned.1.call-done = bf16[1024,1024]{1,0:T(8,128)(2,1)} async-done(((bf16[256,1024]{1,0:T(8,128)(2,1)}), bf16[1024,1024]{1,0:T(8,128)(2,1)}) %all-gather.15.cloned.1.call-update) | async-done | bytes 2097168 | tf_op jit(solution)/shard_map/all_gather | solution.py:156
  351.4 84.0 %while.124 = (s32[]{:T(128)}, f32[8,128,64]{1,2,0:T(8,128)S(1)}, f32[4,256,8,64]{1,0,3,2:T(4,128)}, f32[4,8,128,64]{2,3,1,0:T(8,128)}, f32[4,256,8]{1,2,0:T(8,12...) while((s32[]{:T(128)}, f32[8,128,64]{1,2,0:T(8,128)S(1)}, ...), condition=%wide.region_12.14_spmd.clone, body=%wide.region_9.13_spmd.clone.sunk | while | flops 908924928 | bytes 7541051 | solution.py:74
  358.1 12.3 dynamic_update_slice.193
  379.1 12.3 dynamic_update_slice.193
  400.1 12.3 dynamic_update_slice.193
  421.1 12.3 dynamic_update_slice.193
  441.0 8.6 psum.92
  454.4 46.3 %reduce-scatter.14.cloned.1.call-done = f32[256,1024]{1,0:T(8,128)} async-done(((f32[1024,1024]{1,0:T(8,128)}), f32[256,1024]{1,0:T(8,128)}) %reduce-scatter.14.cloned.1.call-update) | async-done | bytes 1048592 | tf_op jit(solution)/shard_map/reduce_scatter | solution.py:165
  506.8 22.4 %collective-permute-done.1 = f32[256,1024]{1,0:T(8,128)S(1)} collective-permute-done((f32[256,1024]{1,0:T(8,128)S(1)}, f32[256,1024]{1,0:T(8,128)S(1)}, u32[]{:S(2)}, u32[]{:S(2)}) %collective-permute-start.1) | collective-permute-done | bytes 1048608 | tf_op jit(solution)/shard_map/ppermute | solution.py:28
  532.8 30.2 %all-gather.17.cloned.1.call-done = bf16[1024,1024]{1,0:T(8,128)(2,1)} async-done(((bf16[256,1024]{1,0:T(8,128)(2,1)}), bf16[1024,1024]{1,0:T(8,128)(2,1)}) %all-gather.17.cloned.1.call-update) | async-done | bytes 2097168 | tf_op jit(solution)/shard_map/all_gather | solution.py:156
  584.8 83.9 %while.125 = (s32[]{:T(128)}, f32[8,128,64]{1,2,0:T(8,128)S(1)}, f32[4,256,8,64]{1,0,3,2:T(4,128)}, f32[4,8,128,64]{2,3,1,0:T(8,128)}, f32[4,256,8]{1,2,0:T(8,12...) while((s32[]{:T(128)}, f32[8,128,64]{1,2,0:T(8,128)S(1)}, ...), condition=%wide.region_20.22_spmd.clone, body=%wide.region_17.21_spmd.clone.sunk | while | flops 908924928 | bytes 7541051 | solution.py:74
  591.5 12.3 dynamic_update_slice.195
  612.5 12.3 dynamic_update_slice.195
  633.5 12.3 dynamic_update_slice.195
  654.4 12.3 dynamic_update_slice.195
  676.3 8.6 psum.93
  684.9 5.9 multiply_reduce_fusion.26
  690.8 8.9 psum.94
  699.7 6.2 multiply_reduce_fusion.29
  712.3 139.3 %while.126 = (s32[]{:T(128)}, f32[8]{0:T(128)S(1)}, f32[8,128,64]{1,2,0:T(8,128)S(1)}, f32[4,256,8,64]{1,0,3,2:T(4,128)}, f32[4,256,128]{2,1,0:T(8,128)}, /*inde...) while((s32[]{:T(128)}, f32[8]{0:T(128)S(1)}, ...), condition=%wide.region_40.42_spmd.clone, body=%wide.region_26.41_spmd.clone.sunk | while | flops 2124974080 | bytes 18501456 | solution.py:74
  734.2 12.4 dynamic_update_slice.199
  768.9 12.4 dynamic_update_slice.199
  803.6 12.4 dynamic_update_slice.199
  838.3 12.4 dynamic_update_slice.199
  861.2 7.2 multiply_reduce_fusion.23
  879.6 33.2 %reduce-scatter.18.cloned.1.call-done = bf16[256,1280]{1,0:T(8,128)(2,1)} async-done(((bf16[1024,1280]{1,0:T(8,128)(2,1)}), bf16[256,1280]{1,0:T(8,128)(2,1)}) %reduce-scatter.18.cloned.1.call-update) | async-done | bytes 655376 | tf_op jit(solution)/shard_map/reduce_scatter | solution.py:218
  917.4 14.3 collective-permute-done.2
  933.6 30.6 %all-gather.21.cloned.1.call-done = bf16[1024,1024]{1,0:T(8,128)(2,1)} async-done(((bf16[256,1024]{1,0:T(8,128)(2,1)}), bf16[1024,1024]{1,0:T(8,128)(2,1)}) %all-gather.21.cloned.1.call-update) | async-done | bytes 2097168 | tf_op jit(solution)/shard_map/all_gather | solution.py:195
  970.1 8.6 psum.95
  978.6 6.2 multiply_reduce_fusion.28
  991.3 139.1 %while.127 = (s32[]{:T(128)}, f32[8]{0:T(128)S(1)}, f32[8,128,64]{1,2,0:T(8,128)S(1)}, f32[4,256,8,64]{1,0,3,2:T(4,128)}, f32[4,256,128]{2,1,0:T(8,128)}, /*inde...) while((s32[]{:T(128)}, f32[8]{0:T(128)S(1)}, ...), condition=%wide.region_59.61_spmd.clone, body=%wide.region_45.60_spmd.clone.sunk | while | flops 2124974080 | bytes 18501456 | solution.py:74
  1013.2 12.3 dynamic_update_slice.203
  1047.8 12.3 dynamic_update_slice.203
  1082.5 12.3 dynamic_update_slice.203
  1117.1 12.3 dynamic_update_slice.203
  1139.9 7.2 multiply_reduce_fusion.19
  1158.5 33.5 %reduce-scatter.20.cloned.1.call-done = bf16[256,1280]{1,0:T(8,128)(2,1)} async-done(((bf16[1024,1280]{1,0:T(8,128)(2,1)}), bf16[256,1280]{1,0:T(8,128)(2,1)}) %reduce-scatter.20.cloned.1.call-update) | async-done | bytes 655376 | tf_op jit(solution)/shard_map/reduce_scatter | solution.py:218
  1197.0 14.3 collective-permute-done.3
  1213.2 30.7 %all-gather.23.cloned.1.call-done = bf16[1024,1024]{1,0:T(8,128)(2,1)} async-done(((bf16[256,1024]{1,0:T(8,128)(2,1)}), bf16[1024,1024]{1,0:T(8,128)(2,1)}) %all-gather.23.cloned.1.call-update) | async-done | bytes 2097168 | tf_op jit(solution)/shard_map/all_gather | solution.py:195
  1249.1 8.5 psum.96
  1257.7 6.1 multiply_reduce_fusion.27
  1270.1 150.3 %while.128 = (s32[]{:T(128)}, f32[8]{0:T(128)}, f32[8,128,64]{1,2,0:T(8,128)S(1)}, f32[4,256,8,64]{1,0,3,2:T(4,128)}, f32[4,256,128]{2,1,0:T(8,128)S(1)}, /*inde...) while((s32[]{:T(128)}, f32[8]{0:T(128)}, ...), condition=%wide.region_78.80_spmd.clone, body=%wide.region_64.79_spmd.clone.sunk | while | flops 2124974080 | bytes 18500640 | solution.py:74
  1294.2 12.3 dynamic_update_slice.207
  1331.7 12.3 dynamic_update_slice.207
  1369.1 12.3 dynamic_update_slice.207
  1406.6 12.3 dynamic_update_slice.207
  1429.6 6.6 multiply_reduce_fusion.15
  1474.0 6.4 fusion.274
  1497.9 67.6 %all-reduce.56 = (f32[1,5,512]{2,1,0:T(8,128)S(1)}, f32[1,8]{1,0:T(1,128)}, f32[1,8]{1,0:T(1,128)}, f32[1,8]{1,0:T(1,128)}, f32[1,512]{1,0:T(1,128)}) all-reduce(f32[1,5,512]{2,1,0:T(8,128)S(1)} %slice_bitcast_fusion.2, f32[1,8]{1,0:T(1,128)S(1)} %add_bitcast_fusion.10, ...), channel_id=1, replica_groups=mesh['pipe'=2,'dp'=16,'tensor'=4] {'dp'}, use_global_device_ids=true, to_apply=%region_103.105 | all-reduce | flops 3096 | bytes 24768 | tf_op jit(solution)/shard_map/psum | solution.py:267
  1567.5 53.1 %reduce-scatter.26.cloned.1.call-done = bf16[64,512]{1,0:T(8,128)(2,1)} async-done(((bf16[1024,512]{1,0:T(8,128)(2,1)}), bf16[64,512]{1,0:T(8,128)(2,1)}) %reduce-scatter.26.cloned.1.call-update) | async-done | bytes 65552 | tf_op jit(solution)/shard_map/reduce_scatter | solution.py:106
  1622.2 144.4 %all-reduce.59.cloned.1.call-done = bf16[1024,2,512]{2,1,0:T(2,128)(2,1)} async-done(((bf16[1024,2,512]{2,1,0:T(2,128)(2,1)}), bf16[1024,2,512]{2,1,0:T(2,128)(2,1)}) %all-reduce.59.cloned.1.call-update) | async-done | bytes 2097168
  1771.1 176.5 %all-reduce.55 = (f32[1,1024]{1,0:T(1,128)}, f32[1,5,256]{2,0,1:T(1,128)}) all-reduce(f32[1,1024]{1,0:T(1,128)S(1)} %bitcast.1099, f32[1,5,256]{2,0,1:T(1,128)S(1)} %broadcast_in_dim.455), channel_id=1, replica_groups=mesh['pipe'=2,'dp'=16,'tensor'=4] {'dp','tensor'}, use_global_device_ids=true, to_apply=%region_84.86 | all-reduce | flops 2304 | bytes 18432 | tf_op jit(solution)/shard_map/psum | solution.py:270
  1953.5 201.6 %reduce-scatter.24.cloned.1.call-done = f32[16,256]{1,0:T(8,128)} async-done(((f32[1024,256]{1,0:T(8,128)}), f32[16,256]{1,0:T(8,128)}) %reduce-scatter.24.cloned.1.call-update) | async-done | bytes 16400 | tf_op jit(solution)/shard_map/reduce_scatter | solution.py:271
  (1237 shorter events, 665.3 us)
Async XLA Ops:
  7.2 53.0 %copy-start.145 = (f32[1,5,512]{2,0,1:T(1,128)S(1)}, f32[1,5,512]{2,0,1:T(1,128)}, u32[]{:S(2)}) copy-start(f32[1,5,512]{2,0,1:T(1,128)} %param.32) | copy-start | bytes 30724
  7.2 53.0 %copy-start.153 = (f32[1,5,256]{2,0,1:T(1,128)S(1)}, f32[1,5,256]{2,0,1:T(1,128)}, u32[]{:S(2)}) copy-start(f32[1,5,256]{2,0,1:T(1,128)} %param.33) | copy-start | bytes 15364
  7.2 53.0 %copy-start.161 = (f32[1,8]{1,0:T(1,128)S(1)}, f32[1,8]{1,0:T(1,128)}, u32[]{:S(2)}) copy-start(f32[1,8]{1,0:T(1,128)} %param.35) | copy-start | bytes 100
  7.2 53.0 %copy-start.160 = (f32[1,8]{1,0:T(1,128)S(1)}, f32[1,8]{1,0:T(1,128)}, u32[]{:S(2)}) copy-start(f32[1,8]{1,0:T(1,128)} %param.36) | copy-start | bytes 100
  7.2 54.9 %all-gather.25.cloned.1.call-start = ((), (), s32[]{:S(2)}) async-start(), calls=%async_computation.23 | async-start | bytes 2228224 | tf_op jit(solution)/shard_map/all_gather | solution.py:93
  8.9 85.4 %all-gather.13.cloned.1.call-start = ((), (), s32[]{:S(2)}) async-start(), calls=%async_computation.9 | async-start | bytes 2621440 | tf_op jit(solution)/shard_map/all_gather | solution.py:156
  10.2 51.9 %copy-start.146 = (f32[256]{0:T(256)}, f32[256]{0:T(256)S(1)}, u32[]{:S(2)}) copy-start(f32[256]{0:T(256)S(1)} %add_rsqrt_fusion.5) | copy-start | bytes 3076
  12.3 205.0 %all-gather.27.cloned.1.call-start = ((), (), s32[]{:S(2)}) async-start(), calls=%async_computation.24 | async-start | bytes 1114112 | tf_op jit(solution)/shard_map/all_gather | solution.py:96
  13.0 255.4 %reduce-scatter.12.cloned.1.call-start = ((), (), s32[]{:S(2)}) async-start(), calls=%async_computation.10 | async-start | bytes 5242880 | tf_op jit(solution)/shard_map/reduce_scatter | solution.py:165
  40.0 54.4 %copy-start.53 = (bf16[1,1024,256]{2,1,0:T(8,128)(2,1)}, bf16[1,1024,256]{2,1,0:T(8,128)(2,1)S(1)}, u32[]{:S(2)}) copy-start(bf16[1,1024,256]{2,1,0:T(8,128)(2,1)S(1)} %all-gather.1) | copy-start | bytes 1572868
  60.2 34.2 %copy-start.81 = (bf16[1,1024,8]{2,1,0:T(8,128)(2,1)}, bf16[1,1024,8]{2,1,0:T(8,128)(2,1)S(1)}, u32[]{:S(2)}) copy-start(bf16[1,1024,8]{2,1,0:T(8,128)(2,1)S(1)} %all-gather.2) | copy-start | bytes 49156
  60.4 1197.3 %copy-start.90 = (f32[512]{0:T(512)}, f32[512]{0:T(512)S(1)}, u32[]{:S(2)}) copy-start(f32[512]{0:T(512)S(1)} %mul.1962) | copy-start | bytes 6148
  60.4 1086.7 %copy-start.92 = (f32[768]{0:T(1024)}, f32[768]{0:T(1024)S(1)}, u32[]{:S(2)}) copy-start(f32[768]{0:T(1024)S(1)} %get-tuple-element.1994) | copy-start | bytes 9220
  60.5 1086.7 %copy-start.94 = (f32[768]{0:T(1024)}, f32[768]{0:T(1024)S(1)}, u32[]{:S(2)}) copy-start(f32[768]{0:T(1024)S(1)} %get-tuple-element.1995) | copy-start | bytes 9220
  60.5 1086.7 %copy-start.96 = (f32[768]{0:T(1024)}, f32[768]{0:T(1024)S(1)}, u32[]{:S(2)}) copy-start(f32[768]{0:T(1024)S(1)} %get-tuple-element.1996) | copy-start | bytes 9220
  60.5 1086.6 %copy-start.98 = (f32[768]{0:T(1024)}, f32[768]{0:T(1024)S(1)}, u32[]{:S(2)}) copy-start(f32[768]{0:T(1024)S(1)} %get-tuple-element.1997) | copy-start | bytes 9220
  63.8 35.2 %copy-start.78 = (bf16[1024,512]{1,0:T(8,128)(2,1)}, bf16[1024,512]{1,0:T(8,128)(2,1)S(1)}, u32[]{:S(2)}) copy-start(bf16[1024,512]{1,0:T(8,128)(2,1)S(1)} %get-tuple-element.2264) | copy-start | bytes 3145732
  63.8 35.2 %copy-start.80 = (bf16[1024,512]{1,0:T(8,128)(2,1)}, bf16[1024,512]{1,0:T(8,128)(2,1)S(1)}, u32[]{:S(2)}) copy-start(bf16[1024,512]{1,0:T(8,128)(2,1)S(1)} %get-tuple-element.2265) | copy-start | bytes 3145732
  222.0 46.4 %copy-start.49 = (bf16[2,256,1024]{2,1,0:T(8,128)(2,1)S(1)}, bf16[2,256,1024]{2,1,0:T(8,128)(2,1)}, u32[]{:S(2)}) copy-start(bf16[2,256,1024]{2,1,0:T(8,128)(2,1)} %param.26) | copy-start | bytes 3145732
  222.0 74.1 %copy-start.87 = (f32[1,1024]{1,0:T(1,128)S(1)}, f32[1,1024]{1,0:T(1,128)}, u32[]{:S(2)}) copy-start(f32[1,1024]{1,0:T(1,128)} %param.28) | copy-start | bytes 12292
  222.0 106.6 %all-gather.15.cloned.1.call-start = ((), (), s32[]{:S(2)}) async-start(), calls=%async_computation.11 | async-start | bytes 2621440 | tf_op jit(solution)/shard_map/all_gather | solution.py:156
  269.8 58.9 %copy-start.54 = (bf16[1,1024,256]{2,1,0:T(8,128)(2,1)S(1)}, bf16[1,1024,256]{2,1,0:T(8,128)(2,1)}, u32[]{:S(2)}) copy-start(bf16[1,1024,256]{2,1,0:T(8,128)(2,1)} %copy-done.53) | copy-start | bytes 1572868
  269.8 58.9 %copy-start.82 = (bf16[1,1024,8]{2,1,0:T(8,128)(2,1)S(1)}, bf16[1,1024,8]{2,1,0:T(8,128)(2,1)}, u32[]{:S(2)}) copy-start(bf16[1,1024,8]{2,1,0:T(8,128)(2,1)} %copy-done.81) | copy-start | bytes 49156
  269.8 26.1 %collective-permute-start = (f32[256,1024]{1,0:T(8,128)S(1)}, f32[256,1024]{1,0:T(8,128)S(1)}, u32[]{:S(2)}, u32[]{:S(2)}) collective-permute-start(f32[256,1024]{1,0:T(8,128)S(1)} %bitcast_add_fusion.1), channel_id=1, source_target_pairs={{0,64},{1,65},{2,66},{3,67},{4,68},{5,69},{6,70},{7,71},{8,72},{9,... | collective-permute-start | bytes 3145736 | tf_op jit(solution)/shard_map/ppermute | solution.py:28
  296.1 204.6 %copy-start.26 = (f32[256,1024]{1,0:T(8,128)}, f32[256,1024]{1,0:T(8,128)S(1)}, u32[]{:S(2)}) copy-start(f32[256,1024]{1,0:T(8,128)S(1)} %get-tuple-element.2209) | copy-start | bytes 3145732
  296.1 37.8 %copy-start.143 = (f32[256]{0:T(256)}, f32[256]{0:T(256)S(1)}, u32[]{:S(2)}) copy-start(f32[256]{0:T(256)S(1)} %add_rsqrt_fusion.4) | copy-start | bytes 3076
  297.2 203.5 %reduce-scatter.14.cloned.1.call-start = ((), (), s32[]{:S(2)}) async-start(), calls=%async_computation.12 | async-start | bytes 5242880 | tf_op jit(solution)/shard_map/reduce_scatter | solution.py:165
  449.6 529.0 %copy-start.103 = (f32[1024]{0:T(1024)}, f32[1024]{0:T(1024)S(1)}, u32[]{:S(2)}) copy-start(f32[1024]{0:T(1024)S(1)} %add_rsqrt_fusion.1) | copy-start | bytes 12292
  454.3 46.4 %copy-start.62 = (f32[256,1024]{1,0:T(8,128)S(1)}, f32[256,1024]{1,0:T(8,128)}, u32[]{:S(2)}) copy-start(f32[256,1024]{1,0:T(8,128)} %copy-done.61) | copy-start | bytes 3145732
  454.3 74.9 %copy-start.50 = (bf16[2,256,1024]{2,1,0:T(8,128)(2,1)S(1)}, bf16[2,256,1024]{2,1,0:T(8,128)(2,1)}, u32[]{:S(2)}) copy-start(bf16[2,256,1024]{2,1,0:T(8,128)(2,1)} %param.26) | copy-start | bytes 3145732
  454.3 108.6 %all-gather.17.cloned.1.call-start = ((), (), s32[]{:S(2)}) async-start(), calls=%async_computation.13 | async-start | bytes 2621440 | tf_op jit(solution)/shard_map/all_gather | solution.py:156
  503.2 26.0 %collective-permute-start.1 = (f32[256,1024]{1,0:T(8,128)S(1)}, f32[256,1024]{1,0:T(8,128)S(1)}, u32[]{:S(2)}, u32[]{:S(2)}) collective-permute-start(f32[256,1024]{1,0:T(8,128)S(1)} %get-tuple-element.2197), channel_id=1, source_target_pairs={{0,64},{1,65},{2,66},{3,67},{4,68},{5,69},{6,70},{7,71},{8,72},{9,... | collective-permute-start | bytes 3145736 | tf_op jit(solution)/shard_map/ppermute | solution.py:28
  529.5 33.5 %copy-start.55 = (bf16[1,1024,256]{2,1,0:T(8,128)(2,1)S(1)}, bf16[1,1024,256]{2,1,0:T(8,128)(2,1)}, u32[]{:S(2)}) copy-start(bf16[1,1024,256]{2,1,0:T(8,128)(2,1)} %copy-done.53) | copy-start | bytes 1572868
  529.5 385.6 %copy-start.116 = (f32[256]{0:T(256)}, f32[256]{0:T(256)S(1)}, u32[]{:S(2)}) copy-start(f32[256]{0:T(256)S(1)} %add_rsqrt_fusion.3) | copy-start | bytes 3076
  531.5 153.3 %all-gather.19.cloned.1.call-start = ((), (), s32[]{:S(2)}) async-start(), calls=%async_computation.15 | async-start | bytes 2621440 | tf_op jit(solution)/shard_map/all_gather | solution.py:195
  532.5 380.3 %reduce-scatter.18.cloned.1.call-start = ((), (), s32[]{:S(2)}) async-start(), calls=%async_computation.16 | async-start | bytes 3276800 | tf_op jit(solution)/shard_map/reduce_scatter | solution.py:218
  879.6 35.5 %copy-start.38 = (bf16[2,256,1024]{2,1,0:T(8,128)(2,1)S(1)}, bf16[2,256,1024]{2,1,0:T(8,128)(2,1)}, u32[]{:S(2)}) copy-start(bf16[2,256,1024]{2,1,0:T(8,128)(2,1)} %param.27) | copy-start | bytes 3145732
  879.6 84.6 %all-gather.21.cloned.1.call-start = ((), (), s32[]{:S(2)}) async-start(), calls=%async_computation.17 | async-start | bytes 2621440 | tf_op jit(solution)/shard_map/all_gather | solution.py:195
  916.1 15.6 collective-permute-start.2
  933.5 258.5 %reduce-scatter.20.cloned.1.call-start = ((), (), s32[]{:S(2)}) async-start(), calls=%async_computation.18 | async-start | bytes 3276800 | tf_op jit(solution)/shard_map/reduce_scatter | solution.py:218
  933.6 45.1 %copy-start.7 = (f32[1024,768]{0,1:T(8,128)S(1)}, f32[1024,768]{0,1:T(8,128)}, u32[]{:S(2)}) copy-start(f32[1024,768]{0,1:T(8,128)} %copy-done.5) | copy-start | bytes 9437188
  1158.4 33.6 %copy-start.27 = (f32[256,1024]{1,0:T(8,128)S(1)}, f32[256,1024]{1,0:T(8,128)}, u32[]{:S(2)}) copy-start(f32[256,1024]{1,0:T(8,128)} %copy-done.26) | copy-start | bytes 3145732
  1158.4 33.6 %copy-start.57 = (bf16[1,1024,256]{2,1,0:T(8,128)(2,1)S(1)}, bf16[1,1024,256]{2,1,0:T(8,128)(2,1)}, u32[]{:S(2)}) copy-start(bf16[1,1024,256]{2,1,0:T(8,128)(2,1)} %copy-done.53) | copy-start | bytes 1572868
  1158.4 33.6 %copy-start.144 = (f32[256]{0:T(256)S(1)}, f32[256]{0:T(256)}, u32[]{:S(2)}) copy-start(f32[256]{0:T(256)} %copy-done.143) | copy-start | bytes 3076
  1158.4 35.8 %copy-start.39 = (bf16[2,256,1024]{2,1,0:T(8,128)(2,1)S(1)}, bf16[2,256,1024]{2,1,0:T(8,128)(2,1)}, u32[]{:S(2)}) copy-start(bf16[2,256,1024]{2,1,0:T(8,128)(2,1)} %param.27) | copy-start | bytes 3145732
  1158.4 35.8 %copy-start.76 = (bf16[256,1024]{1,0:T(8,128)(2,1)S(1)}, bf16[256,1024]{1,0:T(8,128)(2,1)}, u32[]{:S(2)}) copy-start(bf16[256,1024]{1,0:T(8,128)(2,1)} %copy-done.75) | copy-start | bytes 1572868
  1158.4 85.5 %all-gather.23.cloned.1.call-start = ((), (), s32[]{:S(2)}) async-start(), calls=%async_computation.19 | async-start | bytes 2621440 | tf_op jit(solution)/shard_map/all_gather | solution.py:195
  1195.6 48.3 %copy-start.1 = (f32[1024,512]{0,1:T(8,128)S(1)}, f32[1024,512]{0,1:T(8,128)}, u32[]{:S(2)}) copy-start(f32[1024,512]{0,1:T(8,128)} %copy-done) | copy-start | bytes 6291460
  1195.6 48.3 %copy-start.101 = (f32[1024]{0:T(1024)S(1)}, f32[1024]{0:T(1024)}, u32[]{:S(2)}) copy-start(f32[1024]{0:T(1024)} %copy-done.100) | copy-start | bytes 12292
  1195.6 15.7 collective-permute-start.3
  1213.2 282.2 %reduce-scatter.22.cloned.1.call-start = ((), (), s32[]{:S(2)}) async-start(), calls=%async_computation.20 | async-start | bytes 3276800 | tf_op jit(solution)/shard_map/reduce_scatter | solution.py:218
  1447.5 118.6 %reduce-scatter.28.cloned.1.call-start = ((), (), s32[]{:S(2)}) async-start(), calls=%async_computation.25 | async-start | bytes 278528
  1468.3 152.4 %reduce-scatter.26.cloned.1.call-start = ((), (), s32[]{:S(2)}) async-start(), calls=%async_computation.22 | async-start | bytes 1114112 | tf_op jit(solution)/shard_map/reduce_scatter | solution.py:106
  1473.7 292.8 %all-reduce.59.cloned.1.call-start = ((), (), s32[]{:S(2)}) async-start(), calls=%async_computation.26 | async-start | bytes 4194304
  1484.5 463.1 %reduce-scatter.16.cloned.1.call-start = ((), (), s32[]{:S(2)}) async-start(), calls=%async_computation.14 | async-start | bytes 5242880 | tf_op jit(solution)/shard_map/reduce_scatter | solution.py:165
  1489.6 665.4 %reduce-scatter.24.cloned.1.call-start = ((), (), s32[]{:S(2)}) async-start(), calls=%async_computation.21 | async-start | bytes 1064960 | tf_op jit(solution)/shard_map/reduce_scatter | solution.py:271
  1495.4 272.9 %copy-start.147 = (f32[256]{0:T(256)S(1)}, f32[256]{0:T(256)}, u32[]{:S(2)}) copy-start(f32[256]{0:T(256)} %copy-done.146) | copy-start | bytes 3076
  1567.5 203.6 %copy-start.131 = (f32[1024]{0:T(1024)S(1)}, f32[1024]{0:T(1024)}, u32[]{:S(2)}) copy-start(f32[1024]{0:T(1024)} %get-tuple-element.1987) | copy-start | bytes 12292
  1567.5 203.6 %copy-start.132 = (f32[1024]{0:T(1024)S(1)}, f32[1024]{0:T(1024)}, u32[]{:S(2)}) copy-start(f32[1024]{0:T(1024)} %get-tuple-element.1989) | copy-start | bytes 12292
  1567.5 380.2 %copy-start.25 = (f32[256,1024]{1,0:T(8,128)S(1)}, f32[256,1024]{1,0:T(8,128)}, u32[]{:S(2)}) copy-start(f32[256,1024]{1,0:T(8,128)} %copy-done.23) | copy-start | bytes 3145732
  1567.5 380.2 %copy-start.40 = (bf16[2,256,1024]{2,1,0:T(8,128)(2,1)S(1)}, bf16[2,256,1024]{2,1,0:T(8,128)(2,1)}, u32[]{:S(2)}) copy-start(bf16[2,256,1024]{2,1,0:T(8,128)(2,1)} %param.27) | copy-start | bytes 3145732
  1567.5 380.2 %copy-start.48 = (f32[256,1024]{1,0:T(8,128)S(1)}, f32[256,1024]{1,0:T(8,128)}, u32[]{:S(2)}) copy-start(f32[256,1024]{1,0:T(8,128)} %copy-done.47) | copy-start | bytes 3145732
  1567.5 380.2 %copy-start.117 = (f32[256]{0:T(256)S(1)}, f32[256]{0:T(256)}, u32[]{:S(2)}) copy-start(f32[256]{0:T(256)} %copy-done.116) | copy-start | bytes 3076
  1567.5 380.2 %copy-start.149 = (f32[256]{0:T(256)S(1)}, f32[256]{0:T(256)}, u32[]{:S(2)}) copy-start(f32[256]{0:T(256)} %copy-done.148) | copy-start | bytes 3076
  (135 other events, 788.1 us)
Sparse Core Ops, SparseCore 0:
  11.1 50.9 all-gather.24
  64.4 29.8 all-gather.12
  96.8 45.2 all-gather.26
  222.1 46.2 reduce-scatter.11
  297.4 31.2 all-gather.14
  454.4 46.2 reduce-scatter.13
  531.6 31.2 all-gather.16
  564.6 30.8 all-gather.18
  879.7 33.0 reduce-scatter.17
  933.6 30.5 all-gather.20
  1158.6 33.3 reduce-scatter.19
  1213.3 30.5 all-gather.22
  1447.6 33.3 reduce-scatter.21
  1485.2 64.8 reduce-scatter.27
  1554.8 65.8 reduce-scatter.25
  1623.6 142.8 all-reduce.58
  1768.8 49.6 reduce-scatter.15
  1821.4 333.6 reduce-scatter.23
where the time goes:
time: 2180 us; the launch traced here: 2160 us
  waiting for transfers between devices  788 us (36%)
  local copies, waits for them, and re-layouts  496 us (23%)
  blocking collectives  343 us (16%)
  matrix products  305 us (14%)
  other arithmetic  197 us (9%)
    dynamic_update_slice x48, local copies, waits for them, and re-layouts, scan_ssd(): final, outputs = lax.scan(stepper, start, blocks)  309 us
    reduce_scatter x1, waiting for transfers between devices, body(): lax.psum_scatter(grad_wrw, ('dp', 'tensor'), scatter_dimension=0, tiled=T...  202 us
    psum x1, blocking collectives, body(): lax.psum((grad_gain, grad_taps[:, inner_local:]), ('dp', 'tensor'))  177 us
    unnamed x20, waiting for transfers between devices  145 us
    dot_general x36, matrix products, ssd_block(): within = jnp.einsum('tsh,shp->thp', mixing, block_x, precision=HIGH)  109 us
    reduce_scatter x3, waiting for transfers between devices, body(): lax.psum_scatter(jnp.einsum('ti,di->td', forward_mixed_low, w_out, prefer...  92.6 us
    all_gather x3, waiting for transfers between devices, body(): forward_gathered = lax.all_gather(normed, 'tensor', axis=0, tiled=True)  92 us
    ppermute x4, waiting for transfers between devices, shifted(): lax.ppermute(value, axis, [(source, source + steps) for source in range(l...  73.4 us
  transfers between devices with their start and end apart: 22, of which 17 were waited for; matrix products, arithmetic and copies ran while one was open for 13% of the time, Pallas kernels for 0%

commit v1 on v0

v1 whole, which is shorter than its diff:
```python
from functools import partial

import jax
import jax.numpy as jnp
import numpy as np
from jax import lax
from jax.experimental import pallas as pl
from jax.experimental.pallas import tpu as pltpu
from jax.sharding import PartitionSpec as P

F32, BF16 = jnp.float32, jnp.bfloat16
EPS = 1e-05
ROWS = 256
CHUNK = 128
LANES = 128
EXACT = lax.Precision.HIGHEST


def mm(left, right, contract=((1,), (0,))):
    return lax.dot_general(left, right, (contract, ((), ())), preferred_element_type=F32)


def mm_exact(left, right, contract=((1,), (0,))):
    return lax.dot_general(
        left, right, (contract, ((), ())), precision=EXACT, preferred_element_type=F32
    )


def spread(value, selector, heads):
    high = value.astype(BF16).astype(F32)
    both = high + pltpu.roll(value - high, heads, 1)
    return mm(both.astype(BF16), selector)


def per_head(value, collector):
    high = value.astype(BF16)
    low = (value - high.astype(F32)).astype(BF16)
    return mm(high, collector) + mm(low, collector)


def softplus(value):
    small = jnp.exp(-jnp.abs(value))
    series = small * (1.0 - small * (0.5 - small * (1.0 / 3.0 - small * 0.25)))
    return jnp.maximum(value, 0.0) + jnp.where(small < 0.01, series, jnp.log(1.0 + small))


def sigmoid(value):
    return 1.0 / (1.0 + jnp.exp(-value))


def iota(shape, axis):
    return lax.broadcasted_iota(jnp.int32, shape, axis)


def column_to_row(column):
    size = column.shape[0]
    same = iota((size, size), 0) == iota((size, size), 1)
    return jnp.sum(jnp.where(same, column, 0.0), 0, keepdims=True)


def row_to_column(row):
    size = row.shape[1]
    same = iota((size, size), 0) == iota((size, size), 1)
    return jnp.sum(jnp.where(same, row, 0.0), 1, keepdims=True)


def steps(raw, head, mask):
    delta = softplus(raw + head[0:1]) * mask
    tri = (iota((CHUNK, CHUNK), 0) >= iota((CHUNK, CHUNK), 1)).astype(F32)
    log_decay = mm_exact(tri, delta * head[1:2])
    return delta, log_decay


def forward_kernel(sizes, rows_ref, w_ref, taps_ref, head_ref, wide_ref, selector_ref,
                   part_ref, squares_ref, z_ref, p_ref, c_ref, raw_ref, y_ref, s_ref, state, pad):
    inner, pair, heads = sizes
    states = pair // 2
    split = inner + inner + pair
    conv = inner + pair

    @pl.when(pl.program_id(0) == 0)
    def _():
        state[...] = jnp.zeros_like(state)
        pad[0:8, :] = jnp.zeros((8, conv), F32)

    @pl.when(pl.program_id(0) > 0)
    def _():
        pad[0:8, :] = pad[ROWS : ROWS + 8, :]

    projected = mm(rows_ref[...], w_ref[:, : split + LANES])
    z_ref[...] = projected[:, :inner]
    p_ref[...] = projected[:, inner:split]
    pad[8 : ROWS + 8, :] = projected[:, inner:split]
    raw_ref[...] = projected[:, split:]
    selector = selector_ref[...]
    head = head_ref[...]
    mask = head[2:3]
    first = iota((CHUNK, LANES), 1) < LANES // 2
    causal = iota((CHUNK, CHUNK), 0) >= iota((CHUNK, CHUNK), 1)
    squares = []
    for chunk in range(ROWS // CHUNK):
        at = slice(chunk * CHUNK, (chunk + 1) * CHUNK)
        c = jnp.broadcast_to(taps_ref[4:5, :], (CHUNK, conv))
        for tap in range(4):
            begin = chunk * CHUNK + 5 + tap
            c = c + taps_ref[tap : tap + 1, :] * pad[begin : begin + CHUNK, :]
        c_ref[at, :] = c
        value = c * sigmoid(c)
        xs = value[:, :inner]
        b_low = value[:, inner : inner + states].astype(BF16)
        c_low = value[:, inner + states :].astype(BF16)
        delta, log_decay = steps(raw_ref[at, :], head, mask)
        turned = log_decay.T
        final = log_decay[CHUNK - 1 : CHUNK, :]
        scaled = spread(delta, selector, heads) * xs
        scaled_low = scaled.astype(BF16)
        products = jnp.where(causal, mm(c_low, b_low, ((1,), (1,))), 0.0)
        within = []
        for two in range(heads // 2):
            lanes = slice(two * LANES, (two + 1) * LANES)
            parts = []
            for h in (2 * two, 2 * two + 1):
                gap = jnp.minimum(log_decay[:, h : h + 1] - turned[h : h + 1, :], 0.0)
                parts.append(mm((products * jnp.exp(gap)).astype(BF16), scaled_low[:, lanes]))
            within.append(jnp.where(first, parts[0], parts[1]))
        old = state[...]
        s_ref[chunk] = old
        carried = mm(c_low, old.astype(BF16)) * spread(jnp.exp(log_decay) * mask, selector, heads)
        y = jnp.concatenate(within, 1) + carried + wide_ref[1:2, :] * xs
        y_ref[at, :] = y
        ends = (spread(jnp.exp(final - log_decay) * mask, selector, heads) * scaled).astype(BF16)
        keep = spread(jnp.broadcast_to(jnp.exp(final) * mask, (8, LANES)), selector, heads)[0:1]
        state[...] = keep * old + mm(b_low, ends, ((0,), (0,)))
        z = z_ref[at, :]
        gated = y * (z * sigmoid(z))
        squares.append(jnp.sum(gated * gated, 1, keepdims=True))
        mixed = (gated * wide_ref[0:1, :]).astype(BF16)
        part_ref[at, :] = mm(mixed, w_ref[:, split + LANES :], ((1,), (1,))).astype(part_ref.dtype)
    row = column_to_row(jnp.concatenate(squares, 0))
    squares_ref[0] = jnp.broadcast_to(row, (8, ROWS))


def backward_kernel(sizes, e_ref, scales_ref, w_ref, taps_ref, head_ref, wide_ref, selector_ref,
                    collector_ref, z_ref, p_ref, c_ref, raw_ref, y_ref, s_ref,
                    part_ref, grad_ref, mixed_ref, taps_out, wide_out, head_out, state, later, pad):
    inner, pair, heads = sizes
    states = pair // 2
    split = inner + inner + pair
    conv = inner + pair

    @pl.when(pl.program_id(0) == 0)
    def _():
        state[...] = jnp.zeros_like(state)
        later[...] = jnp.zeros_like(later)
        pad[ROWS : ROWS + 8, :] = jnp.zeros((8, conv), F32)
        taps_out[...] = jnp.zeros_like(taps_out)
        wide_out[...] = jnp.zeros_like(wide_out)
        head_out[...] = jnp.zeros_like(head_out)

    @pl.when(pl.program_id(0) > 0)
    def _():
        pad[ROWS : ROWS + 8, :] = pad[0:8, :]

    selector = selector_ref[...]
    collector = collector_ref[...]
    head = head_ref[...]
    mask = head[2:3]
    first = iota((CHUNK, LANES), 1) < LANES // 2
    later_in = iota((CHUNK, CHUNK), 1) >= iota((CHUNK, CHUNK), 0)
    last = iota((CHUNK, LANES), 0) == CHUNK - 1
    inverse = row_to_column(scales_ref[0, 0:1, :])
    inner_dot = row_to_column(scales_ref[0, 1:2, :])
    mixed_grad = mm(e_ref[...], w_ref[:, split + LANES :])
    for chunk in reversed(range(ROWS // CHUNK)):
        at = slice(chunk * CHUNK, (chunk + 1) * CHUNK)
        z = z_ref[at, :]
        y = y_ref[at, :]
        sig = sigmoid(z)
        act = z * sig
        g = y * act * inverse[at]
        gain = wide_ref[0:1, :]
        mixed_ref[at, :] = (g * gain).astype(BF16)
        mixed_here = mixed_grad[at]
        gated_grad = inverse[at] * (mixed_here * gain - g * inner_dot[at])
        dy = gated_grad * act
        grad_ref[at, :inner] = (gated_grad * y * (sig * (1.0 + z - act))).astype(BF16)
        c = c_ref[at, :]
        csig = sigmoid(c)
        value = c * csig
        slope = csig * (1.0 + c - value)
        xs = value[:, :inner]
        b_low = value[:, inner : inner + states].astype(BF16)
        c_low = value[:, inner + states :].astype(BF16)
        raw = raw_ref[at, :]
        delta, log_decay = steps(raw, head, mask)
        turned = log_decay.T
        final = log_decay[CHUNK - 1 : CHUNK, :]
        wide_delta = spread(delta, selector, heads)
        scaled = wide_delta * xs
        scaled_low = scaled.astype(BF16)
        dy_low = dy.astype(BF16)
        products = jnp.where(later_in, mm(b_low, c_low, ((1,), (1,))), 0.0)
        dproducts = jnp.zeros((CHUNK, CHUNK), F32)
        within = []
        for two in range(heads // 2):
            lanes = slice(two * LANES, (two + 1) * LANES)
            parts = []
            for odd in range(2):
                h = 2 * two + odd
                mine = first if odd == 0 else ~first
                decay = jnp.exp(jnp.minimum(turned[h : h + 1, :] - log_decay[:, h : h + 1], 0.0))
                parts.append(mm((products * decay).astype(BF16), dy_low[:, lanes]))
                own = jnp.where(mine, scaled_low[:, lanes], jnp.zeros((), BF16))
                dproducts = dproducts + decay * mm(own, dy_low[:, lanes], ((1,), (1,)))
            within.append(jnp.where(first, parts[0], parts[1]))
        dproducts = jnp.where(later_in, dproducts, 0.0).astype(BF16)
        old = s_ref[chunk]
        old_low = old.astype(BF16)
        dstate = state[...]
        dstate_low = dstate.astype(BF16)
        to_end = spread(jnp.exp(final - log_decay) * mask, selector, heads)
        from_start = (spread(jnp.exp(log_decay) * mask, selector, heads) * dy).astype(BF16)
        dscaled = jnp.concatenate(within, 1) + to_end * mm(b_low, dstate_low)
        dc_state = mm(from_start, old_low, ((1,), (1,))) + mm(dproducts, b_low, ((0,), (0,)))
        db_state = mm((to_end * scaled).astype(BF16), dstate_low, ((1,), (1,))) + mm(dproducts, c_low)
        carry = jnp.broadcast_to(jnp.sum(later[...] * dstate, 0, keepdims=True), (8, inner))
        carry = per_head(carry, collector)[0:1]
        keep = spread(jnp.broadcast_to(jnp.exp(final) * mask, (8, LANES)), selector, heads)[0:1]
        state[...] = keep * dstate + mm(c_low, from_start, ((0,), (0,)))
        later[...] = old
        skip = wide_ref[1:2, :]
        flow = dy_low.astype(F32) * (y - skip * xs) - scaled_low.astype(F32) * dscaled
        dlog = per_head(flow, collector) + jnp.where(last, carry, 0.0)
        tri = (iota((CHUNK, CHUNK), 1) >= iota((CHUNK, CHUNK), 0)).astype(F32)
        dstep = mm_exact(tri, dlog)
        ddelta = per_head(xs * dscaled, collector) + head[1:2] * dstep
        draw = ddelta * sigmoid(raw + head[0:1]) * mask
        head_out[0:1, :] += jnp.sum(draw, 0, keepdims=True)
        head_out[1:2, :] += jnp.sum(delta * dstep, 0, keepdims=True)
        wide_out[0:1, :] += jnp.sum(mixed_here * g, 0, keepdims=True)
        wide_out[1:2, :] += jnp.sum(dy * xs, 0, keepdims=True)
        dxs = wide_delta * dscaled + skip * dy
        pad[at, :] = jnp.concatenate([dxs, db_state, dc_state], 1) * slope
        grad_ref[at, split:] = draw.astype(BF16)
    for chunk in range(ROWS // CHUNK):
        at = slice(chunk * CHUNK, (chunk + 1) * CHUNK)
        p = p_ref[at, :]
        total = jnp.zeros((CHUNK, conv), F32)
        for tap in range(4):
            begin = chunk * CHUNK + 3 - tap
            shifted = pad[begin : begin + CHUNK, :]
            total = total + taps_ref[tap : tap + 1, :] * shifted
            taps_out[tap : tap + 1, :] += jnp.sum(p * shifted, 0, keepdims=True)
        taps_out[4:5, :] += jnp.sum(pad[at, :], 0, keepdims=True)
        grad_ref[at, inner:split] = total.astype(BF16)
    part_ref[...] = mm(grad_ref[...], w_ref[:, : split + LANES], ((1,), (1,))).astype(part_ref.dtype)


def constants(inner, heads):
    width = inner // heads
    lane = np.arange(LANES)[:, None]
    channel = np.arange(inner)[None, :] // width
    selector = ((lane % heads == channel) & (lane < 2 * heads)).astype(np.float32)
    collector = (lane == channel).astype(np.float32).T
    return jnp.asarray(selector, BF16), jnp.asarray(collector, BF16)


def forward_call(rows, w, taps, head, wide, inner, pair, heads):
    length, width = rows.shape
    count = length // ROWS
    conv = inner + pair
    states = pair // 2
    selector, _ = constants(inner, heads)
    whole = lambda array: pl.BlockSpec(array.shape, lambda i: (0,) * array.ndim)
    by_rows = lambda columns: pl.BlockSpec((ROWS, columns), lambda i: (i, 0))
    chunks = ROWS // CHUNK
    out = lambda columns, kind=F32: jax.ShapeDtypeStruct((length, columns), kind)
    return pl.pallas_call(
        partial(forward_kernel, (inner, pair, heads)),
        grid=(count,),
        in_specs=[by_rows(width), whole(w), whole(taps), whole(head), whole(wide), whole(selector)],
        out_specs=[
            by_rows(width),
            pl.BlockSpec((1, 8, ROWS), lambda i: (i, 0, 0)),
            by_rows(inner),
            by_rows(conv),
            by_rows(conv),
            by_rows(LANES),
            by_rows(inner),
            pl.BlockSpec((chunks, states, inner), lambda i: (i, 0, 0)),
        ],
        out_shape=[
            out(width, BF16),
            jax.ShapeDtypeStruct((count, 8, ROWS), F32),
            out(inner),
            out(conv),
            out(conv),
            out(LANES),
            out(inner),
            jax.ShapeDtypeStruct((count * chunks, states, inner), F32),
        ],
        scratch_shapes=[pltpu.VMEM((states, inner), F32), pltpu.VMEM((ROWS + 8, conv), F32)],
        compiler_params=pltpu.CompilerParams(vmem_limit_bytes=56 * 2**20),
        name="layer_forward",
    )(rows, w, taps, head, wide, selector)


def backward_call(e, scales, w, taps, head, wide, saved, inner, pair, heads):
    length, width = e.shape
    count = length // ROWS
    conv = inner + pair
    states = pair // 2
    split = inner + conv
    z, p, c, raw, y, s = saved
    selector, collector = constants(inner, heads)
    whole = lambda array: pl.BlockSpec(array.shape, lambda i: (0,) * array.ndim)
    by_rows = lambda columns: pl.BlockSpec((ROWS, columns), lambda i: (count - 1 - i, 0))
    fixed = lambda columns: pl.BlockSpec((8, columns), lambda i: (0, 0))
    chunks = ROWS // CHUNK
    by_block = lambda lead, rows, columns: pl.BlockSpec(
        (lead, rows, columns), lambda i: (count - 1 - i, 0, 0)
    )
    out = lambda columns, kind=F32: jax.ShapeDtypeStruct((length, columns), kind)
    few = lambda columns: jax.ShapeDtypeStruct((8, columns), F32)
    return pl.pallas_call(
        partial(backward_kernel, (inner, pair, heads)),
        grid=(count,),
        in_specs=[
            by_rows(width),
            by_block(1, 8, ROWS),
            whole(w),
            whole(taps),
            whole(head),
            whole(wide),
            whole(selector),
            whole(collector),
            by_rows(inner),
            by_rows(conv),
            by_rows(conv),
            by_rows(LANES),
            by_rows(inner),
            by_block(chunks, states, inner),
        ],
        out_specs=[
            by_rows(width),
            by_rows(split + LANES),
            by_rows(inner),
            fixed(conv),
            fixed(inner),
            fixed(LANES),
        ],
        out_shape=[
            out(width, BF16),
            out(split + LANES, BF16),
            out(inner, BF16),
            few(conv),
            few(inner),
            few(LANES),
        ],
        scratch_shapes=[
            pltpu.VMEM((states, inner), F32),
            pltpu.VMEM((states, inner), F32),
            pltpu.VMEM((ROWS + 8, conv), F32),
        ],
        compiler_params=pltpu.CompilerParams(vmem_limit_bytes=56 * 2**20),
        name="layer_backward",
    )(e, scales, w, taps, head, wide, selector, collector, z, p, c, raw, y, s)


def swap(value):
    return lax.ppermute(value, "pipe", [(0, 1), (1, 0)])


def both_layers(value, first):
    other = swap(value)
    return jnp.where(first, value, other), jnp.where(first, other, value)


def by_layer(values, first):
    mine = jnp.where(first, values[0], values[1])
    theirs = swap(jnp.where(first, values[1], values[0]).astype(BF16)).astype(F32)
    return jnp.where(first, jnp.stack([mine, theirs]), jnp.stack([theirs, mine]))


def body(inputs, out_grad, norm_gain, in_gate_x, in_read_write, in_step, conv_main, conv_state,
         step_bias, log_rate, skip_gain, gate_gain, out_weight):
    _, part, width = inputs.shape
    inner = out_weight.shape[2]
    pair = in_read_write.shape[2]
    heads = step_bias.shape[1]
    whole_inner = inner * lax.axis_size("tensor")
    split = 2 * inner + pair
    blocks = lax.axis_size("tensor")
    pipe = lax.axis_index("pipe")
    first = pipe == 0
    shard = jnp.concatenate(
        [
            in_gate_x[0, :, 0],
            in_gate_x[0, :, 1],
            in_read_write[0],
            jnp.pad(in_step[0], ((0, 0), (0, LANES - heads))),
            out_weight[0],
        ],
        1,
    )
    taps = jnp.pad(jnp.concatenate([conv_main[0], conv_state[0]], 1), ((0, 3), (0, 0)))
    rate = -jnp.exp(log_rate[0])
    head = jnp.stack([step_bias[0], rate, jnp.ones_like(rate)])
    head = jnp.pad(head, ((0, 5), (0, LANES - heads)))
    wide = jnp.stack([gate_gain[0], jnp.repeat(skip_gain[0], inner // heads)])
    wide = jnp.pad(wide, ((0, 6), (0, 0)))
    shards = both_layers(shard, first)
    weights = [lax.all_gather(item, "dp", axis=0, tiled=True) for item in shards]
    gains, taps, head, wide = (
        both_layers(item, first) for item in (norm_gain, taps, head, wide)
    )
    residual = lax.dynamic_index_in_dim(inputs, pipe, 0, False).astype(F32)
    kept = []
    activations = []
    for layer in range(2):
        scale = lax.rsqrt(jnp.mean(residual * residual, -1, keepdims=True) + EPS)
        normed = (residual * scale * gains[layer]).astype(BF16)
        rows = lax.all_gather(normed, "tensor", axis=0, tiled=True)
        partial_rows, squares, *saved = forward_call(
            rows, weights[layer], taps[layer], head[layer], wide[layer], inner, pair, heads
        )
        squares = lax.psum_scatter(squares, "tensor", scatter_dimension=0, tiled=True)[0, 0]
        summed = lax.psum_scatter(partial_rows, "tensor", scatter_dimension=0, tiled=True)
        inverse = lax.rsqrt(squares / whole_inner + EPS)
        branch = inverse[:, None] * summed.astype(F32)
        kept.append((residual, scale, rows, inverse, branch, saved))
        residual = residual + branch
        activations.append(residual)
    activations = by_layer(activations, first)
    error = lax.dynamic_index_in_dim(out_grad, pipe, 0, False).astype(F32)
    input_grads = [None, None]
    large = [None, None]
    small = [None, None]
    for layer in (1, 0):
        before, scale, rows, inverse, branch, saved = kept[layer]
        sent = error.astype(BF16)
        dots = jnp.sum(sent.astype(F32) * branch, -1) / whole_inner
        scales = jnp.pad(jnp.stack([inverse, dots]), ((0, 6), (0, 0)))[None]
        scales = lax.all_gather(scales, "tensor", axis=0, tiled=True)
        errors = lax.all_gather(sent, "tensor", axis=0, tiled=True)
        partial_rows, grad, mixed, taps_out, wide_out, head_out = backward_call(
            errors, scales, weights[layer], taps[layer], head[layer], wide[layer], saved,
            inner, pair, heads,
        )
        summed = lax.psum_scatter(partial_rows, "tensor", scatter_dimension=0, tiled=True)
        summed = summed.astype(F32)
        unit = before * scale
        scaled = summed * gains[layer]
        mean = jnp.mean(scaled * unit, -1, keepdims=True)
        error = error + scale * (scaled - unit * mean)
        input_grads[layer] = error
        grad_in = jnp.einsum("td,tc->dc", rows, grad, preferred_element_type=F32)
        grad_out = jnp.einsum("td,tc->dc", errors, mixed, preferred_element_type=F32)
        large[layer] = jnp.concatenate([grad_in, grad_out], 1).astype(BF16)
        small[layer] = (
            taps_out[:5, :inner],
            wide_out[0],
            wide_out[1].reshape(heads, -1).sum(1),
            head_out[0, :heads],
            head_out[1, :heads] * head[layer][1, :heads],
            taps_out[:5, inner:],
            jnp.sum(summed * unit, 0),
        )
    input_grads = by_layer(input_grads, first)
    reduced = [lax.psum_scatter(item, "dp", scatter_dimension=0, tiled=True) for item in large]
    mine = jnp.where(first, reduced[0], reduced[1]).astype(F32)
    theirs = swap(jnp.where(first, reduced[1], reduced[0])).astype(F32)
    large = mine + theirs
    state_grad = lax.psum_scatter(
        large[:, 2 * inner : split], "tensor", scatter_dimension=0, tiled=True
    )
    few = [jnp.concatenate([item.reshape(-1) for item in one]) for one in small]
    few = lax.psum(jnp.stack(few), ("pipe", "dp"))
    few = jnp.where(first, few[0], few[1])
    shared = lax.psum(few[-(5 * pair + width) :], "tensor")
    sizes = np.cumsum([5 * inner, inner, heads, heads, heads])
    main, gate, skip, bias, rates = jnp.split(few[: sizes[-1]], sizes[:-1])
    return (
        activations[None],
        input_grads[None],
        shared[None, 5 * pair :],
        large[:, : 2 * inner].reshape(1, -1, 2, inner),
        state_grad[None],
        large[None, :, split : split + heads],
        main.reshape(1, 5, inner),
        shared[: 5 * pair].reshape(1, 5, pair),
        bias[None],
        rates[None],
        skip[None],
        gate[None],
        large[None, :, split + LANES :],
    )


def solution(mesh):
    in_specs = (
        P("dp", "tensor", None),
        P("dp", "tensor", None),
        P("pipe", None),
        P("pipe", "dp", None, "tensor"),
        P("pipe", "dp", None),
        P("pipe", "dp", "tensor"),
        P("pipe", None, "tensor"),
        P("pipe", None, None),
        P("pipe", "tensor"),
        P("pipe", "tensor"),
        P("pipe", "tensor"),
        P("pipe", "tensor"),
        P("pipe", "dp", "tensor"),
    )
    out_specs = (
        P("pipe", "dp", "tensor", None),
        P("pipe", "dp", "tensor", None),
        P("pipe", None),
        P("pipe", "dp", None, "tensor"),
        P("pipe", ("dp", "tensor"), None),
        P("pipe", "dp", "tensor"),
        P("pipe", None, "tensor"),
        P("pipe", None, None),
        P("pipe", "tensor"),
        P("pipe", "tensor"),
        P("pipe", "tensor"),
        P("pipe", "tensor"),
        P("pipe", "dp", "tensor"),
    )
    return jax.shard_map(body, mesh=mesh, in_specs=in_specs, out_specs=out_specs, check_vma=False)
```

time: 2180 us -> 713 us (0.33)
  local copies, waits for them, and re-layouts: 496 us -> 10.8 us
  waiting for transfers between devices: 788 us -> 371 us
  matrix products: 305 us -> 13.6 us
  blocking collectives: 343 us -> 167 us
  other arithmetic: 197 us -> 35.4 us
  Pallas kernels: 0 us -> 85.9 us
    dynamic_update_slice x48 -> x0, local copies, waits for them, and re-layouts: 309 us -> none  [scan_ssd(): final, outputs = lax.scan(stepper, start, blocks)]
    dot_general x168 -> x4, matrix products: 291 us -> 13.6 us  [the longest x2 7.52 us: body(): grad_in = jnp.einsum('td,tc->dc', rows, grad, preferred_element_type=F32)]
    reduce_scatter x8 -> x9, waiting for transfers between devices: 414 us -> 152 us  [the longest x4 93.3 us: body(): lax.psum_scatter(partial_rows, 'tensor', scatter_dimension=0, tiled=True)]
    psum x8 -> x2, blocking collectives: 296 us -> 142 us  [the longest x1 127 us: body(): few = lax.psum(jnp.stack(few), ('pipe', 'dp'))]
    unnamed x20 -> x15, waiting for transfers between devices: 145 us -> 1.95 us
    pallas_call x0 -> x4, Pallas kernels: none -> 85.9 us  [the longest x2 49.5 us: backward_call(): pl.pallas_call(partial(backward_kernel, (inner, pair, heads)), grid=(coun...]
    another operation x125 -> x8, other arithmetic: 57.6 us -> 3.64 us  [the longest x3 3.5 us: by_layer(): jnp.stack([mine, theirs])]
    ppermute x4 -> x8, waiting for transfers between devices: 73.4 us -> 20.8 us  [swap(): return lax.ppermute(value, 'pipe', [(0, 1), (1, 0)])]
  transfers between devices with their start and end apart: 22 -> 23, of which waited for: 17 -> 18; matrix products, arithmetic and copies ran while one was open for 13% -> 7% of each run, Pallas kernels for 0% -> 0%
where the time goes in v1:
time: 713 us; the launch traced here: 712 us
  waiting for transfers between devices  371 us (52%)
  blocking collectives  167 us (23%)
  Pallas kernels  85.9 us (12%)
  other arithmetic  35.4 us (5%)
  between operations  14.4 us (2%)
  matrix products  13.6 us (2%)
  starting transfers between devices  12.8 us (2%)
  local copies, waits for them, and re-layouts  10.8 us (2%)
    psum x1, blocking collectives, body(): few = lax.psum(jnp.stack(few), ('pipe', 'dp'))  127 us
    all_gather x2, waiting for transfers between devices, body(): lax.all_gather(item, 'dp', axis=0, tiled=True)  113 us
    reduce_scatter x4, waiting for transfers between devices, body(): lax.psum_scatter(partial_rows, 'tensor', scatter_dimension=0, tiled=True)  93.3 us
    all_gather x2, waiting for transfers between devices, body(): rows = lax.all_gather(normed, 'tensor', axis=0, tiled=True)  49.5 us
    pallas_call x2, Pallas kernels, backward_call(): pl.pallas_call(partial(backward_kernel, (inner, pair, heads)), grid=(coun...  49.5 us
    reduce_scatter x2, waiting for transfers between devices, body(): lax.psum_scatter(squares, 'tensor', scatter_dimension=0, tiled=True)[0, 0]  37.3 us
    pallas_call x2, Pallas kernels, forward_call(): pl.pallas_call(partial(forward_kernel, (inner, pair, heads)), grid=(count...  36.4 us
    all_gather x2, waiting for transfers between devices, body(): errors = lax.all_gather(sent, 'tensor', axis=0, tiled=True)  34.5 us
  transfers between devices with their start and end apart: 23, of which 18 were waited for; matrix products, arithmetic and copies ran while one was open for 7% of the time, Pallas kernels for 0%

profile of v1, /device:TPU:0, one launch (start us, length us, event | category | flops | bytes accessed | tf_op | source)
XLA Modules:
  0.0 711.6 jit_solution(17741912964306071366)
XLA Ops:
  7.3 2.1 collective-permute-start
  9.3 1.2 fusion.19
  11.9 2.0 fusion.16
  14.4 2.1 collective-permute-start.1
  16.4 4.9 collective-permute-done.1
  21.4 0.8 broadcast_select_fusion.1
  22.4 1.7 collective-permute-start.3
  24.8 1.7 collective-permute-start.2
  27.1 1.0 collective-permute-done.4
  29.3 18.0 %all-gather.10.cloned.1.call-done.rows_ref = bf16[1024,1024]{1,0:T(8,128)(2,1)} async-done(((bf16[256,1024]{1,0:T(8,128)(2,1)}), bf16[1024,1024]{1,0:T(8,128)(2,1)}) %all-gather.10.cloned.1.call-update) | async-done | bytes 2097168 | tf_op jit(solution)/shard_map/all_gather | solution.py:423
  47.3 58.3 %all-gather.12.cloned.1.call-done.w_ref = bf16[1024,1920]{1,0:T(8,128)(2,1)} async-done(((bf16[64,1920]{1,0:T(8,128)(2,1)}), bf16[1024,1920]{1,0:T(8,128)(2,1)}) %all-gather.12.cloned.1.call-update) | async-done | bytes 3932176 | tf_op jit(solution)/shard_map/all_gather | solution.py:413
  105.7 18.2 %layer_forward.2 = (bf16[1024,1024]{1,0:T(8,128)(2,1)}, f32[4,8,256]{2,1,0:T(8,128)}, f32[1024,512]{1,0:T(8,128)}, f32[1024,768]{1,0:T(8,128)}, f32[1024,768]{1,...) custom-call(bf16[1024,1024]{1,0:T(8,128)(2,1)} %all-gather.10.cloned.1.call-done.rows_ref, ...), custom_call_target="tpu_custom_call" | custom-call | tf_op jit(solution)/shard_map/layer_forward/pallas_call | solution.py:278
  125.1 17.7 %reduce-scatter.10.cloned.1.call-done = f32[1,8,256]{2,1,0:T(8,128)} async-done(((f32[4,8,256]{2,1,0:T(8,128)}), f32[1,8,256]{2,1,0:T(8,128)}) %reduce-scatter.10.cloned.1.call-update) | async-done | bytes 8208 | tf_op jit(solution)/shard_map/reduce_scatter | solution.py:427
  142.8 0.7 fusion.25
  143.5 31.7 %reduce-scatter.12.cloned.1.call-done = bf16[256,1024]{1,0:T(8,128)(2,1)} async-done(((bf16[1024,1024]{1,0:T(8,128)(2,1)}), bf16[256,1024]{1,0:T(8,128)(2,1)}) %reduce-scatter.12.cloned.1.call-update) | async-done | bytes 524304 | tf_op jit(solution)/shard_map/reduce_scatter | solution.py:428
  175.2 1.4 multiply_reduce_fusion.1
  176.6 2.1 multiply_convert_fusion
  178.8 54.2 %all-gather.16.cloned.1.call-done.w_ref = bf16[1024,1920]{1,0:T(8,128)(2,1)} async-done(((bf16[64,1920]{1,0:T(8,128)(2,1)}), bf16[1024,1920]{1,0:T(8,128)(2,1)}) %all-gather.16.cloned.1.call-update) | async-done | bytes 3932176 | tf_op jit(solution)/shard_map/all_gather | solution.py:413
  233.0 31.5 %all-gather.14.cloned.1.call-done.rows_ref = bf16[1024,1024]{1,0:T(8,128)(2,1)} async-done(((bf16[256,1024]{1,0:T(8,128)(2,1)}), bf16[1024,1024]{1,0:T(8,128)(2,1)}) %all-gather.14.cloned.1.call-update) | async-done | bytes 2097168 | tf_op jit(solution)/shard_map/all_gather | solution.py:423
  264.5 18.2 %layer_forward.3 = (bf16[1024,1024]{1,0:T(8,128)(2,1)}, f32[4,8,256]{2,1,0:T(8,128)}, f32[1024,512]{1,0:T(8,128)}, f32[1024,768]{1,0:T(8,128)}, f32[1024,768]{1,...) custom-call(bf16[1024,1024]{1,0:T(8,128)(2,1)} %all-gather.14.cloned.1.call-done.rows_ref, ...), custom_call_target="tpu_custom_call" | custom-call | tf_op jit(solution)/shard_map/layer_forward/pallas_call | solution.py:278
  282.8 0.7 reduce-scatter.16.cloned.1.call-update
  283.6 19.6 %reduce-scatter.14.cloned.1.call-done = f32[1,8,256]{2,1,0:T(8,128)} async-done(((f32[4,8,256]{2,1,0:T(8,128)}), f32[1,8,256]{2,1,0:T(8,128)}) %reduce-scatter.14.cloned.1.call-update) | async-done | bytes 8208 | tf_op jit(solution)/shard_map/reduce_scatter | solution.py:427
  303.2 0.7 fusion.23
  303.9 31.8 %reduce-scatter.16.cloned.1.call-done = bf16[256,1024]{1,0:T(8,128)(2,1)} async-done(((bf16[1024,1024]{1,0:T(8,128)(2,1)}), bf16[256,1024]{1,0:T(8,128)(2,1)}) %reduce-scatter.16.cloned.1.call-update) | async-done | bytes 524304 | tf_op jit(solution)/shard_map/reduce_scatter | solution.py:428
  335.7 2.1 fusion.11
  337.9 0.7 fusion.37
  338.6 12.8 %all-gather.1 = f32[32,256]{1,0:T(8,128)} all-gather(f32[8,256]{1,0:T(8,128)S(1)} %select_maximum_fusion.3), channel_id=3, replica_groups=mesh['pipe'=2,'dp'=16,'tensor'=4] {'tensor'}, dimensions={0}, use_global_device_ids=true | all-gather | bytes 40960 | tf_op jit(solution)/shard_map/all_gather | solution.py:444
  351.4 17.2 %all-gather.20.cloned.1.call-done = bf16[1,1024,1024]{2,1,0:T(8,128)(2,1)} async-done(((bf16[1,256,1024]{2,1,0:T(8,128)(2,1)}), bf16[1,1024,1024]{2,1,0:T(8,128)(2,1)}) %all-gather.20.cloned.1.call-update) | async-done | bytes 2097168 | tf_op jit(solution)/shard_map/all_gather | solution.py:445
  368.5 24.7 %layer_backward.2 = (bf16[1024,1024]{1,0:T(8,128)(2,1)}, bf16[1024,1408]{1,0:T(8,128)(2,1)}, bf16[1024,512]{1,0:T(8,128)(2,1)}, f32[8,768]{1,0:T(8,128)}, f32[8,512]{1,0:T(8,128)}, /*index=5*/f32[8,128]{1,0:T(8,128)}) custom-call(bf16[1024,1024]{1,0:T(8,128)(2,1)} %bitcast.99, f32[4,8,256]{2,1,0:T(8,128)} %bitcast.103, ...), custom_call_target="tpu_custom_call" | custom-call | tf_op jit(solution)/shard_map/layer_backward/pallas_call | solution.py:325
  393.4 29.7 %reduce-scatter.18.cloned.1.call-done = bf16[256,1024]{1,0:T(8,128)(2,1)} async-done(((bf16[1024,1024]{1,0:T(8,128)(2,1)}), bf16[256,1024]{1,0:T(8,128)(2,1)}) %reduce-scatter.18.cloned.1.call-update) | async-done | bytes 524304 | tf_op jit(solution)/shard_map/reduce_scatter | solution.py:450
  423.1 1.6 fusion.10
  424.7 3.3 multiply_reduce_fusion
  428.1 0.7 fusion.36
  428.8 12.6 %all-gather.2 = f32[32,256]{1,0:T(8,128)} all-gather(f32[8,256]{1,0:T(8,128)S(1)} %select_maximum_fusion.2), channel_id=4, replica_groups=mesh['pipe'=2,'dp'=16,'tensor'=4] {'tensor'}, dimensions={0}, use_global_device_ids=true | all-gather | bytes 40960 | tf_op jit(solution)/shard_map/all_gather | solution.py:444
  441.5 17.3 %all-gather.18.cloned.1.call-done.e_ref = bf16[1024,1024]{1,0:T(8,128)(2,1)} async-done(((bf16[256,1024]{1,0:T(8,128)(2,1)}), bf16[1024,1024]{1,0:T(8,128)(2,1)}) %all-gather.18.cloned.1.call-update) | async-done | bytes 2097168 | tf_op jit(solution)/shard_map/all_gather | solution.py:445
  458.8 24.7 %layer_backward.3 = (bf16[1024,1024]{1,0:T(8,128)(2,1)}, bf16[1024,1408]{1,0:T(8,128)(2,1)}, bf16[1024,512]{1,0:T(8,128)(2,1)}, f32[8,768]{1,0:T(8,128)}, f32[8,512]{1,0:T(8,128)}, /*index=5*/f32[8,128]{1,0:T(8,128)}) custom-call(bf16[1024,1024]{1,0:T(8,128)(2,1)} %all-gather.18.cloned.1.call-done.e_ref, f32[4,8,256]{2,1,0:T(8,128)} %bitcast.102, ...), custom_call_target="tpu_custom_call" | custom-call | tf_op jit(solution)/shard_map/layer_backward/pallas_call | solution.py:325
  483.8 0.9 copy-done.22
  484.7 3.0 convolution_convert_fusion.2
  487.8 3.8 convolution_convert_fusion
  491.6 2.2 pad_maximum_fusion.1
  493.8 1.1 copy-done.23
  495.0 3.0 convolution_convert_fusion.3
  498.1 3.8 convolution_convert_fusion.1
  501.8 2.2 pad_maximum_fusion
  504.1 1.6 collective-permute-start.5
  505.7 0.8 slice_reduce_fusion.1
  506.8 0.8 multiply_bitcast_fusion
  507.6 10.5 %collective-permute-done.5 = bf16[256,1024]{1,0:T(8,128)(2,1)} collective-permute-done((bf16[256,1024]{1,0:T(8,128)(2,1)}, bf16[256,1024]{1,0:T(8,128)(2,1)}, u32[]{:S(2)}, u32[]{:S(2)}) %collective-permute-start.5) | collective-permute-done | bytes 524320 | tf_op jit(solution)/shard_map/ppermute | solution.py:371
  518.1 1.1 bitcast_convert_fusion.1
  519.3 1.5 maximum_select_fusion
  520.8 0.8 slice_reduce_fusion.2
  521.8 0.8 multiply_bitcast_fusion.1
  522.6 1.5 fusion.18
  524.2 2.3 fusion.14
  526.5 1.6 collective-permute-start.6
  528.1 126.8 %psum.14 = f32[2,5400]{1,0:T(2,128)S(1)} all-reduce(f32[2,5400]{1,0:T(2,128)S(1)} %pad_maximum_fusion.2), channel_id=1, replica_groups=mesh['pipe'=2,'dp'=16,'tensor'=4] {'pipe','dp'}, use_global_device_ids=true, to_apply=%region_16.17 | all-reduce | flops 10800 | bytes 86400 | tf_op jit(solution)/shard_map/psum | solution.py:478
  656.8 15.2 %psum.15 = f32[2304]{0:T(1024)S(1)} all-reduce(f32[2304]{0:T(1024)S(1)} %slice_reduce_fusion), channel_id=1, replica_groups=mesh['pipe'=2,'dp'=16,'tensor'=4] {'tensor'}, use_global_device_ids=true, to_apply=%region_17.18 | all-reduce | flops 2304 | bytes 18432 | tf_op jit(solution)/shard_map/psum | solution.py:480
  673.2 4.2 reduce-scatter.22.cloned.1.call-done
  677.5 1.0 broadcast_select_fusion
  678.4 0.7 collective-permute-start.7
  679.3 1.5 maximum_select_fusion.1
  680.9 3.8 collective-permute-done.7
  686.2 0.9 reshape.296
  687.8 17.3 %reduce-scatter.26.cloned.1.call-done = f32[16,256]{1,0:T(8,128)} async-done(((f32[64,256]{1,0:T(8,128)}), f32[16,256]{1,0:T(8,128)}) %reduce-scatter.26.cloned.1.call-update) | async-done | bytes 16400 | tf_op jit(solution)/shard_map/reduce_scatter | solution.py:474
  (145 shorter events, 12.4 us)
Async XLA Ops:
  7.2 6.8 copy-start.17
  7.2 6.9 copy-start.8
  7.2 7.1 copy-start.11
  7.2 7.1 %copy-start.10 = (bf16[1,64,512]{2,1,0:T(8,128)(2,1)S(1)}, bf16[1,64,512]{2,1,0:T(8,128)(2,1)}, u32[]{:S(2)}) copy-start(bf16[1,64,512]{2,1,0:T(8,128)(2,1)} %param.31) | copy-start | bytes 196612
  7.2 40.1 %all-gather.10.cloned.1.call-start = ((), (), s32[]{:S(2)}) async-start(), calls=%async_computation.9 | async-start | bytes 2621440 | tf_op jit(solution)/shard_map/all_gather | solution.py:423
  7.3 3.9 collective-permute-start
  10.6 11.8 %copy-start.24 = (f32[1,8]{1,0:T(1,128)S(1)}, f32[1,8]{1,0:T(1,128)}, u32[]{:S(2)}) copy-start(f32[1,8]{1,0:T(1,128)} %param.28) | copy-start | bytes 100
  10.6 11.8 %copy-start.18 = (f32[1,8]{1,0:T(1,128)S(1)}, f32[1,8]{1,0:T(1,128)}, u32[]{:S(2)}) copy-start(f32[1,8]{1,0:T(1,128)} %param.27) | copy-start | bytes 100
  10.6 13.5 %copy-start.19 = (f32[1,8]{1,0:T(1,128)S(1)}, f32[1,8]{1,0:T(1,128)}, u32[]{:S(2)}) copy-start(f32[1,8]{1,0:T(1,128)} %param.29) | copy-start | bytes 100
  10.6 13.6 %copy-start.15 = (f32[1,512]{1,0:T(1,128)S(1)}, f32[1,512]{1,0:T(1,128)}, u32[]{:S(2)}) copy-start(f32[1,512]{1,0:T(1,128)} %param.30) | copy-start | bytes 6148
  10.6 14.1 %copy-start.16 = (f32[1,5,256]{2,0,1:T(1,128)S(1)}, f32[1,5,256]{2,0,1:T(1,128)}, u32[]{:S(2)}) copy-start(f32[1,5,256]{2,0,1:T(1,128)} %param.26) | copy-start | bytes 15364
  10.6 14.1 %copy-start.14 = (f32[1,5,512]{2,0,1:T(1,128)S(1)}, f32[1,5,512]{2,0,1:T(1,128)}, u32[]{:S(2)}) copy-start(f32[1,5,512]{2,0,1:T(1,128)} %param.25) | copy-start | bytes 30724
  13.9 91.8 %all-gather.12.cloned.1.call-start = ((), (), s32[]{:S(2)}) async-start(), calls=%async_computation.10 | async-start | bytes 4177920 | tf_op jit(solution)/shard_map/all_gather | solution.py:413
  14.4 7.0 collective-permute-start.1
  22.2 120.6 %reduce-scatter.10.cloned.1.call-start = ((), (), s32[]{:S(2)}) async-start(), calls=%async_computation.11 | async-start | bytes 40960 | tf_op jit(solution)/shard_map/reduce_scatter | solution.py:427
  22.4 4.0 collective-permute-start.3
  24.3 3.8 collective-permute-start.4
  24.8 3.9 collective-permute-start.2
  123.9 51.3 %copy-start = (bf16[2,256,1024]{2,1,0:T(8,128)(2,1)S(1)}, bf16[2,256,1024]{2,1,0:T(8,128)(2,1)}, u32[]{:S(2)}) copy-start(bf16[2,256,1024]{2,1,0:T(8,128)(2,1)} %param.19) | copy-start | bytes 3145732
  123.9 51.3 %reduce-scatter.12.cloned.1.call-start = ((), (), s32[]{:S(2)}) async-start(), calls=%async_computation.12 | async-start | bytes 2621440 | tf_op jit(solution)/shard_map/reduce_scatter | solution.py:428
  124.5 108.6 %all-gather.16.cloned.1.call-start = ((), (), s32[]{:S(2)}) async-start(), calls=%async_computation.14 | async-start | bytes 4177920 | tf_op jit(solution)/shard_map/all_gather | solution.py:413
  125.1 139.5 %all-gather.14.cloned.1.call-start = ((), (), s32[]{:S(2)}) async-start(), calls=%async_computation.13 | async-start | bytes 2621440 | tf_op jit(solution)/shard_map/all_gather | solution.py:423
  178.8 124.4 %reduce-scatter.14.cloned.1.call-start = ((), (), s32[]{:S(2)}) async-start(), calls=%async_computation.15 | async-start | bytes 40960 | tf_op jit(solution)/shard_map/reduce_scatter | solution.py:427
  282.7 53.0 %copy-start.9 = (bf16[2,256,1024]{2,1,0:T(8,128)(2,1)S(1)}, bf16[2,256,1024]{2,1,0:T(8,128)(2,1)}, u32[]{:S(2)}) copy-start(bf16[2,256,1024]{2,1,0:T(8,128)(2,1)} %param.20) | copy-start | bytes 3145732
  282.8 52.9 %reduce-scatter.16.cloned.1.call-start = ((), (), s32[]{:S(2)}) async-start(), calls=%async_computation.16 | async-start | bytes 2621440 | tf_op jit(solution)/shard_map/reduce_scatter | solution.py:428
  283.5 85.0 %all-gather.20.cloned.1.call-start = ((), (), s32[]{:S(2)}) async-start(), calls=%async_computation.23 | async-start | bytes 2621440 | tf_op jit(solution)/shard_map/all_gather | solution.py:445
  337.8 85.3 %reduce-scatter.18.cloned.1.call-start = ((), (), s32[]{:S(2)}) async-start(), calls=%async_computation.17 | async-start | bytes 2621440 | tf_op jit(solution)/shard_map/reduce_scatter | solution.py:450
  393.3 29.8 %copy-start.1 = (bf16[256,1024]{1,0:T(8,128)(2,1)S(1)}, bf16[256,1024]{1,0:T(8,128)(2,1)}, u32[]{:S(2)}) copy-start(bf16[256,1024]{1,0:T(8,128)(2,1)} %reduce-scatter.12.cloned.1.call-done) | copy-start | bytes 1572868
  393.3 31.4 %copy-start.2 = (bf16[1,256,1024]{2,1,0:T(8,128)(2,1)S(1)}, bf16[1,256,1024]{2,1,0:T(8,128)(2,1)}, u32[]{:S(2)}) copy-start(bf16[1,256,1024]{2,1,0:T(8,128)(2,1)} %get-tuple-element.90) | copy-start | bytes 1572868
  393.3 65.4 %all-gather.18.cloned.1.call-start = ((), (), s32[]{:S(2)}) async-start(), calls=%async_computation.18 | async-start | bytes 2621440 | tf_op jit(solution)/shard_map/all_gather | solution.py:445
  428.1 94.5 %reduce-scatter.20.cloned.1.call-start = ((), (), s32[]{:S(2)}) async-start(), calls=%async_computation.19 | async-start | bytes 2621440 | tf_op jit(solution)/shard_map/reduce_scatter | solution.py:450
  483.5 1.2 copy-start.22
  483.5 189.7 %reduce-scatter.24.cloned.1.call-start = ((), (), s32[]{:S(2)}) async-start(), calls=%async_computation.21 | async-start | bytes 4177920 | tf_op jit(solution)/shard_map/reduce_scatter | solution.py:470
  484.7 3.0 copy-start.5
  484.7 3.1 copy-start.20
  493.8 1.2 copy-start.23
  493.8 183.7 %reduce-scatter.22.cloned.1.call-start = ((), (), s32[]{:S(2)}) async-start(), calls=%async_computation.20 | async-start | bytes 4177920 | tf_op jit(solution)/shard_map/reduce_scatter | solution.py:470
  495.0 3.0 copy-start.4
  495.0 3.1 copy-start.21
  504.0 1.7 copy-start.12
  504.0 15.3 %copy-start.3 = (f32[1,1,256,1024]{3,2,1,0:T(8,128)S(1)}, f32[1,1,256,1024]{3,2,1,0:T(8,128)}, u32[]{:S(2)}) copy-start(f32[1,1,256,1024]{3,2,1,0:T(8,128)} %get-tuple-element.96) | copy-start | bytes 3145732
  504.0 201.1 %reduce-scatter.26.cloned.1.call-start = ((), (), s32[]{:S(2)}) async-start(), calls=%async_computation.22 | async-start | bytes 81920 | tf_op jit(solution)/shard_map/reduce_scatter | solution.py:474
  504.1 14.1 %collective-permute-start.5 = (bf16[256,1024]{1,0:T(8,128)(2,1)}, bf16[256,1024]{1,0:T(8,128)(2,1)}, u32[]{:S(2)}, u32[]{:S(2)}) collective-permute-start(bf16[256,1024]{1,0:T(8,128)(2,1)} %get-tuple-element.95), channel_id=1, source_target_pairs={{0,64},{64,0},{1,65},{65,1},{2,66},{66,2},{3,67},{67,3},{4,68},{68... | collective-permute-start | bytes 1572872 | tf_op jit(solution)/shard_map/ppermute | solution.py:371
  519.3 1.5 copy-start.13
  526.5 152.7 %collective-permute-start.6 = (bf16[256,1024]{1,0:T(8,128)(2,1)}, bf16[256,1024]{1,0:T(8,128)(2,1)S(1)}, u32[]{:S(2)}, u32[]{:S(2)}) collective-permute-start(bf16[256,1024]{1,0:T(8,128)(2,1)} %get-tuple-element.92), channel_id=1, source_target_pairs={{0,64},{64,0},{1,65},{65,1},{2,66},{66,2},{3,67},{67,3},{4,68},{68... | collective-permute-start | bytes 1572872 | tf_op jit(solution)/shard_map/ppermute | solution.py:371
  678.4 6.3 collective-permute-start.7
  679.3 5.4 copy-start.6
  679.3 5.4 copy-start.7
Sparse Core Ops, SparseCore 0:
  14.0 33.2 all-gather.9
  50.3 55.2 all-gather.11
  124.0 18.7 reduce-scatter.9
  145.8 29.3 reduce-scatter.11
  178.0 54.9 all-gather.15
  235.1 29.3 all-gather.13
  282.9 20.2 reduce-scatter.13
  306.3 29.3 reduce-scatter.15
  337.9 30.5 all-gather.19
  393.4 29.6 reduce-scatter.17
  428.2 30.5 all-gather.17
  483.7 29.6 reduce-scatter.19
  517.4 78.6 reduce-scatter.23
  600.1 77.3 reduce-scatter.21
  686.3 18.7 reduce-scatter.25

commit v2 on v1

v2 whole, which is shorter than its diff:
```python
from functools import partial

import jax
import jax.numpy as jnp
import numpy as np
from jax import lax
from jax.experimental import pallas as pl
from jax.experimental.pallas import tpu as pltpu
from jax.sharding import PartitionSpec as P

F32, BF16 = jnp.float32, jnp.bfloat16
EPS = 1e-05
ROWS = 256
CHUNK = 128
LANES = 128
EXACT = lax.Precision.HIGHEST


def mm(left, right, contract=((1,), (0,))):
    return lax.dot_general(left, right, (contract, ((), ())), preferred_element_type=F32)


def mm_exact(left, right, contract=((1,), (0,))):
    return lax.dot_general(
        left, right, (contract, ((), ())), precision=EXACT, preferred_element_type=F32
    )


def spread(value, selector, heads):
    high = value.astype(BF16).astype(F32)
    both = high + pltpu.roll(value - high, heads, 1)
    return mm(both.astype(BF16), selector)


def per_head(value, collector):
    high = value.astype(BF16)
    low = (value - high.astype(F32)).astype(BF16)
    return mm(high, collector) + mm(low, collector)


def softplus(value):
    small = jnp.exp(-jnp.abs(value))
    series = small * (1.0 - small * (0.5 - small * (1.0 / 3.0 - small * 0.25)))
    return jnp.maximum(value, 0.0) + jnp.where(small < 0.01, series, jnp.log(1.0 + small))


def sigmoid(value):
    return 1.0 / (1.0 + jnp.exp(-value))


def iota(shape, axis):
    return lax.broadcasted_iota(jnp.int32, shape, axis)


def column_to_row(column):
    size = column.shape[0]
    same = iota((size, size), 0) == iota((size, size), 1)
    return jnp.sum(jnp.where(same, column, 0.0), 0, keepdims=True)


def row_to_column(row):
    size = row.shape[1]
    same = iota((size, size), 0) == iota((size, size), 1)
    return jnp.sum(jnp.where(same, row, 0.0), 1, keepdims=True)


def steps(raw, bias, rate, mask):
    delta = softplus(raw + bias) * mask
    tri = (iota((CHUNK, CHUNK), 0) >= iota((CHUNK, CHUNK), 1)).astype(F32)
    log_decay = mm_exact(tri, delta * rate)
    return delta, log_decay


def forward_kernel(sizes, rows_ref, w_ref, few_ref, selector_ref,
                   part_ref, squares_ref, z_ref, p_ref, c_ref, raw_ref, y_ref, s_ref, state, pad):
    inner, pair, heads = sizes
    states = pair // 2
    split = inner + inner + pair
    conv = inner + pair

    @pl.when(pl.program_id(0) == 0)
    def _():
        state[...] = jnp.zeros_like(state)
        pad[0:8, :] = jnp.zeros((8, conv), F32)

    @pl.when(pl.program_id(0) > 0)
    def _():
        pad[0:8, :] = pad[ROWS : ROWS + 8, :]

    projected = mm(rows_ref[...], w_ref[:, : split + LANES])
    z_ref[...] = projected[:, :inner]
    p_ref[...] = projected[:, inner:split]
    pad[8 : ROWS + 8, :] = projected[:, inner:split]
    raw_ref[...] = projected[:, split:]
    selector = selector_ref[...]
    bias = few_ref[0, 5:6, inner : inner + LANES]
    rate = few_ref[0, 5:6, inner + LANES : inner + 2 * LANES]
    gain = few_ref[0, 5:6, :inner]
    skip = few_ref[0, 6:7, :inner]
    mask = (iota((1, LANES), 1) < heads).astype(F32)
    first = iota((CHUNK, LANES), 1) < LANES // 2
    causal = iota((CHUNK, CHUNK), 0) >= iota((CHUNK, CHUNK), 1)
    squares = []
    for chunk in range(ROWS // CHUNK):
        at = slice(chunk * CHUNK, (chunk + 1) * CHUNK)
        c = jnp.broadcast_to(few_ref[0, 4:5, :], (CHUNK, conv))
        for tap in range(4):
            begin = chunk * CHUNK + 5 + tap
            c = c + few_ref[0, tap : tap + 1, :] * pad[begin : begin + CHUNK, :]
        c_ref[at, :] = c
        value = c * sigmoid(c)
        xs = value[:, :inner]
        b_low = value[:, inner : inner + states].astype(BF16)
        c_low = value[:, inner + states :].astype(BF16)
        delta, log_decay = steps(raw_ref[at, :], bias, rate, mask)
        turned = log_decay.T
        final = log_decay[CHUNK - 1 : CHUNK, :]
        scaled = spread(delta, selector, heads) * xs
        scaled_low = scaled.astype(BF16)
        products = jnp.where(causal, mm(c_low, b_low, ((1,), (1,))), 0.0)
        within = []
        for two in range(heads // 2):
            lanes = slice(two * LANES, (two + 1) * LANES)
            parts = []
            for h in (2 * two, 2 * two + 1):
                gap = jnp.minimum(log_decay[:, h : h + 1] - turned[h : h + 1, :], 0.0)
                parts.append(mm((products * jnp.exp(gap)).astype(BF16), scaled_low[:, lanes]))
            within.append(jnp.where(first, parts[0], parts[1]))
        old = state[...]
        s_ref[chunk] = old
        carried = mm(c_low, old.astype(BF16)) * spread(jnp.exp(log_decay) * mask, selector, heads)
        y = jnp.concatenate(within, 1) + carried + skip * xs
        y_ref[at, :] = y
        ends = (spread(jnp.exp(final - log_decay) * mask, selector, heads) * scaled).astype(BF16)
        keep = spread(jnp.broadcast_to(jnp.exp(final) * mask, (8, LANES)), selector, heads)[0:1]
        state[...] = keep * old + mm(b_low, ends, ((0,), (0,)))
        z = z_ref[at, :]
        gated = y * (z * sigmoid(z))
        squares.append(jnp.sum(gated * gated, 1, keepdims=True))
        mixed = (gated * gain).astype(BF16)
        part_ref[at, :] = mm(mixed, w_ref[:, split + LANES :], ((1,), (1,))).astype(part_ref.dtype)
    row = column_to_row(jnp.concatenate(squares, 0))
    squares_ref[0] = jnp.broadcast_to(row, (8, ROWS))


def backward_kernel(sizes, e_ref, scales_ref, w_ref, few_ref, selector_ref,
                    collector_ref, z_ref, p_ref, c_ref, raw_ref, y_ref, s_ref,
                    part_ref, grad_ref, mixed_ref, few_out, state, later, pad):
    inner, pair, heads = sizes
    states = pair // 2
    split = inner + inner + pair
    conv = inner + pair

    @pl.when(pl.program_id(0) == 0)
    def _():
        state[...] = jnp.zeros_like(state)
        later[...] = jnp.zeros_like(later)
        pad[ROWS : ROWS + 8, :] = jnp.zeros((8, conv), F32)
        few_out[...] = jnp.zeros_like(few_out)

    @pl.when(pl.program_id(0) > 0)
    def _():
        pad[ROWS : ROWS + 8, :] = pad[0:8, :]

    selector = selector_ref[...]
    collector = collector_ref[...]
    bias = few_ref[0, 5:6, inner : inner + LANES]
    rate = few_ref[0, 5:6, inner + LANES : inner + 2 * LANES]
    gain = few_ref[0, 5:6, :inner]
    skip = few_ref[0, 6:7, :inner]
    mask = (iota((1, LANES), 1) < heads).astype(F32)
    first = iota((CHUNK, LANES), 1) < LANES // 2
    later_in = iota((CHUNK, CHUNK), 1) >= iota((CHUNK, CHUNK), 0)
    last = iota((CHUNK, LANES), 0) == CHUNK - 1
    inverse = row_to_column(scales_ref[0, 0:1, :])
    inner_dot = row_to_column(scales_ref[0, 1:2, :])
    mixed_grad = mm(e_ref[...], w_ref[:, split + LANES :])
    for chunk in reversed(range(ROWS // CHUNK)):
        at = slice(chunk * CHUNK, (chunk + 1) * CHUNK)
        z = z_ref[at, :]
        y = y_ref[at, :]
        sig = sigmoid(z)
        act = z * sig
        g = y * act * inverse[at]
        mixed_ref[at, :] = (g * gain).astype(BF16)
        mixed_here = mixed_grad[at]
        gated_grad = inverse[at] * (mixed_here * gain - g * inner_dot[at])
        dy = gated_grad * act
        grad_ref[at, :inner] = (gated_grad * y * (sig * (1.0 + z - act))).astype(BF16)
        c = c_ref[at, :]
        csig = sigmoid(c)
        value = c * csig
        slope = csig * (1.0 + c - value)
        xs = value[:, :inner]
        b_low = value[:, inner : inner + states].astype(BF16)
        c_low = value[:, inner + states :].astype(BF16)
        raw = raw_ref[at, :]
        delta, log_decay = steps(raw, bias, rate, mask)
        turned = log_decay.T
        final = log_decay[CHUNK - 1 : CHUNK, :]
        wide_delta = spread(delta, selector, heads)
        scaled = wide_delta * xs
        scaled_low = scaled.astype(BF16)
        dy_low = dy.astype(BF16)
        products = jnp.where(later_in, mm(b_low, c_low, ((1,), (1,))), 0.0)
        dproducts = jnp.zeros((CHUNK, CHUNK), F32)
        within = []
        for two in range(heads // 2):
            lanes = slice(two * LANES, (two + 1) * LANES)
            parts = []
            for odd in range(2):
                h = 2 * two + odd
                mine = first if odd == 0 else ~first
                decay = jnp.exp(jnp.minimum(turned[h : h + 1, :] - log_decay[:, h : h + 1], 0.0))
                parts.append(mm((products * decay).astype(BF16), dy_low[:, lanes]))
                own = jnp.where(mine, scaled_low[:, lanes], jnp.zeros((), BF16))
                dproducts = dproducts + decay * mm(own, dy_low[:, lanes], ((1,), (1,)))
            within.append(jnp.where(first, parts[0], parts[1]))
        dproducts = jnp.where(later_in, dproducts, 0.0).astype(BF16)
        old = s_ref[chunk]
        old_low = old.astype(BF16)
        dstate = state[...]
        dstate_low = dstate.astype(BF16)
        to_end = spread(jnp.exp(final - log_decay) * mask, selector, heads)
        from_start = (spread(jnp.exp(log_decay) * mask, selector, heads) * dy).astype(BF16)
        dscaled = jnp.concatenate(within, 1) + to_end * mm(b_low, dstate_low)
        dc_state = mm(from_start, old_low, ((1,), (1,))) + mm(dproducts, b_low, ((0,), (0,)))
        db_state = mm((to_end * scaled).astype(BF16), dstate_low, ((1,), (1,))) + mm(dproducts, c_low)
        carry = jnp.broadcast_to(jnp.sum(later[...] * dstate, 0, keepdims=True), (8, inner))
        carry = per_head(carry, collector)[0:1]
        keep = spread(jnp.broadcast_to(jnp.exp(final) * mask, (8, LANES)), selector, heads)[0:1]
        state[...] = keep * dstate + mm(c_low, from_start, ((0,), (0,)))
        later[...] = old
        flow = dy_low.astype(F32) * (y - skip * xs) - scaled_low.astype(F32) * dscaled
        dlog = per_head(flow, collector) + jnp.where(last, carry, 0.0)
        tri = (iota((CHUNK, CHUNK), 1) >= iota((CHUNK, CHUNK), 0)).astype(F32)
        dstep = mm_exact(tri, dlog)
        ddelta = per_head(xs * dscaled, collector) + rate * dstep
        draw = ddelta * sigmoid(raw + bias) * mask
        few_out[5:6, inner : inner + LANES] += jnp.sum(draw, 0, keepdims=True)
        few_out[5:6, inner + LANES : inner + 2 * LANES] += jnp.sum(delta * dstep, 0, keepdims=True)
        few_out[5:6, :inner] += jnp.sum(mixed_here * g, 0, keepdims=True)
        few_out[6:7, :inner] += jnp.sum(dy * xs, 0, keepdims=True)
        dxs = wide_delta * dscaled + skip * dy
        pad[at, :] = jnp.concatenate([dxs, db_state, dc_state], 1) * slope
        grad_ref[at, split:] = draw.astype(BF16)
    for chunk in range(ROWS // CHUNK):
        at = slice(chunk * CHUNK, (chunk + 1) * CHUNK)
        p = p_ref[at, :]
        total = jnp.zeros((CHUNK, conv), F32)
        for tap in range(4):
            begin = chunk * CHUNK + 3 - tap
            shifted = pad[begin : begin + CHUNK, :]
            total = total + few_ref[0, tap : tap + 1, :] * shifted
            few_out[tap : tap + 1, :] += jnp.sum(p * shifted, 0, keepdims=True)
        few_out[4:5, :] += jnp.sum(pad[at, :], 0, keepdims=True)
        grad_ref[at, inner:split] = total.astype(BF16)
    part_ref[...] = mm(grad_ref[...], w_ref[:, : split + LANES], ((1,), (1,))).astype(part_ref.dtype)


def constants(inner, heads):
    width = inner // heads
    lane = np.arange(LANES)[:, None]
    channel = np.arange(inner)[None, :] // width
    selector = ((lane % heads == channel) & (lane < 2 * heads)).astype(np.float32)
    collector = (lane == channel).astype(np.float32).T
    return jnp.asarray(selector, BF16), jnp.asarray(collector, BF16)


def whole(array):
    return pl.BlockSpec(array.shape, lambda i: (0,) * array.ndim)


def forward_call(layer, rows, w, few, inner, pair, heads):
    length, width = rows.shape
    count = length // ROWS
    conv = inner + pair
    states = pair // 2
    selector, _ = constants(inner, heads)
    by_rows = lambda columns: pl.BlockSpec((ROWS, columns), lambda i: (i, 0))
    chunks = ROWS // CHUNK
    out = lambda columns, kind=F32: jax.ShapeDtypeStruct((length, columns), kind)
    return pl.pallas_call(
        partial(forward_kernel, (inner, pair, heads)),
        grid=(count,),
        in_specs=[
            by_rows(width),
            whole(w),
            pl.BlockSpec((1, 8, conv), lambda i: (layer, 0, 0)),
            whole(selector),
        ],
        out_specs=[
            by_rows(width),
            pl.BlockSpec((1, 8, ROWS), lambda i: (i, 0, 0)),
            by_rows(inner),
            by_rows(conv),
            by_rows(conv),
            by_rows(LANES),
            by_rows(inner),
            pl.BlockSpec((chunks, states, inner), lambda i: (i, 0, 0)),
        ],
        out_shape=[
            out(width, BF16),
            jax.ShapeDtypeStruct((count, 8, ROWS), F32),
            out(inner),
            out(conv),
            out(conv),
            out(LANES),
            out(inner),
            jax.ShapeDtypeStruct((count * chunks, states, inner), F32),
        ],
        scratch_shapes=[pltpu.VMEM((states, inner), F32), pltpu.VMEM((ROWS + 8, conv), F32)],
        compiler_params=pltpu.CompilerParams(vmem_limit_bytes=56 * 2**20),
        name="layer_forward",
    )(rows, w, few, selector)


def backward_call(layer, e, scales, w, few, saved, inner, pair, heads):
    length, width = e.shape
    count = length // ROWS
    conv = inner + pair
    states = pair // 2
    split = inner + conv
    z, p, c, raw, y, s = saved
    selector, collector = constants(inner, heads)
    by_rows = lambda columns: pl.BlockSpec((ROWS, columns), lambda i: (count - 1 - i, 0))
    chunks = ROWS // CHUNK
    by_block = lambda lead, rows, columns: pl.BlockSpec(
        (lead, rows, columns), lambda i: (count - 1 - i, 0, 0)
    )
    out = lambda columns, kind=F32: jax.ShapeDtypeStruct((length, columns), kind)
    return pl.pallas_call(
        partial(backward_kernel, (inner, pair, heads)),
        grid=(count,),
        in_specs=[
            by_rows(width),
            by_block(1, 8, ROWS),
            whole(w),
            pl.BlockSpec((1, 8, conv), lambda i: (layer, 0, 0)),
            whole(selector),
            whole(collector),
            by_rows(inner),
            by_rows(conv),
            by_rows(conv),
            by_rows(LANES),
            by_rows(inner),
            by_block(chunks, states, inner),
        ],
        out_specs=[
            by_rows(width),
            by_rows(split + LANES),
            by_rows(inner),
            pl.BlockSpec((8, conv), lambda i: (0, 0)),
        ],
        out_shape=[
            out(width, BF16),
            out(split + LANES, BF16),
            out(inner, BF16),
            jax.ShapeDtypeStruct((8, conv), F32),
        ],
        scratch_shapes=[
            pltpu.VMEM((states, inner), F32),
            pltpu.VMEM((states, inner), F32),
            pltpu.VMEM((ROWS + 8, conv), F32),
        ],
        compiler_params=pltpu.CompilerParams(vmem_limit_bytes=56 * 2**20),
        name="layer_backward",
    )(e, scales, w, few, selector, collector, z, p, c, raw, y, s)


def weight_kernel(rows_ref, grad_ref, errors_ref, mixed_ref, out_ref):
    columns = grad_ref.shape[1]
    turn = ((0,), (0,))
    out_ref[:, :columns] = mm(rows_ref[...], grad_ref[...], turn).astype(out_ref.dtype)
    out_ref[:, columns:] = mm(errors_ref[...], mixed_ref[...], turn).astype(out_ref.dtype)


def weight_call(rows, grad, errors, mixed):
    length, width = rows.shape
    columns = grad.shape[1] + mixed.shape[1]
    by_columns = pl.BlockSpec((length, ROWS), lambda i: (0, i))
    return pl.pallas_call(
        weight_kernel,
        grid=(width // ROWS,),
        in_specs=[by_columns, whole(grad), by_columns, whole(mixed)],
        out_specs=pl.BlockSpec((ROWS, columns), lambda i: (i, 0)),
        out_shape=jax.ShapeDtypeStruct((width, columns), BF16),
        compiler_params=pltpu.CompilerParams(vmem_limit_bytes=56 * 2**20),
        name="weight_gradients",
    )(rows, grad, errors, mixed)


MESH = pl.DeviceIdType.MESH
ANY = pl.BlockSpec(memory_space=pl.ANY)
VMEM = pl.BlockSpec(memory_space=pltpu.VMEM)


def place():
    pipe, dp, x = lax.axis_index("pipe"), lax.axis_index("dp"), lax.axis_index("tensor")
    return (dp // 8) * 2 + pipe, (dp // 2) % 4, dp % 2, x


def at_z(z):
    _, y, core, _ = place()
    return {"pipe": z % 2, "dp": ((z // 2) * 4 + y) * 2 + core}


def at_y(y):
    z, _, core, _ = place()
    return {"dp": ((z // 2) * 4 + y) * 2 + core}


def at_core(core):
    z, y, _, _ = place()
    return {"dp": ((z // 2) * 4 + y) * 2 + core}


def at_x(x):
    return {"tensor": x}


def at_pipe(pipe):
    return {"pipe": pipe}


def greet(*devices):
    barrier = pltpu.get_barrier_semaphore()
    for device in devices:
        pl.semaphore_signal(barrier, inc=1, device_id=device, device_id_type=MESH)
    pl.semaphore_wait(barrier, len(devices))


def around(me, device, steps=(1, 3)):
    return [device((me + step) % 4) for step in steps]


def remote(source, target, sems, index, device):
    return pltpu.make_async_remote_copy(
        src_ref=source,
        dst_ref=target,
        send_sem=sems[0].at[index],
        recv_sem=sems[1].at[index],
        device_id=device,
        device_id_type=MESH,
    )


class RingGather:
    def __init__(self, me, device, own, slot, sems):
        right, left, across = (me + 1) % 4, (me + 3) % 4, (me + 2) % 4
        to_right, to_left = device(right), device(left)
        self.copies = [
            remote(own(0), slot(me, 0), sems, 0, to_right),
            remote(own(1), slot(me, 1), sems, 1, to_left),
            remote(own(1), slot(me, 1), sems, 2, to_right),
            remote(own(0), slot(me, 0), sems, 3, to_left),
            remote(slot(left, 0), slot(left, 0), sems, 4, to_right),
            remote(slot(right, 1), slot(right, 1), sems, 5, to_left),
        ]
        self.origins = [(left, 0), (right, 1), (left, 1), (right, 0), (across, 0), (across, 1)]
        self.local = [
            pltpu.make_async_copy(own(half), slot(me, half), sems[2].at[half]) for half in range(2)
        ]

    def start(self):
        for copy in self.copies[:4]:
            copy.start()
        for copy in self.local:
            copy.start()

    def relay(self):
        for index in range(2):
            self.copies[index].wait_recv()
            self.copies[4 + index].start()

    def wait(self, *indices):
        for index in indices:
            self.copies[index].wait_recv()

    def finish(self):
        for copy in self.local:
            copy.wait()
        for copy in self.copies:
            copy.wait_send()


class RingScatter:
    def __init__(self, me, device, blocks, buffers, sems):
        self.me, self.right, self.left = me, (me + 1) % 4, (me + 3) % 4
        across = (me + 2) % 4
        self.blocks, self.buffers = blocks, buffers
        relays, sums, arrived = buffers
        to_right, to_left = device(self.right), device(self.left)
        self.copies = [
            remote(blocks.at[across, 0], relays.at[0], sems, 0, to_right),
            remote(blocks.at[across, 1], relays.at[1], sems, 1, to_left),
            remote(blocks.at[self.right, 1], arrived.at[0, 1], sems, 2, to_right),
            remote(blocks.at[self.left, 0], arrived.at[1, 0], sems, 3, to_left),
            remote(sums.at[0], arrived.at[0, 0], sems, 4, to_right),
            remote(sums.at[1], arrived.at[1, 1], sems, 5, to_left),
        ]

    def start(self):
        for copy in self.copies[:4]:
            copy.start()

    def relay(self):
        relays, sums, _ = self.buffers
        for half, block in ((0, self.right), (1, self.left)):
            self.copies[half].wait_recv()
            total = relays[half].astype(F32) + self.blocks[block, half].astype(F32)
            sums[half] = total.astype(sums.dtype)
            self.copies[4 + half].start()

    def wait(self):
        for index in range(2, 6):
            self.copies[index].wait_recv()

    def result(self, half):
        arrived = self.buffers[2]
        mine = self.blocks[self.me, half].astype(F32)
        return mine + arrived[0, half].astype(F32) + arrived[1, half].astype(F32)

    def finish(self):
        for copy in self.copies:
            copy.wait_send()


class Everyone:
    def __init__(self, me, device, source, target, sems):
        self.copies = [
            remote(source((me + step) % 4), target(me), sems, step - 1, device((me + step) % 4))
            for step in (1, 2, 3)
        ]

    def start(self):
        for copy in self.copies:
            copy.start()

    def wait(self):
        for copy in self.copies:
            copy.wait()


def dma(count):
    return [pltpu.SemaphoreType.DMA((count,)), pltpu.SemaphoreType.DMA((count,))]


def gather_sems():
    return dma(6) + [pltpu.SemaphoreType.DMA((2,))]


def scatter_buffers(rows, columns):
    return [
        pltpu.VMEM((2, rows // 2, columns), BF16),
        pltpu.VMEM((2, rows // 2, columns), BF16),
        pltpu.VMEM((2, 2, rows // 2, columns), BF16),
    ]


def norm_scale(value):
    return lax.rsqrt(jnp.mean(value * value, -1, keepdims=True) + EPS)


def norm_gain_of(few, layer, lead):
    return jnp.concatenate([few[layer, 6:7, lead:], few[layer, 7:8, :]], 1)


class WeightGather:
    def __init__(self, source, target, sems, core_sems):
        _, y, core, _ = place()
        self.core_sems, self.device = core_sems, at_core(1 - core)
        self.slot = lambda origin, half: target.at[half, origin, core]
        self.ring = RingGather(y, at_y, source, self.slot, sems)
        self.hand = [remote(source(half), self.slot(y, half), core_sems, 6 + half, self.device) for half in range(2)]

    def start(self):
        self.ring.start()
        for copy in self.hand:
            copy.start()

    def pass_on(self, index):
        piece = self.slot(*self.ring.origins[index])
        copy = remote(piece, piece, self.core_sems, index, self.device)
        copy.start()
        self.hand.append(copy)

    def relay(self):
        self.ring.relay()
        for index in range(2):
            self.pass_on(index)

    def finish(self):
        for index in range(2, 6):
            self.ring.wait(index)
            self.pass_on(index)
        self.ring.finish()
        for copy in self.hand:
            copy.wait()


def open_kernel(lead, inputs, shard, few_in, rows, spread_weights, weights, few, raw, normed, few_both,
                xs, xr, xl, zs, zr, zl, ys, yr, yl, cs, cr, fs, fr, load):
    z, y, core, x = place()
    pipe = z % 2
    read = pltpu.make_async_copy(inputs.at[pipe], raw, load.at[0])
    read.start()
    few_both[pipe] = few_in[...]
    greet(*around(x, at_x), *around(y, at_y), *around(z, at_z), at_core(1 - core), at_pipe(1 - pipe))
    swap = remote(few_both.at[pipe], few_both.at[pipe], (fs, fr), 0, at_pipe(1 - pipe))
    swap.start()
    z_slot = lambda origin, half: spread_weights.at[(origin % 2) * 2 + origin // 2, half]
    z_ring = RingGather(z, at_z, lambda half: shard.at[half], z_slot, (zs, zr, zl))
    z_ring.start()
    read.wait()
    swap.wait()
    few[...] = few_both[...]
    gain = norm_gain_of(few_both, 0, lead)
    for half in range(2):
        value = raw[half].astype(F32)
        normed[half] = (value * norm_scale(value) * gain).astype(BF16)
    x_ring = RingGather(x, at_x, lambda half: normed.at[half], lambda origin, half: rows.at[origin, half], (xs, xr, xl))
    x_ring.start()
    z_ring.relay()
    z_ring.wait(2, 3, 4, 5)
    z_ring.finish()
    y_ring = WeightGather(lambda half: spread_weights.at[half], weights, (ys, yr, yl), (cs, cr))
    y_ring.start()
    x_ring.relay()
    y_ring.relay()
    y_ring.finish()
    x_ring.wait(2, 3, 4, 5)
    x_ring.finish()


def remote_params(collective_id):
    return pltpu.CompilerParams(
        collective_id=collective_id, has_side_effects=True, vmem_limit_bytes=56 * 2**20
    )


def open_call(inputs, shard, few):
    _, part, width = inputs.shape
    rows, columns = shard.shape
    lead = few.shape[1] - (width - few.shape[1])
    inputs = inputs.reshape(2, 2, part // 2, width)
    got, spread_weights, weights, few = pl.pallas_call(
        partial(open_kernel, lead),
        out_shape=[
            jax.ShapeDtypeStruct((4, 2, part // 2, width), BF16),
            jax.ShapeDtypeStruct((4, 2, rows // 2, columns), BF16),
            jax.ShapeDtypeStruct((2, 4, 2, 2, rows // 2, columns), BF16),
            jax.ShapeDtypeStruct((2,) + few.shape, F32),
        ],
        in_specs=[ANY, ANY, VMEM],
        out_specs=[ANY, ANY, ANY, VMEM],
        scratch_shapes=[
            pltpu.VMEM((2, part // 2, width), BF16),
            pltpu.VMEM((2, part // 2, width), BF16),
            pltpu.VMEM((2,) + few.shape, F32),
        ]
        + gather_sems() * 3 + dma(8) + dma(1) + [pltpu.SemaphoreType.DMA((1,))],
        compiler_params=remote_params(0),
        name="gather_first",
    )(inputs, shard.reshape(2, rows // 2, columns), few)
    return got.reshape(4 * part, width), spread_weights, weights.reshape(16 * rows, columns), few


def scale_rows(squares, arrived, me, inner):
    total = squares[me, 0:1, :]
    for step in (1, 2, 3):
        total = total + arrived[(me + step) % 4, 0:1, :]
    return lax.rsqrt(total / inner + EPS)


def middle_kernel(inner, lead, part, squares, inputs, few, spread_weights, rows, weights, residual, branch,
                  scales, swapped, raw, normed, low, others, b0, b1, b2, xs, xr, gs, gr, gl,
                  ys, yr, yl, cs, cr, qs, qr, ps, pr, load):
    z, y, core, x = place()
    pipe = z % 2
    read = pltpu.make_async_copy(inputs.at[pipe], raw, load.at[0])
    read.start()
    greet(*around(x, at_x, (1, 2, 3)), *around(y, at_y), at_core(1 - core), at_pipe(1 - pipe))
    sums = RingScatter(x, at_x, part, (b0, b1, b2), (xs, xr))
    sums.start()
    share = Everyone(x, at_x, lambda to: squares.at[to], lambda me: others.at[me], (qs, qr))
    share.start()
    y_ring = WeightGather(lambda half: spread_weights.at[2 + half], weights, (ys, yr, yl), (cs, cr))
    y_ring.start()
    share.wait()
    inverse = scale_rows(squares, others, x, inner)
    scales[...] = jnp.broadcast_to(inverse, scales.shape)
    column = row_to_column(inverse)
    read.wait()
    gain = norm_gain_of(few, 1, lead)
    sums.relay()
    y_ring.relay()
    sums.wait()
    half_rows = part.shape[2]
    for half in range(2):
        here = column[half * half_rows : (half + 1) * half_rows] * sums.result(half)
        branch[half] = here
        value = raw[half].astype(F32) + here
        residual[half] = value
        low[half] = value.astype(BF16)
        normed[half] = (value * norm_scale(value) * gain).astype(BF16)
    x_ring = RingGather(x, at_x, lambda half: normed.at[half], lambda origin, half: rows.at[origin, half], (gs, gr, gl))
    x_ring.start()
    swap = remote(low, swapped, (ps, pr), 0, at_pipe(1 - pipe))
    swap.start()
    y_ring.finish()
    x_ring.relay()
    swap.wait()
    x_ring.wait(2, 3, 4, 5)
    x_ring.finish()
    sums.finish()


def middle_call(part, squares, inputs, few, spread_weights, inner):
    _, rows, width = inputs.shape
    piece, columns = spread_weights.shape[2:]
    lead = few.shape[2] - (width - few.shape[2])
    half = (2, rows // 2, width)
    got, weights, residual, branch, scales, swapped = pl.pallas_call(
        partial(middle_kernel, inner, lead),
        out_shape=[
            jax.ShapeDtypeStruct((4,) + half, BF16),
            jax.ShapeDtypeStruct((2, 4, 2, 2, piece, columns), BF16),
            jax.ShapeDtypeStruct(half, F32),
            jax.ShapeDtypeStruct(half, F32),
            jax.ShapeDtypeStruct((8, rows), F32),
            jax.ShapeDtypeStruct(half, BF16),
        ],
        in_specs=[VMEM, VMEM, ANY, VMEM, ANY],
        out_specs=[ANY, ANY, VMEM, VMEM, VMEM, ANY],
        scratch_shapes=[pltpu.VMEM(half, BF16), pltpu.VMEM(half, BF16), pltpu.VMEM(half, BF16),
                        pltpu.VMEM((4, 8, rows), F32)]
        + scatter_buffers(rows, width)
        + dma(6) + gather_sems() + gather_sems() + dma(8) + dma(3) + dma(1)
        + [pltpu.SemaphoreType.DMA((1,))],
        compiler_params=remote_params(1),
        name="between_layers",
    )(part.reshape((4,) + half), squares, inputs.reshape((2,) + half), few, spread_weights)
    return (got.reshape(4 * rows, width), weights.reshape(-1, columns),
            residual, branch, scales, swapped)


def last_kernel(inner, part, squares, residual, out_grad, output, scales, own, raw, others,
                b0, b1, b2, xs, xr, qs, qr, ds, dr, load):
    z, y, core, x = place()
    pipe = z % 2
    read = pltpu.make_async_copy(out_grad.at[pipe], raw, load.at[0])
    read.start()
    greet(*around(x, at_x, (1, 2, 3)))
    sums = RingScatter(x, at_x, part, (b0, b1, b2), (xs, xr))
    sums.start()
    share = Everyone(x, at_x, lambda to: squares.at[to], lambda me: others.at[me], (qs, qr))
    share.start()
    share.wait()
    inverse = scale_rows(squares, others, x, inner)
    column = row_to_column(inverse)
    read.wait()
    sums.relay()
    sums.wait()
    half_rows = part.shape[2]
    dots = []
    for half in range(2):
        here = column[half * half_rows : (half + 1) * half_rows] * sums.result(half)
        output[half] = residual[half] + here
        dots.append(jnp.sum(raw[half].astype(F32) * here, -1, keepdims=True))
    dots = column_to_row(jnp.concatenate(dots, 0)) / inner
    own[...] = jnp.zeros_like(own)
    own[0:1, :] = inverse
    own[1:2, :] = dots
    tell = Everyone(x, at_x, lambda to: own, lambda me: scales.at[me], (ds, dr))
    tell.start()
    keep = pltpu.make_async_copy(own, scales.at[x], load.at[1])
    keep.start()
    keep.wait()
    tell.wait()
    sums.finish()


def last_call(part, squares, residual, out_grad, inner):
    half = residual.shape
    rows = half[0] * half[1]
    return pl.pallas_call(
        partial(last_kernel, inner),
        out_shape=[jax.ShapeDtypeStruct(half, F32), jax.ShapeDtypeStruct((4, 8, rows), F32)],
        in_specs=[VMEM, VMEM, VMEM, ANY],
        out_specs=[VMEM, ANY],
        scratch_shapes=[pltpu.VMEM((8, rows), F32), pltpu.VMEM(half, BF16), pltpu.VMEM((4, 8, rows), F32)]
        + scatter_buffers(rows, half[2])
        + dma(6) + dma(3) + dma(3) + [pltpu.SemaphoreType.DMA((2,))],
        compiler_params=remote_params(2),
        name="last_output",
    )(part.reshape((4,) + half), squares, residual, out_grad.reshape((2,) + half))


class CoreSum:
    def __init__(self, grads, kept, arrived, total, sems, load):
        _, _, core, _ = place()
        self.kept, self.arrived, self.total = kept, arrived, total
        self.pieces = [(y, half) for y in range(4) for half in range(2)]
        self.copies, self.reads = [], []
        for index, (y, half) in enumerate(self.pieces):
            target = arrived.at[y, half]
            self.copies.append(remote(grads.at[half, y, 1 - core], target, sems, index, at_core(1 - core)))
            self.reads.append(pltpu.make_async_copy(grads.at[half, y, core], kept.at[y, half], load.at[index]))

    def start(self):
        for copy, read in zip(self.copies, self.reads):
            copy.start()
            read.start()

    def finish(self):
        for copy, read, (y, half) in zip(self.copies, self.reads, self.pieces):
            read.wait()
            copy.wait_recv()
            value = self.kept[y, half].astype(F32) + self.arrived[y, half].astype(F32)
            self.total[y, half] = value.astype(BF16)
        for copy in self.copies:
            copy.wait_send()


def core_buffers(rows, columns):
    return [pltpu.VMEM((4, 2, rows, columns), BF16)] * 3


def back_through_norm(value, grad_out, summed, gain):
    scale = norm_scale(value)
    unit = value * scale
    scaled = summed * gain
    mean = jnp.mean(scaled * unit, -1, keepdims=True)
    return grad_out + scale * (scaled - unit * mean), jnp.sum(summed * unit, 0, keepdims=True)


def add_norm_grad(target, source, gain_grad, lead):
    wide = target.shape[1]
    first = wide - lead
    target[...] = source[...]
    target[6:7, lead:] = gain_grad[:, :first]
    target[7:8, :] = gain_grad[:, first:]


def turn_kernel(inner, lead, part, residual, few, out_grad, branch, inverse, output, grads, few_grad,
                errors, scales, input_grad, few_total, swapped_out, swapped_grad, middle,
                raw, own, sent, low_out, low_grad, b0, b1, b2, kept, arrived, total, d0, d1, d2,
                xs, xr, gs, gr, gl, ts, tr, ps, pr, cs, cr, ys, yr, load):
    z, y, core, x = place()
    pipe = z % 2
    read = pltpu.make_async_copy(out_grad.at[pipe], raw, load.at[8])
    read.start()
    low_out[...] = output[...].astype(BF16)
    greet(*around(x, at_x, (1, 2, 3)), *around(y, at_y), at_core(1 - core), at_pipe(1 - pipe))
    sums = RingScatter(x, at_x, part, (b0, b1, b2), (xs, xr))
    sums.start()
    swap_out = remote(low_out, swapped_out, (ps, pr), 0, at_pipe(1 - pipe))
    swap_out.start()
    cores = CoreSum(grads, kept, arrived, total, (cs, cr), load)
    cores.start()
    cores.finish()
    y_sums = RingScatter(y, at_y, total, (d0, d1, d2), (ys, yr))
    y_sums.start()
    read.wait()
    gain = norm_gain_of(few, 1, lead)
    sums.relay()
    y_sums.relay()
    sums.wait()
    gain_grad = jnp.zeros_like(gain)
    dots = []
    for half in range(2):
        value, gain_part = back_through_norm(residual[half], raw[half].astype(F32), sums.result(half), gain)
        gain_grad = gain_grad + gain_part
        input_grad[half] = value
        low = value.astype(BF16)
        sent[half] = low
        dots.append(jnp.sum(low.astype(F32) * branch[half], -1, keepdims=True))
    x_ring = RingGather(x, at_x, lambda half: sent.at[half], lambda origin, half: errors.at[origin, half], (gs, gr, gl))
    x_ring.start()
    swap_grad = remote(sent, swapped_grad, (ps, pr), 1, at_pipe(1 - pipe))
    swap_grad.start()
    own[...] = jnp.zeros_like(own)
    own[0:1, :] = inverse[0:1, :]
    own[1:2, :] = column_to_row(jnp.concatenate(dots, 0)) / inner
    tell = Everyone(x, at_x, lambda to: own, lambda me: scales.at[me], (ts, tr))
    tell.start()
    keep = pltpu.make_async_copy(own, scales.at[x], load.at[9])
    keep.start()
    add_norm_grad(few_total, few_grad, gain_grad, lead)
    y_sums.wait()
    for half in range(2):
        middle[half] = y_sums.result(half).astype(BF16)
    y_sums.finish()
    x_ring.relay()
    swap_out.wait()
    swap_grad.wait()
    keep.wait()
    tell.wait()
    x_ring.wait(2, 3, 4, 5)
    x_ring.finish()
    sums.finish()


def turn_call(part, residual, few, out_grad, branch, inverse, output, grads, few_grad, inner):
    half = residual.shape
    rows, width = half[0] * half[1], half[2]
    lead = few.shape[2] - (width - few.shape[2])
    columns = grads.shape[1]
    piece = grads.shape[0] // 16
    return pl.pallas_call(
        partial(turn_kernel, inner, lead),
        out_shape=[
            jax.ShapeDtypeStruct((4,) + half, BF16),
            jax.ShapeDtypeStruct((4, 8, rows), F32),
            jax.ShapeDtypeStruct(half, F32),
            jax.ShapeDtypeStruct(few_grad.shape, F32),
            jax.ShapeDtypeStruct(half, BF16),
            jax.ShapeDtypeStruct(half, BF16),
            jax.ShapeDtypeStruct((2, piece, columns), BF16),
        ],
        in_specs=[VMEM, VMEM, VMEM, ANY, VMEM, VMEM, VMEM, ANY, VMEM],
        out_specs=[ANY, ANY, VMEM, VMEM, ANY, ANY, VMEM],
        scratch_shapes=[
            pltpu.VMEM(half, BF16),
            pltpu.VMEM((8, rows), F32),
            pltpu.VMEM(half, BF16),
            pltpu.VMEM(half, BF16),
            pltpu.VMEM((8, LANES), BF16),
        ]
        + scatter_buffers(rows, width)
        + core_buffers(piece, columns)
        + scatter_buffers(2 * piece, columns)
        + dma(6) + gather_sems() + dma(3) + dma(2) + dma(8) + dma(6)
        + [pltpu.SemaphoreType.DMA((10,))],
        compiler_params=remote_params(3),
        name="between_gradients",
    )(part.reshape((4,) + half), residual, few, out_grad.reshape((2,) + half), branch, inverse, output,
      grads.reshape(2, 4, 2, piece, columns), few_grad)


def final_kernel(sizes, part, inputs, few, error, grads, middle, few_grad, few_later,
                 input_grad, swapped, large, few_sum, few_shared, state_grad,
                 raw, low, b0, b1, b2, kept, arrived, total, d0, d1, d2, e0, e1, e2, z_blocks,
                 mine, pair, y_few, z_few, x_few, state_parts,
                 xs, xr, ps, pr, cs, cr, ys, yr, zs, zr, fs, fr, hs, hr, js, jr, ks, kr, ws, wr, load):
    lead, state_at, state_columns = sizes
    z, y, core, x = place()
    pipe = z % 2
    every = (1, 2, 3)
    read = pltpu.make_async_copy(inputs.at[pipe], raw, load.at[8])
    read.start()
    greet(*around(x, at_x, every), *around(y, at_y, every), *around(z, at_z, every), at_core(1 - core),
          at_pipe(1 - pipe))
    sums = RingScatter(x, at_x, part, (b0, b1, b2), (xs, xr))
    sums.start()
    cores = CoreSum(grads, kept, arrived, total, (cs, cr), load)
    cores.start()
    cores.finish()
    y_sums = RingScatter(y, at_y, total, (d0, d1, d2), (ys, yr))
    y_sums.start()
    read.wait()
    gain = norm_gain_of(few, 0, lead)
    sums.relay()
    y_sums.relay()
    sums.wait()
    gain_grad = jnp.zeros_like(gain)
    for half in range(2):
        value, gain_part = back_through_norm(raw[half].astype(F32), error[half], sums.result(half), gain)
        gain_grad = gain_grad + gain_part
        input_grad[half] = value
        low[half] = value.astype(BF16)
    swap = remote(low, swapped, (ps, pr), 0, at_pipe(1 - pipe))
    swap.start()
    mine[1] = few_later[...]
    add_norm_grad(mine.at[0], few_grad, gain_grad, lead)
    few_core = remote(mine, pair, (fs, fr), 0, at_core(1 - core))
    few_core.start()
    few_core.wait()
    mine[...] = mine[...] + pair[...]
    few_y = Everyone(y, at_y, lambda to: mine, lambda me: y_few.at[me], (hs, hr))
    few_y.start()
    y_sums.wait()
    rows = z_blocks.shape[2]
    for z_hi in range(2):
        first = y_sums.result(z_hi).astype(BF16)
        second = middle[z_hi]
        for half in range(2):
            z_blocks[2 * z_hi, half] = first[half * rows : (half + 1) * rows]
            z_blocks[2 * z_hi + 1, half] = second[half * rows : (half + 1) * rows]
    y_sums.finish()
    z_sums = RingScatter(z, at_z, z_blocks, (e0, e1, e2), (zs, zr))
    z_sums.start()
    few_y.wait()
    y_few[y] = mine[...]
    mine[...] = (y_few[0] + y_few[1]) + (y_few[2] + y_few[3])
    few_z = Everyone(z, at_z, lambda to: mine.at[to % 2], lambda me: z_few.at[me], (js, jr))
    few_z.start()
    z_sums.relay()
    few_z.wait()
    z_few[z] = mine[pipe]
    few_sum[...] = (z_few[0] + z_few[1]) + (z_few[2] + z_few[3])
    x_few[x] = few_sum[...]
    few_x = Everyone(x, at_x, lambda to: few_sum, lambda me: x_few.at[me], (ks, kr))
    few_x.start()
    z_sums.wait()
    for half in range(2):
        large[half * rows : (half + 1) * rows, :] = z_sums.result(half)
    z_sums.finish()
    quarter = 2 * rows // 4
    columns = pl.ds(state_at, state_columns)
    for block in range(4):
        state_parts[0, block] = large[block * quarter : (block + 1) * quarter, state_at : state_at + state_columns]
    state_x = Everyone(x, at_x, lambda to: state_parts.at[0, to], lambda me: state_parts.at[1, me], (ws, wr))
    state_x.start()
    few_x.wait()
    few_shared[...] = (x_few[0] + x_few[1]) + (x_few[2] + x_few[3])
    state_x.wait()
    total_state = state_parts[0, x]
    for step in every:
        total_state = total_state + state_parts[1, (x + step) % 4]
    state_grad[...] = total_state
    swap.wait()
    sums.finish()


def final_call(part, inputs, few, error, grads, middle, few_grad, few_later, sizes):
    half = error.shape
    rows, width = half[0] * half[1], half[2]
    wide = few.shape[2]
    lead = wide - (width - wide)
    columns = grads.shape[1]
    piece = grads.shape[0] // 16
    state_at, state_columns = sizes
    both = (2,) + few_grad.shape
    return pl.pallas_call(
        partial(final_kernel, (lead, state_at, state_columns)),
        out_shape=[
            jax.ShapeDtypeStruct(half, F32),
            jax.ShapeDtypeStruct(half, BF16),
            jax.ShapeDtypeStruct((piece, columns), F32),
            jax.ShapeDtypeStruct(few_grad.shape, F32),
            jax.ShapeDtypeStruct(few_grad.shape, F32),
            jax.ShapeDtypeStruct((piece // 4, state_columns), F32),
        ],
        in_specs=[VMEM, ANY, VMEM, VMEM, ANY, VMEM, VMEM, VMEM],
        out_specs=[VMEM, ANY, VMEM, VMEM, VMEM, VMEM],
        scratch_shapes=[pltpu.VMEM(half, BF16), pltpu.VMEM(half, BF16)]
        + scatter_buffers(rows, width)
        + core_buffers(piece, columns)
        + scatter_buffers(2 * piece, columns)
        + scatter_buffers(piece, columns)
        + [
            pltpu.VMEM((4, 2, piece // 2, columns), BF16),
            pltpu.VMEM(both, F32),
            pltpu.VMEM(both, F32),
            pltpu.VMEM((4,) + both, F32),
            pltpu.VMEM((4,) + few_grad.shape, F32),
            pltpu.VMEM((4,) + few_grad.shape, F32),
            pltpu.VMEM((2, 4, piece // 4, state_columns), F32),
        ]
        + dma(6) + dma(1) + dma(8) + dma(6) + dma(6) + dma(1) + dma(3) + dma(3) + dma(3) + dma(3)
        + [pltpu.SemaphoreType.DMA((9,))],
        compiler_params=remote_params(4),
        name="final_sums",
    )(part.reshape((4,) + half), inputs.reshape((2,) + half), few, error,
      grads.reshape(2, 4, 2, piece, columns), middle, few_grad, few_later)


def body(inputs, out_grad, norm_gain, in_gate_x, in_read_write, in_step, conv_main, conv_state,
         step_bias, log_rate, skip_gain, gate_gain, out_weight):
    _, part, width = inputs.shape
    inner = out_weight.shape[2]
    pair = in_read_write.shape[2]
    heads = step_bias.shape[1]
    whole_inner = inner * lax.axis_size("tensor")
    split = 2 * inner + pair
    wide = inner + pair
    pipe = lax.axis_index("pipe")
    first = pipe == 0
    shard = jnp.concatenate(
        [
            in_gate_x[0, :, 0],
            in_gate_x[0, :, 1],
            in_read_write[0],
            jnp.pad(in_step[0], ((0, 0), (0, LANES - heads))),
            out_weight[0],
        ],
        1,
    )
    rate = -jnp.exp(log_rate[0])
    pad = ((0, 0), (0, LANES - heads))
    skip = jnp.broadcast_to(skip_gain[0][:, None], (heads, inner // heads)).reshape(1, inner)
    few = jnp.concatenate(
        [
            jnp.concatenate([conv_main[0], conv_state[0]], 1),
            jnp.concatenate([gate_gain, jnp.pad(step_bias, pad), jnp.pad(rate[None], pad)], 1),
            jnp.concatenate([skip, norm_gain], 1).reshape(2, wide),
        ],
        0,
    )
    rows0, spread_weights, w0, few = open_call(inputs, shard, few)
    mine = lax.dynamic_index_in_dim(out_grad, pipe, 0, False)
    mine, w0 = lax.optimization_barrier((mine, w0))
    errors1 = lax.all_gather(mine, "tensor", axis=0, tiled=True)
    part0, squares0, *saved0 = forward_call(0, rows0, w0, few, inner, pair, heads)
    rows1, w1, residual, branch0, inverse0, swapped0 = middle_call(
        part0, squares0, inputs, few, spread_weights, whole_inner
    )
    part1, squares1, *saved1 = forward_call(1, rows1, w1, few, inner, pair, heads)
    output, scales1 = last_call(part1, squares1, residual, out_grad, whole_inner)
    part1, grad1, mixed1, few_grad1 = backward_call(
        1, errors1, scales1, w1, few, saved1, inner, pair, heads
    )
    large1 = weight_call(rows1, grad1, errors1, mixed1)
    errors0, scales0, input_grad1, few_grad1, swapped1, swapped_grad1, middle = turn_call(
        part1, residual, few, out_grad, branch0, inverse0, output, large1, few_grad1, whole_inner
    )
    errors0 = errors0.reshape(4 * part, width)
    part0, grad0, mixed0, few_grad0 = backward_call(
        0, errors0, scales0, w0, few, saved0, inner, pair, heads
    )
    large0 = weight_call(rows0, grad0, errors0, mixed0)
    input_grad0, swapped_grad0, large, few_sum, few_shared, state_grad = final_call(
        part0, inputs, few, input_grad1, large0, middle, few_grad0, few_grad1, (2 * inner, pair)
    )

    def by_layer(zero, one, from_zero, from_one):
        own = jnp.where(first, zero, one).reshape(part, width)
        other = jnp.where(first, from_zero, from_one).reshape(part, width).astype(F32)
        return jnp.where(first, jnp.stack([own, other]), jnp.stack([other, own]))[None]

    activations = by_layer(residual, output, swapped0, swapped1)
    input_grads = by_layer(input_grad0, input_grad1, swapped_grad0, swapped_grad1)
    rates = few_sum[5, inner + LANES : inner + LANES + heads] * rate
    return (
        activations,
        input_grads,
        few_shared[6:].reshape(1, 2 * wide)[:, inner:],
        large[:, : 2 * inner].reshape(1, -1, 2, inner),
        state_grad[None],
        large[None, :, split : split + heads],
        few_sum[None, :5, :inner],
        few_shared[None, :5, inner:],
        few_sum[5:6, inner : inner + heads],
        rates[None],
        few_sum[6, :inner].reshape(1, heads, -1).sum(2),
        few_sum[5:6, :inner],
        large[None, :, split + LANES :],
    )


def solution(mesh):
    in_specs = (
        P("dp", "tensor", None),
        P("dp", "tensor", None),
        P("pipe", None),
        P("pipe", "dp", None, "tensor"),
        P("pipe", "dp", None),
        P("pipe", "dp", "tensor"),
        P("pipe", None, "tensor"),
        P("pipe", None, None),
        P("pipe", "tensor"),
        P("pipe", "tensor"),
        P("pipe", "tensor"),
        P("pipe", "tensor"),
        P("pipe", "dp", "tensor"),
    )
    out_specs = (
        P("pipe", "dp", "tensor", None),
        P("pipe", "dp", "tensor", None),
        P("pipe", None),
        P("pipe", "dp", None, "tensor"),
        P("pipe", ("dp", "tensor"), None),
        P("pipe", "dp", "tensor"),
        P("pipe", None, "tensor"),
        P("pipe", None, None),
        P("pipe", "tensor"),
        P("pipe", "tensor"),
        P("pipe", "tensor"),
        P("pipe", "tensor"),
        P("pipe", "dp", "tensor"),
    )
    return jax.shard_map(body, mesh=mesh, in_specs=in_specs, out_specs=out_specs, check_vma=False)
```

time: 713 us -> 359 us (0.50)
  waiting for transfers between devices: 371 us -> 0.04 us
  Pallas kernels: 85.9 us -> 313 us
  blocking collectives: 167 us -> 0 us
  other arithmetic: 35.4 us -> 10.3 us
  matrix products: 13.6 us -> 0 us
  starting transfers between devices: 12.8 us -> 0.04 us
  local copies, waits for them, and re-layouts: 10.8 us -> 19.2 us
    pallas_call x0 -> x7, Pallas kernels: none -> 227 us  [the longest x1 50.4 us: middle_call(): pl.pallas_call(partial(middle_kernel, inner, lead), out_shape=[jax.ShapeD...]
    all_gather x6 -> x1, waiting for transfers between devices: 197 us -> 0.02 us  [body(): errors1 = lax.all_gather(mine, 'tensor', axis=0, tiled=True)]
    reduce_scatter x9 -> x0, waiting for transfers between devices: 152 us -> none  [the longest x4 93.3 us: body(): lax.psum_scatter(partial_rows, 'tensor', scatter_dimension=0, tiled=True)]
    psum x2 -> x0, blocking collectives: 142 us -> none  [the longest x1 127 us: body(): few = lax.psum(jnp.stack(few), ('pipe', 'dp'))]
    all_gather x2 -> x0, blocking collectives: 25.4 us -> none  [body(): scales = lax.all_gather(scales, 'tensor', axis=0, tiled=True)]
    ppermute x8 -> x0, waiting for transfers between devices: 20.8 us -> none  [swap(): return lax.ppermute(value, 'pipe', [(0, 1), (1, 0)])]
    dot_general x4 -> x0, matrix products: 13.6 us -> none  [the longest x2 7.52 us: body(): grad_in = jnp.einsum('td,tc->dc', rows, grad, preferred_element_type=F32)]
    ppermute x8 -> x0, starting transfers between devices: 11.9 us -> none  [swap(): return lax.ppermute(value, 'pipe', [(0, 1), (1, 0)])]
  transfers between devices with their start and end apart: 23 -> 1, of which waited for: 18 -> 0; matrix products, arithmetic and copies ran while one was open for 7% -> 0% of each run, Pallas kernels for 0% -> 32%
where the time goes in v2:
time: 359 us; the launch traced here: 357 us
  Pallas kernels  313 us (87%)
  local copies, waits for them, and re-layouts  19.2 us (5%)
  between operations  14.3 us (4%)
  other arithmetic  10.3 us (3%)
    pallas_call x1, Pallas kernels, middle_call(): pl.pallas_call(partial(middle_kernel, inner, lead), out_shape=[jax.ShapeD...  50.4 us
    pallas_call x1, Pallas kernels, final_call(): pl.pallas_call(partial(final_kernel, (lead, state_at, state_columns)), ou...  50.3 us
    pallas_call x2, Pallas kernels, backward_call(): pl.pallas_call(partial(backward_kernel, (inner, pair, heads)), grid=(coun...  49.7 us
    pallas_call x1, Pallas kernels, turn_call(): pl.pallas_call(partial(turn_kernel, inner, lead), out_shape=[jax.ShapeDty...  42.3 us
    pallas_call x1, Pallas kernels, open_call(): pl.pallas_call(partial(open_kernel, lead), out_shape=[jax.ShapeDtypeStruc...  38.2 us
    pallas_call x2, Pallas kernels, forward_call(): pl.pallas_call(partial(forward_kernel, (inner, pair, heads)), grid=(count...  36.2 us
    pallas_call x1, Pallas kernels, last_call(): pl.pallas_call(partial(last_kernel, inner), out_shape=[jax.ShapeDtypeStru...  27.8 us
    pallas_call x2, Pallas kernels, weight_call(): pl.pallas_call(weight_kernel, grid=(width // ROWS,), in_specs=[by_columns...  18 us
  transfers between devices with their start and end apart: 1, of which 0 were waited for; matrix products, arithmetic and copies ran while one was open for 0% of the time, Pallas kernels for 32%

profile of v2, /device:TPU:0, one launch (start us, length us, event | category | flops | bytes accessed | tf_op | source)
XLA Modules:
  0.0 356.7 jit_solution(3729835912059870168)
XLA Ops:
  7.2 0.0 copy-start.11
  7.2 0.0 copy-start.12
  7.2 0.0 all-gather.2.cloned.1.call-start
  7.2 0.7 exponential_negate_fusion
  7.9 0.7 broadcast_in_dim.27
  8.6 0.1 reshape.229
  8.7 0.7 maximum_reduce_fusion
  9.4 0.7 copy.51
  10.1 0.8 copy.46
  10.9 0.7 copy.50
  11.6 1.2 fusion.6
  12.9 0.8 constant_dynamic-update-slice_fusion.2
  13.7 0.8 constant_dynamic-update-slice_fusion.shard
  14.5 2.0 dynamic-slice_bitcast_fusion
  16.5 0.0 copy-done.11
  16.5 0.0 copy-done.12
  16.5 0.6 fusion.1.few_in
  17.2 0.0 copy-done.9
  17.2 38.2 %gather_first.1 = (bf16[4,2,128,1024]{3,2,1,0:T(8,128)(2,1)}, bf16[4,2,32,1920]{3,2,1,0:T(8,128)(2,1)}, bf16[2,4,2,2,32,1920]{5,4,3,2,1,0:T(8,128)(2,1)}, f32[2,8,768]{2,1,0:T(8,128)}) custom-call(bf16[2,2,128,1024]{3,2,1,0:T(8,128)(2,1)} %bitcast.54, bf16[2,32,1920]{2,1,0:T(8,128)(2,1)} %copy-done.9, f32[8,768]{1,0:T(8,128)} %fusion.1.few_in), custom_call_target="tpu_custom_call" | custom-call | tf_op jit(solution)/shard_map/gather_first/pallas_call | solution.py:647
  55.4 0.0 all-gather.2.cloned.1.call-update
  55.4 18.1 %layer_forward.2 = (bf16[1024,1024]{1,0:T(8,128)(2,1)}, f32[4,8,256]{2,1,0:T(8,128)}, f32[1024,512]{1,0:T(8,128)}, f32[1024,768]{1,0:T(8,128)}, f32[1024,768]{1,...) custom-call(bf16[1024,1024]{1,0:T(8,128)(2,1)} %bitcast.57, ...), custom_call_target="tpu_custom_call" | custom-call | tf_op jit(solution)/shard_map/layer_forward/pallas_call | solution.py:283
  73.5 50.4 %between_layers.1 = (bf16[4,2,128,1024]{3,2,1,0:T(8,128)(2,1)}, bf16[2,4,2,2,32,1920]{5,4,3,2,1,0:T(8,128)(2,1)}, f32[2,128,1024]{2,1,0:T(8,128)}, f32[2,128,102...) custom-call(bf16[4,2,128,1024]{3,2,1,0:T(8,128)(2,1)} %bitcast.68, ...), custom_call_target="tpu_custom_call" | custom-call | tf_op jit(solution)/shard_map/between_layers/pallas_call | solution.py:724
  123.9 18.1 %layer_forward.3 = (bf16[1024,1024]{1,0:T(8,128)(2,1)}, f32[4,8,256]{2,1,0:T(8,128)}, f32[1024,512]{1,0:T(8,128)}, f32[1024,768]{1,0:T(8,128)}, f32[1024,768]{1,...) custom-call(bf16[1024,1024]{1,0:T(8,128)(2,1)} %bitcast.59, ...), custom_call_target="tpu_custom_call" | custom-call | tf_op jit(solution)/shard_map/layer_forward/pallas_call | solution.py:283
  142.0 27.8 %last_output.1 = (f32[2,128,1024]{2,1,0:T(8,128)}, f32[4,8,256]{2,1,0:T(8,128)}) custom-call(bf16[4,2,128,1024]{3,2,1,0:T(8,128)(2,1)} %bitcast.69, f32[4,8,256]{2,1,0:T(8,128)} %get-tuple-element.75.squares, f32[2,128,1024]{2,1,0:T(8,128)} %get-tuple-element.71.residual, bf16[2,2,128,1024]{3,2,1,0:T(8,128)(2,1)} %bitcast.63), custom_call_target="tpu_custom_call" | custom-call | tf_op jit(solution)/shard_map/last_output/pallas_call | solution.py:787
  169.9 0.0 all-gather.2.cloned.1.call-done.e_ref.errors_ref
  169.9 24.9 %layer_backward.2 = (bf16[1024,1024]{1,0:T(8,128)(2,1)}, bf16[1024,1408]{1,0:T(8,128)(2,1)}, bf16[1024,512]{1,0:T(8,128)(2,1)}, f32[8,768]{1,0:T(8,128)}) custom-call(bf16[1024,1024]{1,0:T(8,128)(2,1)} %all-gather.2.cloned.1.call-done.e_ref.errors_ref, f32[4,8,256]{2,1,0:T(8,128)} %get-tuple-element.79.scales_ref, bf16[1024,1920]{1,0:T(8,128)(2,1)} %bitcast.51, ...), custom_call_target="tpu_custom_call" | custom-call | tf_op jit(solution)/shard_map/layer_backward/pallas_call | solution.py:332
  194.8 9.0 %weight_gradients.2 = bf16[1024,1920]{1,0:T(8,128)(2,1)} custom-call(bf16[1024,1024]{1,0:T(8,128)(2,1)} %bitcast.60, bf16[1024,1408]{1,0:T(8,128)(2,1)} %get-tuple-element.89.grad_ref, bf16[1024,1024]{1,0:T(8,128)(2,1)} %all-gather.2.cloned.1.call-done.e_ref.errors_ref, bf16[1024,512]{1,0:T(8,128)(2,1)} %get-tuple-element.90.mixed_ref), custom_call_target="tpu_custom_call" | custom-call | tf_op jit(solution)/shard_map/weight_gradients/pallas_call | solution.py:382
  203.8 42.3 %between_gradients.1 = (bf16[4,2,128,1024]{3,2,1,0:T(8,128)(2,1)}, f32[4,8,256]{2,1,0:T(8,128)}, f32[2,128,1024]{2,1,0:T(8,128)}, f32[8,768]{1,0:T(8,128)}, bf16...) custom-call(bf16[4,2,128,1024]{3,2,1,0:T(8,128)(2,1)} %bitcast.67, ...), custom_call_target="tpu_custom_call" | custom-call | tf_op jit(solution)/shard_map/between_gradients/pallas_call | solution.py:911
  246.1 24.8 %layer_backward.3 = (bf16[1024,1024]{1,0:T(8,128)(2,1)}, bf16[1024,1408]{1,0:T(8,128)(2,1)}, bf16[1024,512]{1,0:T(8,128)(2,1)}, f32[8,768]{1,0:T(8,128)}) custom-call(bf16[1024,1024]{1,0:T(8,128)(2,1)} %bitcast.61, f32[4,8,256]{2,1,0:T(8,128)} %get-tuple-element.94.scales_ref, bf16[1024,1920]{1,0:T(8,128)(2,1)} %bitcast.49, ...), custom_call_target="tpu_custom_call" | custom-call | tf_op jit(solution)/shard_map/layer_backward/pallas_call | solution.py:332
  270.9 9.0 %weight_gradients.3 = bf16[1024,1920]{1,0:T(8,128)(2,1)} custom-call(bf16[1024,1024]{1,0:T(8,128)(2,1)} %bitcast.58, bf16[1024,1408]{1,0:T(8,128)(2,1)} %get-tuple-element.103.grad_ref, bf16[1024,1024]{1,0:T(8,128)(2,1)} %bitcast.62, bf16[1024,512]{1,0:T(8,128)(2,1)} %get-tuple-element.104.mixed_ref), custom_call_target="tpu_custom_call" | custom-call | tf_op jit(solution)/shard_map/weight_gradients/pallas_call | solution.py:382
  279.9 50.3 %final_sums.1 = (f32[2,128,1024]{2,1,0:T(8,128)}, bf16[2,128,1024]{2,1,0:T(8,128)(2,1)}, f32[64,1920]{1,0:T(8,128)}, f32[8,768]{1,0:T(8,128)}, f32[8,768]{1,0:T(8,128)}, /*index=5*/f32[16,256]{1,0:T(8,128)}) custom-call(bf16[4,2,128,1024]{3,2,1,0:T(8,128)(2,1)} %bitcast.72, bf16[2,2,128,1024]{3,2,1,0:T(8,128)(2,1)} %bitcast.56, ...), custom_call_target="tpu_custom_call" | custom-call | tf_op jit(solution)/shard_map/final_sums/pallas_call | solution.py:1036
  330.1 0.0 copy-start
  330.1 0.0 copy-done.13
  330.2 1.3 slice_multiply_fusion
  331.5 1.4 fusion.7
  332.8 0.7 slice_bitcast_fusion.2
  333.5 0.7 slice_bitcast_fusion.4
  334.3 0.7 slice_bitcast_fusion.3
  335.0 0.8 slice_bitcast_fusion.1
  335.7 1.6 slice_bitcast_fusion
  337.3 1.0 slice.43
  338.3 0.6 copy.40
  338.9 0.1 reshape_squeeze.3
  339.0 0.6 copy.41
  339.6 0.6 slice.52
  340.2 0.7 copy.39
  340.8 0.9 reshape.244
  341.8 0.0 copy-done.1
  341.8 0.0 copy-start.6
  341.8 0.0 copy-start.7
  341.8 0.0 copy-start.8
  341.8 3.1 broadcast_select_fusion.1
  344.9 0.0 copy-done.7
  344.9 0.0 copy-done.8
  344.9 0.1 broadcast_select_fusion
  345.0 0.0 copy-start.4
  345.0 0.1 convert.2
  345.1 0.1 convert.3
  345.3 0.6 reduce_sum.11
  345.9 0.4 copy-done.4
  346.2 1.5 maximum_select_fusion
  347.7 0.0 copy-done.3
  347.8 1.5 maximum_select_fusion.1
  349.3 0.6 copy.57
  (20 shorter events, 0.1 us)
Async XLA Ops:
  7.2 9.4 %copy-start.11 = (f32[1,512]{1,0:T(1,128)S(1)}, f32[1,512]{1,0:T(1,128)}, u32[]{:S(2)}) copy-start(f32[1,512]{1,0:T(1,128)} %param.30) | copy-start | bytes 6148
  7.2 9.3 %copy-start.12 = (f32[1,8]{1,0:T(1,128)S(1)}, f32[1,8]{1,0:T(1,128)}, u32[]{:S(2)}) copy-start(f32[1,8]{1,0:T(1,128)} %param.27) | copy-start | bytes 100
  7.2 162.7 %all-gather.2.cloned.1.call-start = ((), (), s32[]{:S(2)}) async-start(), calls=%async_computation | async-start | bytes 2621440 | tf_op jit(solution)/shard_map/all_gather | solution.py:1105
  14.5 2.6 copy-start.9
  279.9 50.3 %copy-start.13 = (f32[1,8]{1,0:T(1,128)S(1)}, f32[1,8]{1,0:T(1,128)}, u32[]{:S(2)}) copy-start(f32[1,8]{1,0:T(1,128)} %param.28) | copy-start | bytes 100
  279.9 61.9 %copy-start.1 = (f32[2,128,1024]{2,1,0:T(8,128)S(1)}, f32[2,128,1024]{2,1,0:T(8,128)}, u32[]{:S(2)}) copy-start(f32[2,128,1024]{2,1,0:T(8,128)} %get-tuple-element.76.output) | copy-start | bytes 3145732
  279.9 61.9 %copy-start.2 = (f32[2,128,1024]{2,1,0:T(8,128)S(1)}, f32[2,128,1024]{2,1,0:T(8,128)}, u32[]{:S(2)}) copy-start(f32[2,128,1024]{2,1,0:T(8,128)} %get-tuple-element.102.error) | copy-start | bytes 3145732
  330.1 11.6 %copy-start = (f32[2,128,1024]{2,1,0:T(8,128)S(1)}, f32[2,128,1024]{2,1,0:T(8,128)}, u32[]{:S(2)}) copy-start(f32[2,128,1024]{2,1,0:T(8,128)} %get-tuple-element.71.residual) | copy-start | bytes 3145732
  341.8 3.1 copy-start.5
  341.8 3.1 copy-start.6
  341.8 3.1 copy-start.7
  341.8 3.1 copy-start.8
  345.0 1.2 copy-start.4
  346.2 1.5 copy-start.3
  347.8 1.5 copy-start.10
Sparse Core Ops, SparseCore 0:
  55.5 31.6 all-gather.1

commit v3 on v2

v3 whole, which is shorter than its diff:
```python
from functools import partial

import jax
import jax.numpy as jnp
import numpy as np
from jax import lax
from jax.experimental import pallas as pl
from jax.experimental.pallas import tpu as pltpu
from jax.sharding import PartitionSpec as P

F32, BF16 = jnp.float32, jnp.bfloat16
EPS = 1e-05
ROWS = 256
CHUNK = 128
LANES = 128
EXACT = lax.Precision.HIGHEST


def mm(left, right, contract=((1,), (0,))):
    return lax.dot_general(left, right, (contract, ((), ())), preferred_element_type=F32)


def mm_exact(left, right, contract=((1,), (0,))):
    return lax.dot_general(
        left, right, (contract, ((), ())), precision=EXACT, preferred_element_type=F32
    )


def spread(value, selector, heads):
    high = value.astype(BF16).astype(F32)
    both = high + pltpu.roll(value - high, heads, 1)
    return mm(both.astype(BF16), selector)


def per_head(value, collector):
    high = value.astype(BF16)
    low = (value - high.astype(F32)).astype(BF16)
    return mm(high, collector) + mm(low, collector)


def softplus(value):
    small = jnp.exp(-jnp.abs(value))
    series = small * (1.0 - small * (0.5 - small * (1.0 / 3.0 - small * 0.25)))
    return jnp.maximum(value, 0.0) + jnp.where(small < 0.01, series, jnp.log(1.0 + small))


def sigmoid(value):
    return 1.0 / (1.0 + jnp.exp(-value))


def iota(shape, axis):
    return lax.broadcasted_iota(jnp.int32, shape, axis)


def column_to_row(column):
    size = column.shape[0]
    same = iota((size, size), 0) == iota((size, size), 1)
    return jnp.sum(jnp.where(same, column, 0.0), 0, keepdims=True)


def row_to_column(row):
    size = row.shape[1]
    same = iota((size, size), 0) == iota((size, size), 1)
    return jnp.sum(jnp.where(same, row, 0.0), 1, keepdims=True)


def steps(raw, bias, rate, mask):
    delta = softplus(raw + bias) * mask
    tri = (iota((CHUNK, CHUNK), 0) >= iota((CHUNK, CHUNK), 1)).astype(F32)
    log_decay = mm_exact(tri, delta * rate)
    return delta, log_decay


def backward_kernel(sizes, e_ref, scales_ref, w_ref, few_ref, selector_ref,
                    collector_ref, saved_ref, s_ref,
                    part_ref, grad_ref, mixed_ref, few_out, state, later, pad):
    inner, pair, heads = sizes
    states = pair // 2
    split = inner + inner + pair
    conv = inner + pair
    (z_at, p_at, c_at, raw_at, y_at), _ = columns_of(inner, conv)

    @pl.when(pl.program_id(0) == 0)
    def _():
        state[...] = jnp.zeros_like(state)
        later[...] = jnp.zeros_like(later)
        pad[ROWS : ROWS + 8, :] = jnp.zeros((8, conv), F32)
        few_out[...] = jnp.zeros_like(few_out)

    @pl.when(pl.program_id(0) > 0)
    def _():
        pad[ROWS : ROWS + 8, :] = pad[0:8, :]

    selector = selector_ref[...]
    collector = collector_ref[...]
    bias = few_ref[0, 5:6, inner : inner + LANES]
    rate = few_ref[0, 5:6, inner + LANES : inner + 2 * LANES]
    gain = few_ref[0, 5:6, :inner]
    skip = few_ref[0, 6:7, :inner]
    mask = (iota((1, LANES), 1) < heads).astype(F32)
    first = iota((CHUNK, LANES), 1) < LANES // 2
    later_in = iota((CHUNK, CHUNK), 1) >= iota((CHUNK, CHUNK), 0)
    last = iota((CHUNK, LANES), 0) == CHUNK - 1
    quarter = ROWS // 4
    column = lambda row: jnp.concatenate(
        [row_to_column(scales_ref[0, owner, row : row + 1, :])[:quarter] for owner in range(4)], 0
    )
    inverse = column(0)
    inner_dot = column(1)
    mixed_grad = mm(e_ref[...], w_ref[0, :, split + LANES :])
    for chunk in reversed(range(ROWS // CHUNK)):
        at = slice(chunk * CHUNK, (chunk + 1) * CHUNK)
        z = saved_ref[0, at, z_at]
        y = saved_ref[0, at, y_at]
        sig = sigmoid(z)
        act = z * sig
        g = y * act * inverse[at]
        mixed_ref[at, :] = (g * gain).astype(BF16)
        mixed_here = mixed_grad[at]
        gated_grad = inverse[at] * (mixed_here * gain - g * inner_dot[at])
        dy = gated_grad * act
        grad_ref[at, :inner] = (gated_grad * y * (sig * (1.0 + z - act))).astype(BF16)
        c = saved_ref[0, at, c_at]
        csig = sigmoid(c)
        value = c * csig
        slope = csig * (1.0 + c - value)
        xs = value[:, :inner]
        b_low = value[:, inner : inner + states].astype(BF16)
        c_low = value[:, inner + states :].astype(BF16)
        raw = saved_ref[0, at, raw_at]
        delta, log_decay = steps(raw, bias, rate, mask)
        turned = log_decay.T
        final = log_decay[CHUNK - 1 : CHUNK, :]
        wide_delta = spread(delta, selector, heads)
        scaled = wide_delta * xs
        scaled_low = scaled.astype(BF16)
        dy_low = dy.astype(BF16)
        products = jnp.where(later_in, mm(b_low, c_low, ((1,), (1,))), 0.0)
        dproducts = jnp.zeros((CHUNK, CHUNK), F32)
        within = []
        for two in range(heads // 2):
            lanes = slice(two * LANES, (two + 1) * LANES)
            parts = []
            for odd in range(2):
                h = 2 * two + odd
                mine = first if odd == 0 else ~first
                decay = jnp.exp(jnp.minimum(turned[h : h + 1, :] - log_decay[:, h : h + 1], 0.0))
                parts.append(mm((products * decay).astype(BF16), dy_low[:, lanes]))
                own = jnp.where(mine, scaled_low[:, lanes], jnp.zeros((), BF16))
                dproducts = dproducts + decay * mm(own, dy_low[:, lanes], ((1,), (1,)))
            within.append(jnp.where(first, parts[0], parts[1]))
        dproducts = jnp.where(later_in, dproducts, 0.0).astype(BF16)
        old = s_ref[0, chunk]
        old_low = old.astype(BF16)
        dstate = state[...]
        dstate_low = dstate.astype(BF16)
        to_end = spread(jnp.exp(final - log_decay) * mask, selector, heads)
        from_start = (spread(jnp.exp(log_decay) * mask, selector, heads) * dy).astype(BF16)
        dscaled = jnp.concatenate(within, 1) + to_end * mm(b_low, dstate_low)
        dc_state = mm(from_start, old_low, ((1,), (1,))) + mm(dproducts, b_low, ((0,), (0,)))
        db_state = mm((to_end * scaled).astype(BF16), dstate_low, ((1,), (1,))) + mm(dproducts, c_low)
        carry = jnp.broadcast_to(jnp.sum(later[...] * dstate, 0, keepdims=True), (8, inner))
        carry = per_head(carry, collector)[0:1]
        keep = spread(jnp.broadcast_to(jnp.exp(final) * mask, (8, LANES)), selector, heads)[0:1]
        state[...] = keep * dstate + mm(c_low, from_start, ((0,), (0,)))
        later[...] = old
        flow = dy_low.astype(F32) * (y - skip * xs) - scaled_low.astype(F32) * dscaled
        dlog = per_head(flow, collector) + jnp.where(last, carry, 0.0)
        tri = (iota((CHUNK, CHUNK), 1) >= iota((CHUNK, CHUNK), 0)).astype(F32)
        dstep = mm_exact(tri, dlog)
        ddelta = per_head(xs * dscaled, collector) + rate * dstep
        draw = ddelta * sigmoid(raw + bias) * mask
        few_out[5:6, inner : inner + LANES] += jnp.sum(draw, 0, keepdims=True)
        few_out[5:6, inner + LANES : inner + 2 * LANES] += jnp.sum(delta * dstep, 0, keepdims=True)
        few_out[5:6, :inner] += jnp.sum(mixed_here * g, 0, keepdims=True)
        few_out[6:7, :inner] += jnp.sum(dy * xs, 0, keepdims=True)
        dxs = wide_delta * dscaled + skip * dy
        pad[at, :] = jnp.concatenate([dxs, db_state, dc_state], 1) * slope
        grad_ref[at, split:] = draw.astype(BF16)
    for chunk in range(ROWS // CHUNK):
        at = slice(chunk * CHUNK, (chunk + 1) * CHUNK)
        p = saved_ref[0, at, p_at]
        total = jnp.zeros((CHUNK, conv), F32)
        for tap in range(4):
            begin = chunk * CHUNK + 3 - tap
            shifted = pad[begin : begin + CHUNK, :]
            total = total + few_ref[0, tap : tap + 1, :] * shifted
            few_out[tap : tap + 1, :] += jnp.sum(p * shifted, 0, keepdims=True)
        few_out[4:5, :] += jnp.sum(pad[at, :], 0, keepdims=True)
        grad_ref[at, inner:split] = total.astype(BF16)
    part_ref[...] = mm(grad_ref[...], w_ref[0, :, : split + LANES], ((1,), (1,))).astype(part_ref.dtype)


def constants(inner, heads):
    width = inner // heads
    lane = np.arange(LANES)[:, None]
    channel = np.arange(inner)[None, :] // width
    selector = ((lane % heads == channel) & (lane < 2 * heads)).astype(np.float32)
    collector = (lane == channel).astype(np.float32).T
    return jnp.asarray(selector, BF16), jnp.asarray(collector, BF16)


def whole(array):
    return pl.BlockSpec(array.shape, lambda i: (0,) * array.ndim)


def backward_call(layer, e, scales, w, few, saved, states, inner, pair, heads):
    length, width = e.shape
    count = length // ROWS
    conv = inner + pair
    split = inner + conv
    selector, collector = constants(inner, heads)
    by_rows = lambda columns: pl.BlockSpec((ROWS, columns), lambda i: (count - 1 - i, 0))
    of_layer = lambda array: pl.BlockSpec((1,) + array.shape[1:], lambda i: (layer, 0, 0))
    chunks = ROWS // CHUNK
    out = lambda columns, kind=F32: jax.ShapeDtypeStruct((length, columns), kind)
    return pl.pallas_call(
        partial(backward_kernel, (inner, pair, heads)),
        grid=(count,),
        in_specs=[
            by_rows(width),
            pl.BlockSpec((1,) + scales.shape[1:], lambda i: (count - 1 - i, 0, 0, 0)),
            of_layer(w),
            of_layer(few),
            whole(selector),
            whole(collector),
            pl.BlockSpec((1, ROWS, saved.shape[2]), lambda i: (layer, count - 1 - i, 0)),
            pl.BlockSpec((1, chunks) + states.shape[2:], lambda i: (layer, count - 1 - i, 0, 0)),
        ],
        out_specs=[
            by_rows(width),
            by_rows(split + LANES),
            by_rows(inner),
            pl.BlockSpec((8, conv), lambda i: (0, 0)),
        ],
        out_shape=[
            out(width, BF16),
            out(split + LANES, BF16),
            out(inner, BF16),
            jax.ShapeDtypeStruct((8, conv), F32),
        ],
        scratch_shapes=[
            pltpu.VMEM((pair // 2, inner), F32),
            pltpu.VMEM((pair // 2, inner), F32),
            pltpu.VMEM((ROWS + 8, conv), F32),
        ],
        compiler_params=pltpu.CompilerParams(vmem_limit_bytes=56 * 2**20),
        name="layer_backward",
    )(e, scales, w, few, selector, collector, saved, states)


def weight_kernel(rows_ref, grad_ref, errors_ref, mixed_ref, out_ref):
    columns = grad_ref.shape[1]
    turn = ((0,), (0,))
    out_ref[:, :columns] = mm(rows_ref[0], grad_ref[...], turn).astype(out_ref.dtype)
    out_ref[:, columns:] = mm(errors_ref[...], mixed_ref[...], turn).astype(out_ref.dtype)


def weight_call(layer, normed, grad, errors, mixed):
    length, width = errors.shape
    columns = grad.shape[1] + mixed.shape[1]
    return pl.pallas_call(
        weight_kernel,
        grid=(width // ROWS,),
        in_specs=[
            pl.BlockSpec((1, length, ROWS), lambda i: (layer, 0, i)),
            whole(grad),
            pl.BlockSpec((length, ROWS), lambda i: (0, i)),
            whole(mixed),
        ],
        out_specs=pl.BlockSpec((ROWS, columns), lambda i: (i, 0)),
        out_shape=jax.ShapeDtypeStruct((width, columns), BF16),
        compiler_params=pltpu.CompilerParams(vmem_limit_bytes=56 * 2**20),
        name="weight_gradients",
    )(normed, grad, errors, mixed)


MESH = pl.DeviceIdType.MESH
ANY = pl.BlockSpec(memory_space=pl.ANY)
VMEM = pl.BlockSpec(memory_space=pltpu.VMEM)


def place():
    pipe, dp, x = lax.axis_index("pipe"), lax.axis_index("dp"), lax.axis_index("tensor")
    return (dp // 8) * 2 + pipe, (dp // 2) % 4, dp % 2, x


def at_z(z):
    _, y, core, _ = place()
    return {"pipe": z % 2, "dp": ((z // 2) * 4 + y) * 2 + core}


def at_y(y):
    z, _, core, _ = place()
    return {"dp": ((z // 2) * 4 + y) * 2 + core}


def at_core(core):
    z, y, _, _ = place()
    return {"dp": ((z // 2) * 4 + y) * 2 + core}


def at_x(x):
    return {"tensor": x}


def at_pipe(pipe):
    return {"pipe": pipe}


def greet(*devices):
    barrier = pltpu.get_barrier_semaphore()
    for device in devices:
        pl.semaphore_signal(barrier, inc=1, device_id=device, device_id_type=MESH)
    pl.semaphore_wait(barrier, len(devices))


def around(me, device, steps=(1, 3)):
    return [device((me + step) % 4) for step in steps]


def remote(source, target, sems, index, device):
    return pltpu.make_async_remote_copy(
        src_ref=source,
        dst_ref=target,
        send_sem=sems[0].at[index],
        recv_sem=sems[1].at[index],
        device_id=device,
        device_id_type=MESH,
    )


class RingGather:
    def __init__(self, me, device, own, slot, sems, local=True):
        right, left, across = (me + 1) % 4, (me + 3) % 4, (me + 2) % 4
        to_right, to_left = device(right), device(left)
        self.copies = [
            remote(own(0), slot(me, 0), sems, 0, to_right),
            remote(own(1), slot(me, 1), sems, 1, to_left),
            remote(own(1), slot(me, 1), sems, 2, to_right),
            remote(own(0), slot(me, 0), sems, 3, to_left),
            remote(slot(left, 0), slot(left, 0), sems, 4, to_right),
            remote(slot(right, 1), slot(right, 1), sems, 5, to_left),
        ]
        self.origins = [(left, 0), (right, 1), (left, 1), (right, 0), (across, 0), (across, 1)]
        self.local = [
            pltpu.make_async_copy(own(half), slot(me, half), sems[2].at[half]) for half in range(2 * local)
        ]

    def start(self):
        for copy in self.copies[:4]:
            copy.start()
        for copy in self.local:
            copy.start()

    def relay(self):
        for index in range(2):
            self.copies[index].wait_recv()
            self.copies[4 + index].start()

    def wait(self, *indices):
        for index in indices:
            self.copies[index].wait_recv()

    def finish(self):
        for copy in self.local:
            copy.wait()
        for copy in self.copies:
            copy.wait_send()


class RingScatter:
    def __init__(self, me, device, piece, buffers, sems):
        self.me, self.right, self.left = me, (me + 1) % 4, (me + 3) % 4
        across = (me + 2) % 4
        self.piece, self.buffers = piece, buffers
        relays, sums, arrived = buffers
        to_right, to_left = device(self.right), device(self.left)
        self.copies = [
            remote(piece(across, 0), relays.at[0], sems, 0, to_right),
            remote(piece(across, 1), relays.at[1], sems, 1, to_left),
            remote(piece(self.right, 1), arrived.at[0, 1], sems, 2, to_right),
            remote(piece(self.left, 0), arrived.at[1, 0], sems, 3, to_left),
            remote(sums.at[0], arrived.at[0, 0], sems, 4, to_right),
            remote(sums.at[1], arrived.at[1, 1], sems, 5, to_left),
        ]

    def start(self):
        for copy in self.copies[:4]:
            copy.start()

    def relay(self):
        relays, sums, _ = self.buffers
        for half, block in ((0, self.right), (1, self.left)):
            self.copies[half].wait_recv()
            total = relays[half].astype(F32) + self.piece(block, half)[...].astype(F32)
            sums[half] = total.astype(sums.dtype)
            self.copies[4 + half].start()

    def wait(self):
        for index in range(2, 6):
            self.copies[index].wait_recv()

    def result(self, half):
        arrived = self.buffers[2]
        mine = self.piece(self.me, half)[...].astype(F32)
        return mine + arrived[0, half].astype(F32) + arrived[1, half].astype(F32)

    def finish(self):
        for copy in self.copies:
            copy.wait_send()


class Everyone:
    def __init__(self, me, device, source, target, sems):
        self.copies = [
            remote(source((me + step) % 4), target(me), sems, step - 1, device((me + step) % 4))
            for step in (1, 2, 3)
        ]

    def start(self):
        for copy in self.copies:
            copy.start()

    def wait(self):
        for copy in self.copies:
            copy.wait()


def dma(count):
    return [pltpu.SemaphoreType.DMA((count,)), pltpu.SemaphoreType.DMA((count,))]


def gather_sems():
    return dma(6) + [pltpu.SemaphoreType.DMA((2,))]


def scatter_buffers(*half):
    return [pltpu.VMEM((2,) + half, BF16), pltpu.VMEM((2,) + half, BF16), pltpu.VMEM((2, 2) + half, BF16)]


def norm_scale(value):
    return lax.rsqrt(jnp.mean(value * value, -1, keepdims=True) + EPS)


def norm_gain_of(few, layer, lead):
    return jnp.concatenate([few[layer, 6:7, lead:], few[layer, 7:8, :]], 1)


def remote_params(collective_id):
    return pltpu.CompilerParams(
        collective_id=collective_id, has_side_effects=True, vmem_limit_bytes=56 * 2**20
    )


class CoreSum:
    def __init__(self, grads, kept, arrived, total, sems, load):
        _, _, core, _ = place()
        self.kept, self.arrived, self.total = kept, arrived, total
        self.pieces = [(y, half) for y in range(4) for half in range(2)]
        self.copies, self.reads = [], []
        for index, (y, half) in enumerate(self.pieces):
            target = arrived.at[y, half]
            self.copies.append(remote(grads.at[half, y, 1 - core], target, sems, index, at_core(1 - core)))
            self.reads.append(pltpu.make_async_copy(grads.at[half, y, core], kept.at[y, half], load.at[index]))

    def start(self):
        for copy, read in zip(self.copies, self.reads):
            copy.start()
            read.start()

    def finish(self):
        for copy, read, (y, half) in zip(self.copies, self.reads, self.pieces):
            read.wait()
            copy.wait_recv()
            value = self.kept[y, half].astype(F32) + self.arrived[y, half].astype(F32)
            self.total[y, half] = value.astype(BF16)
        for copy in self.copies:
            copy.wait_send()


def core_buffers(rows, columns):
    return [pltpu.VMEM((4, 2, rows, columns), BF16)] * 3


def back_through_norm(value, grad_out, summed, gain):
    scale = norm_scale(value)
    unit = value * scale
    scaled = summed * gain
    mean = jnp.mean(scaled * unit, -1, keepdims=True)
    return grad_out + scale * (scaled - unit * mean), jnp.sum(summed * unit, 0, keepdims=True)


def add_norm_grad(target, source, gain_grad, lead):
    wide = target.shape[1]
    first = wide - lead
    target[...] = source[...]
    target[6:7, lead:] = gain_grad[:, :first]
    target[7:8, :] = gain_grad[:, first:]


def owned(block, x, rows):
    return pl.ds(pl.multiple_of(block * ROWS + x * rows, rows), rows)


class BlockSums:
    def __init__(self, x, piece, relays, sums, arrived, sems, op):
        self.right, self.left, self.me = (x + 1) % 4, (x + 3) % 4, x
        across = (x + 2) % 4
        self.piece, self.relays, self.sums, self.arrived = piece, relays, sums, arrived
        at_op = [sem.at[op] for sem in sems]
        to_right, to_left = at_x(self.right), at_x(self.left)
        self.copies = [
            remote(piece(across, 0), relays.at[op, 0], at_op, 0, to_right),
            remote(piece(across, 1), relays.at[op, 1], at_op, 1, to_left),
            remote(piece(self.right, 1), arrived.at[op, 0, 1], at_op, 2, to_right),
            remote(piece(self.left, 0), arrived.at[op, 1, 0], at_op, 3, to_left),
            remote(sums.at[op, 0], arrived.at[op, 0, 0], at_op, 4, to_right),
            remote(sums.at[op, 1], arrived.at[op, 1, 1], at_op, 5, to_left),
        ]
        self.op = op

    def start(self):
        for copy in self.copies[:4]:
            copy.start()

    def relay(self):
        for half, block in ((0, self.right), (1, self.left)):
            self.copies[half].wait_recv()
            total = self.relays[self.op, half].astype(F32) + self.piece(block, half)[...].astype(F32)
            self.sums[self.op, half] = total.astype(BF16)
            self.copies[4 + half].start()

    def wait(self):
        for index in range(2, 6):
            self.copies[index].wait_recv()

    def result(self):
        return jnp.concatenate(
            [
                self.piece(self.me, half)[...].astype(F32)
                + self.arrived[self.op, 0, half].astype(F32)
                + self.arrived[self.op, 1, half].astype(F32)
                for half in range(2)
            ],
            0,
        )

    def finish(self):
        for copy in self.copies:
            copy.wait_send()


def to_everyone(me, device, source, target, sems, op):
    at_op = [sem.at[op] for sem in sems]
    return Everyone(me, device, source, target, at_op)


def columns_of(inner, conv):
    ends = np.cumsum([0, inner, conv, conv, LANES, inner])
    return [slice(int(begin), int(end)) for begin, end in zip(ends[:-1], ends[1:])], int(ends[-1])


def forward_block(sizes, first_block, rows, w, few, selector, save, states, part, squares, state, pad):
    inner, pair, heads = sizes
    states_count = pair // 2
    split = inner + inner + pair
    conv = inner + pair
    (z_at, p_at, c_at, raw_at, y_at), _ = columns_of(inner, conv)

    @pl.when(first_block)
    def _():
        state[...] = jnp.zeros_like(state)
        pad[0:8, :] = jnp.zeros((8, conv), F32)

    @pl.when(jnp.logical_not(first_block))
    def _():
        pad[0:8, :] = pad[ROWS : ROWS + 8, :]

    projected = mm(rows, w[:, : split + LANES])
    save[:, z_at] = projected[:, :inner]
    save[:, p_at] = projected[:, inner:split]
    pad[8 : ROWS + 8, :] = projected[:, inner:split]
    save[:, raw_at] = projected[:, split:]
    bias = few[5:6, inner : inner + LANES]
    rate = few[5:6, inner + LANES : inner + 2 * LANES]
    gain = few[5:6, :inner]
    skip = few[6:7, :inner]
    mask = (iota((1, LANES), 1) < heads).astype(F32)
    first = iota((CHUNK, LANES), 1) < LANES // 2
    causal = iota((CHUNK, CHUNK), 0) >= iota((CHUNK, CHUNK), 1)
    owner_rows = ROWS // 4
    for chunk in range(ROWS // CHUNK):
        at = slice(chunk * CHUNK, (chunk + 1) * CHUNK)
        c = jnp.broadcast_to(few[4:5, :], (CHUNK, conv))
        for tap in range(4):
            begin = chunk * CHUNK + 5 + tap
            c = c + few[tap : tap + 1, :] * pad[begin : begin + CHUNK, :]
        save[at, c_at] = c
        value = c * sigmoid(c)
        xs = value[:, :inner]
        b_low = value[:, inner : inner + states_count].astype(BF16)
        c_low = value[:, inner + states_count :].astype(BF16)
        delta, log_decay = steps(save[at, raw_at], bias, rate, mask)
        turned = log_decay.T
        final = log_decay[CHUNK - 1 : CHUNK, :]
        scaled = spread(delta, selector, heads) * xs
        scaled_low = scaled.astype(BF16)
        products = jnp.where(causal, mm(c_low, b_low, ((1,), (1,))), 0.0)
        within = []
        for two in range(heads // 2):
            lanes = slice(two * LANES, (two + 1) * LANES)
            parts = []
            for h in (2 * two, 2 * two + 1):
                gap = jnp.minimum(log_decay[:, h : h + 1] - turned[h : h + 1, :], 0.0)
                parts.append(mm((products * jnp.exp(gap)).astype(BF16), scaled_low[:, lanes]))
            within.append(jnp.where(first, parts[0], parts[1]))
        old = state[...]
        states[chunk] = old
        carried = mm(c_low, old.astype(BF16)) * spread(jnp.exp(log_decay) * mask, selector, heads)
        y = jnp.concatenate(within, 1) + carried + skip * xs
        save[at, y_at] = y
        ends = (spread(jnp.exp(final - log_decay) * mask, selector, heads) * scaled).astype(BF16)
        keep = spread(jnp.broadcast_to(jnp.exp(final) * mask, (8, LANES)), selector, heads)[0:1]
        state[...] = keep * old + mm(b_low, ends, ((0,), (0,)))
        z = save[at, z_at]
        gated = y * (z * sigmoid(z))
        total = jnp.sum(gated * gated, 1, keepdims=True)
        for piece in range(CHUNK // owner_rows):
            row = column_to_row(total[piece * owner_rows : (piece + 1) * owner_rows])
            squares[chunk * (CHUNK // owner_rows) + piece, 0:1, 0:owner_rows] = row
        mixed = (gated * gain).astype(BF16)
        part[at, :] = mm(mixed, w[:, split + LANES :], ((1,), (1,))).astype(BF16)


def forward_all_kernel(sizes, inputs, out_grad, shard, few_in, selector,
                       few_both, weights, errors, normed, saved, states, res, inverses, scales, firsts,
                       hidden, w_held, part, relays, sums, arrived, squares, others, stage, state_stage, norm_stage,
                       error_rows, own_scales, state, pad, spread_weights, few,
                       xs, xr, xl, es, er, el, zs, zr, zl, ys, yr, yl, cs, cr, y1s, y1r, y1l, c1s, c1r,
                       fs, fr, rs, rr, gs, gr, gl, qs, qr, ss, sr, ps, pr, outs, load):
    inner, pair, heads, lead, whole_inner = sizes
    layer_sizes = (inner, pair, heads)
    z, y, core, x = place()
    pipe = z % 2
    quarter = ROWS // 4
    few[pipe] = few_in[...]
    squares[...] = jnp.zeros_like(squares)
    greet(*around(x, at_x, (1, 2, 3)), *around(y, at_y), *around(z, at_z), at_core(1 - core), at_pipe(1 - pipe))
    few_swap = remote(few.at[pipe], few.at[pipe], (fs, fr), 0, at_pipe(1 - pipe))
    few_swap.start()
    piece = spread_weights.shape[1]
    shard_rows = lambda half: pl.ds(half * (piece // 2), piece // 2)
    z_slot = lambda origin, half: spread_weights.at[(origin % 2) * 2 + origin // 2, shard_rows(half)]
    z_ring = RingGather(z, at_z, lambda half: shard.at[shard_rows(half)], z_slot, (zs, zr, zl))
    z_ring.start()
    block_rows = lambda origin, half: pl.ds(pl.multiple_of(origin * ROWS + half * (ROWS // 2), ROWS // 2), ROWS // 2)
    x_ring = RingGather(x, at_x, lambda half: inputs.at[pipe, half],
                        lambda origin, half: hidden.at[0, block_rows(origin, half)], (xs, xr, xl))
    x_ring.start()
    e_ring = RingGather(x, at_x, lambda half: out_grad.at[pipe, half],
                        lambda origin, half: errors.at[block_rows(origin, half)], (es, er, el))
    weight_rings = []
    for layer, sems, core_sems in ((0, (ys, yr, yl), (cs, cr)), (1, (y1s, y1r, y1l), (c1s, c1r))):
        weight_rings.append(
            WeightRows(
                lambda half, layer=layer: spread_weights.at[2 * layer + half],
                lambda origin, half, core, layer=layer: weights.at[layer, (half * 4 + origin) * 2 + core],
                sems,
                core_sems,
            )
        )
    z_ring.relay()
    z_ring.wait(2, 3, 4, 5)
    z_ring.finish()
    weight_rings[0].start()
    x_ring.relay()
    e_ring.start()
    weight_rings[0].relay()
    few_swap.wait()
    few_both[...] = few[...]
    x_ring.wait(2, 3, 4, 5)
    x_ring.finish()
    for block in range(4):
        res[0, block] = hidden[0, owned(block, x, quarter)].astype(F32)
    weight_rings[0].finish()
    weight_rings[1].start()
    w_loads = [
        [
            pltpu.make_async_copy(
                weights.at[layer, index],
                w_held.at[layer, pl.ds(index * piece, piece)],
                load.at[layer * 16 + index],
            )
            for index in range(16)
        ]
        for layer in range(2)
    ]
    for copy in w_loads[0]:
        copy.start()
    for copy in w_loads[0]:
        copy.wait()

    def sums_of(op):
        rows = lambda owner, half: part.at[op, pl.ds(pl.multiple_of(owner * quarter + half * (quarter // 2), quarter // 2), quarter // 2)]
        return BlockSums(x, rows, relays, sums, arrived, (rs, rr), op)

    def squares_of(op):
        return to_everyone(x, at_x, lambda to: squares.at[op, to], lambda me: others.at[op, me], (qs, qr), op)

    def gather_of(block):
        place_of = lambda origin, half: hidden.at[
            1, pl.ds(pl.multiple_of(block * ROWS + origin * quarter + half * (quarter // 2), quarter // 2), quarter // 2)
        ]
        return RingGather(x, at_x, lambda half: place_of(x, half), place_of, (gs.at[block], gr.at[block], gl), local=False)

    def scales_of(block):
        return to_everyone(x, at_x, lambda to: own_scales.at[block], lambda me: scales.at[block, me], (ss, sr), block)

    def outs_of(op):
        layer, block = op // 4, op % 4
        slot = op % 2
        at = pl.ds(pl.multiple_of(block * ROWS, ROWS), ROWS)
        count = ROWS // CHUNK
        return [
            pltpu.make_async_copy(stage.at[slot], saved.at[layer, at], outs.at[0, slot]),
            pltpu.make_async_copy(state_stage.at[slot], states.at[layer, pl.ds(block * count, count)], outs.at[1, slot]),
            pltpu.make_async_copy(norm_stage.at[slot], normed.at[layer, at], outs.at[2, slot]),
        ]

    def finish_sums(op):
        layer, block = op // 4, op % 4
        job = sums_of(op)
        squares_of(op).wait()
        total = squares[op, x, 0:1, :]
        for step in (1, 2, 3):
            total = total + others[op, (x + step) % 4, 0:1, :]
        inverse = lax.rsqrt(total / whole_inner + EPS)
        inverses[layer, block] = jnp.broadcast_to(inverse, (8, LANES))
        column = row_to_column(inverse)[:quarter]
        job.wait()
        branch = column * job.result()
        value = res[layer, block] + branch
        res[layer + 1, block] = value
        job.finish()

        @pl.when(layer == 0)
        def _():
            hidden[1, owned(block, x, quarter)] = value.astype(BF16)
            gather_of(block).start()

        @pl.when(layer == 1)
        def _():
            dots = jnp.sum(error_rows[block].astype(F32) * branch, -1, keepdims=True) / whole_inner
            own_scales[block] = jnp.zeros((8, LANES), F32)
            own_scales[block, 0:1, :] = inverse
            own_scales[block, 1:2, 0:quarter] = column_to_row(dots)
            scales_of(block).start()

    error_loads = [
        pltpu.make_async_copy(errors.at[owned(block, x, quarter)], error_rows.at[block], load.at[32 + block])
        for block in range(4)
    ]
    own_block = hidden.at[1, pl.ds(pl.multiple_of(x * ROWS, ROWS), ROWS)]
    first_copy = pltpu.make_async_copy(own_block, firsts.at[pipe], load.at[36])
    swap = remote(own_block, firsts.at[pipe], (ps, pr), 0, at_pipe(1 - pipe))

    def step(op, carry):
        layer, block = op // 4, op % 4

        @pl.when(op < 8)
        def _():
            @pl.when(layer == 1)
            def _():
                job = gather_of(block)
                job.wait(2, 3, 4, 5)
                job.finish()

            @pl.when(op == 7)
            def _():
                first_copy.start()
                swap.start()

            @pl.when(op >= 2)
            def _():
                for copy in outs_of(op - 2):
                    copy.wait()

            slot = op % 2
            at = pl.ds(pl.multiple_of(block * ROWS, ROWS), ROWS)
            value = hidden[layer, at].astype(F32)
            gain = jnp.concatenate([few[layer, 6:7, lead:], few[layer, 7:8, :]], 1)
            norm_stage[slot] = (value * norm_scale(value) * gain).astype(BF16)
            forward_block(layer_sizes, block == 0, norm_stage[slot], w_held.at[layer], few.at[layer], selector[...],
                          stage.at[slot], state_stage.at[slot], part.at[op], squares.at[op], state, pad)
            for copy in outs_of(op):
                copy.start()

        @pl.when(op == 0)
        def _():
            e_ring.relay()

        @pl.when(op == 1)
        def _():
            weight_rings[1].relay()

        @pl.when(op == 2)
        def _():
            e_ring.wait(2, 3, 4, 5)
            e_ring.finish()
            for copy in error_loads:
                copy.start()

        @pl.when(op == 3)
        def _():
            weight_rings[1].finish()
            for copy in w_loads[1]:
                copy.start()
            for copy in error_loads:
                copy.wait()

        @pl.when((op >= 3) & (op < 7))
        def _():
            gather_of(op - 3).relay()

        @pl.when(op >= 2)
        def _():
            finish_sums(op - 2)

        @pl.when((op >= 1) & (op < 9))
        def _():
            sums_of(op - 1).relay()

        @pl.when(op < 8)
        def _():
            sums_of(op).start()
            squares_of(op).start()

        @pl.when(op == 3)
        def _():
            for copy in w_loads[1]:
                copy.wait()

        return carry

    lax.fori_loop(0, 10, step, 0)
    for op in (6, 7):
        for copy in outs_of(op):
            copy.wait()
    keep = [pltpu.make_async_copy(own_scales.at[block], scales.at[block, x], load.at[37 + block]) for block in range(4)]
    for copy in keep:
        copy.start()
    for block in range(4):
        scales_of(block).wait()
    for copy in keep:
        copy.wait()
    first_copy.wait()
    swap.wait()


class WeightRows:
    def __init__(self, source, slot, sems, core_sems):
        _, y, core, _ = place()
        self.core_sems, self.device = core_sems, at_core(1 - core)
        self.slot = lambda origin, half: slot(origin, half, core)
        self.ring = RingGather(y, at_y, source, self.slot, sems)
        self.hand = [remote(source(half), self.slot(y, half), core_sems, 6 + half, self.device) for half in range(2)]
        for index in range(6):
            held = self.slot(*self.ring.origins[index])
            self.hand.append(remote(held, held, core_sems, index, self.device))

    def start(self):
        self.ring.start()
        for copy in self.hand[:2]:
            copy.start()

    def relay(self):
        self.ring.relay()
        for index in range(2):
            self.hand[2 + index].start()

    def finish(self):
        for index in range(2, 6):
            self.ring.wait(index)
            self.hand[2 + index].start()
        self.ring.finish()
        for copy in self.hand:
            copy.wait()


def forward_all(inputs, out_grad, shard, few, inner, pair, heads, whole_inner):
    _, part, width = inputs.shape
    rows, columns = shard.shape
    conv = inner + pair
    lead = conv - (width - conv)
    length = 4 * part
    _, saved_columns = columns_of(inner, conv)
    quarter = ROWS // 4
    chunks = ROWS // CHUNK
    selector, _ = constants(inner, heads)
    half = (2, 2, part // 2, width)
    shape = jax.ShapeDtypeStruct
    return pl.pallas_call(
        partial(forward_all_kernel, (inner, pair, heads, lead, whole_inner)),
        out_shape=[
            shape((2,) + few.shape, F32),
            shape((2, 16, rows, columns), BF16),
            shape((length, width), BF16),
            shape((2, length, width), BF16),
            shape((2, length, saved_columns), F32),
            shape((2, length // CHUNK, pair // 2, inner), F32),
            shape((3, 4, quarter, width), F32),
            shape((2, 4, 8, LANES), F32),
            shape((4, 4, 8, LANES), F32),
            shape((2, part, width), BF16),
        ],
        in_specs=[ANY, ANY, ANY, VMEM, VMEM],
        out_specs=[VMEM, ANY, ANY, ANY, ANY, ANY, VMEM, VMEM, ANY, ANY],
        scratch_shapes=[
            pltpu.VMEM((2, length, width), BF16),
            pltpu.VMEM((2, 16 * rows, columns), BF16),
            pltpu.VMEM((8, ROWS, width), BF16),
            pltpu.VMEM((8, 2, quarter // 2, width), BF16),
            pltpu.VMEM((8, 2, quarter // 2, width), BF16),
            pltpu.VMEM((8, 2, 2, quarter // 2, width), BF16),
            pltpu.VMEM((8, 4, 8, LANES), F32),
            pltpu.VMEM((8, 4, 8, LANES), F32),
            pltpu.VMEM((2, ROWS, saved_columns), F32),
            pltpu.VMEM((2, chunks, pair // 2, inner), F32),
            pltpu.VMEM((2, ROWS, width), BF16),
            pltpu.VMEM((4, quarter, width), BF16),
            pltpu.VMEM((4, 8, LANES), F32),
            pltpu.VMEM((pair // 2, inner), F32),
            pltpu.VMEM((ROWS + 8, conv), F32),
            pltpu.VMEM((4, rows, columns), BF16),
            pltpu.VMEM((2,) + few.shape, F32),
        ]
        + gather_sems() * 3
        + (gather_sems() + dma(8)) * 2
        + dma(1)
        + [pltpu.SemaphoreType.DMA((8, 6))] * 2
        + [pltpu.SemaphoreType.DMA((4, 6))] * 2
        + [pltpu.SemaphoreType.DMA((2,))]
        + [pltpu.SemaphoreType.DMA((8, 3))] * 2
        + [pltpu.SemaphoreType.DMA((4, 3))] * 2
        + dma(1)
        + [pltpu.SemaphoreType.DMA((3, 2)), pltpu.SemaphoreType.DMA((41,))],
        compiler_params=remote_params(0),
        name="forward_layers",
    )(inputs.reshape(half), out_grad.reshape(half), shard, few, selector)


class Deliver:
    def __init__(self, layer, source, target, sends, recvs, local):
        z, _, _, x = place()
        self.pipe = z % 2
        self.here = self.pipe == layer
        self.copies = [
            pltpu.make_async_remote_copy(
                src_ref=source.at[(x + step) % 4],
                dst_ref=target.at[self.pipe, x],
                send_sem=sends.at[step],
                recv_sem=recvs.at[self.pipe * 4 + step],
                device_id={"pipe": layer, "tensor": (x + step) % 4},
                device_id_type=MESH,
            )
            for step in range(4)
        ]
        self.arrivals = [
            pltpu.make_async_remote_copy(
                src_ref=source.at[x],
                dst_ref=target.at[1 - self.pipe, x],
                send_sem=sends.at[step],
                recv_sem=recvs.at[(1 - self.pipe) * 4 + step],
                device_id={"pipe": 1 - self.pipe, "tensor": x},
                device_id_type=MESH,
            )
            for step in range(4)
        ]
        self.local = pltpu.make_async_copy(source.at[x], target.at[self.pipe, x], local)

    def start(self):
        for copy in self.copies[1:]:
            copy.start()

        @pl.when(self.here)
        def _():
            self.local.start()

        @pl.when(jnp.logical_not(self.here))
        def _():
            self.copies[0].start()

    def wait(self):
        for copy in self.copies[1:]:
            copy.wait_send()

        @pl.when(self.here)
        def _():
            self.local.wait()
            for copy in self.copies[1:] + self.arrivals:
                copy.wait_recv()

        @pl.when(jnp.logical_not(self.here))
        def _():
            self.copies[0].wait_send()


def both_pipes(x, pipe):
    return [{"pipe": 1 - pipe, "tensor": (x + step) % 4} for step in range(4)]


def turn_kernel(inner, lead, part, res, few, errors_later, inverses, grads, few_grad,
                errors, scales, input_grad, few_total, middle,
                raw, own, sent, b0, b1, b2, kept, arrived, total, d0, d1, d2,
                xs, xr, gs, gr, gl, ts, tr, cs, cr, ys, yr, load):
    z, y, core, x = place()
    quarter = ROWS // 4
    reads = [
        pltpu.make_async_copy(errors_later.at[owned(block, x, quarter)], raw.at[block], load.at[8 + block])
        for block in range(4)
    ]
    for read in reads:
        read.start()
    greet(*around(x, at_x, (1, 2, 3)), *around(y, at_y), at_core(1 - core))
    two = lambda half: pl.ds(2 * half, 2)
    sums = RingScatter(x, at_x, lambda owner, half: part.at[two(half), owner], (b0, b1, b2), (xs, xr))
    sums.start()
    cores = CoreSum(grads, kept, arrived, total, (cs, cr), load)
    cores.start()
    cores.finish()
    y_sums = RingScatter(y, at_y, lambda owner, half: total.at[owner, half], (d0, d1, d2), (ys, yr))
    y_sums.start()
    for read in reads:
        read.wait()
    gain = norm_gain_of(few, 1, lead)
    sums.relay()
    y_sums.relay()
    sums.wait()
    gain_grad = jnp.zeros_like(gain)
    own[...] = jnp.zeros_like(own)
    for half in range(2):
        result = sums.result(half)
        for index in range(2):
            block = 2 * half + index
            value, gain_part = back_through_norm(res[1, block], raw[block].astype(F32), result[index], gain)
            gain_grad = gain_grad + gain_part
            input_grad[block] = value
            low = value.astype(BF16)
            sent[block] = low
            branch = res[1, block] - res[0, block]
            dots = jnp.sum(low.astype(F32) * branch, -1, keepdims=True) / inner
            own[block, 0:1, :] = inverses[0, block, 0:1, :]
            own[block, 1:2, 0:quarter] = column_to_row(dots)
    x_ring = RingGather(x, at_x, lambda half: sent.at[two(half)], lambda origin, half: errors.at[two(half), origin], (gs, gr, gl))
    x_ring.start()
    tell = Everyone(x, at_x, lambda to: own, lambda me: scales.at[pl.ds(0, 4), me], (ts, tr))
    tell.start()
    keep = pltpu.make_async_copy(own, scales.at[pl.ds(0, 4), x], load.at[12])
    keep.start()
    add_norm_grad(few_total, few_grad, gain_grad, lead)
    y_sums.wait()
    for half in range(2):
        middle[half] = y_sums.result(half).astype(BF16)
    y_sums.finish()
    x_ring.relay()
    keep.wait()
    tell.wait()
    x_ring.wait(2, 3, 4, 5)
    x_ring.finish()
    sums.finish()


def turn_call(part, res, few, errors, inverses, grads, few_grad, inner):
    _, blocks, quarter, width = res.shape
    lead = few.shape[2] - (width - few.shape[2])
    columns = grads.shape[1]
    piece = grads.shape[0] // 16
    owned_rows = (blocks, quarter, width)
    shape = jax.ShapeDtypeStruct
    return pl.pallas_call(
        partial(turn_kernel, inner, lead),
        out_shape=[
            shape((blocks, 4, quarter, width), BF16),
            shape((blocks, 4, 8, LANES), F32),
            shape(owned_rows, F32),
            shape(few_grad.shape, F32),
            shape((2, piece, columns), BF16),
        ],
        in_specs=[VMEM, VMEM, VMEM, ANY, VMEM, ANY, VMEM],
        out_specs=[ANY, ANY, VMEM, VMEM, VMEM],
        scratch_shapes=[
            pltpu.VMEM(owned_rows, BF16),
            pltpu.VMEM((blocks, 8, LANES), F32),
            pltpu.VMEM(owned_rows, BF16),
        ]
        + scatter_buffers(2, quarter, width)
        + core_buffers(piece, columns)
        + scatter_buffers(piece, columns)
        + dma(6) + gather_sems() + dma(3) + dma(8) + dma(6)
        + [pltpu.SemaphoreType.DMA((13,))],
        compiler_params=remote_params(3),
        name="between_gradients",
    )(part.reshape(blocks, 4, quarter, width), res, few, errors, inverses,
      grads.reshape(2, 4, 2, piece, columns), few_grad)


def final_kernel(sizes, part, res, few, error, errors, grads, middle, few_grad, few_later,
                 last_out, first_grad, second_grad, large, few_sum, few_shared, state_grad,
                 low_out, low_grad, b0, b1, b2, kept, arrived, total, d0, d1, d2, e0, e1, e2, z_blocks,
                 mine, pair, y_few, z_few, x_few, state_parts,
                 xs, xr, ps, pr, cs, cr, ys, yr, zs, zr, fs, fr, hs, hr, js, jr, ks, kr, ws, wr,
                 os, og, is_, ig, load):
    lead, state_at, state_columns = sizes
    z, y, core, x = place()
    pipe = z % 2
    every = (1, 2, 3)
    for block in range(4):
        low_out[block] = res[2, block].astype(BF16)
    greet(*around(x, at_x, every), *around(y, at_y, every), *around(z, at_z, every), at_core(1 - core),
          *both_pipes(x, pipe))
    two = lambda half: pl.ds(2 * half, 2)
    sums = RingScatter(x, at_x, lambda owner, half: part.at[two(half), owner], (b0, b1, b2), (xs, xr))
    sums.start()
    cores = CoreSum(grads, kept, arrived, total, (cs, cr), load)
    cores.start()
    own_block = errors.at[x]
    keep = pltpu.make_async_copy(own_block, second_grad.at[pipe], load.at[8])
    keep.start()
    swap = remote(own_block, second_grad.at[pipe], (ps, pr), 0, at_pipe(1 - pipe))
    swap.start()
    output = Deliver(1, low_out, last_out, os, og, load.at[9])
    cores.finish()
    y_sums = RingScatter(y, at_y, lambda owner, half: total.at[owner, half], (d0, d1, d2), (ys, yr))
    y_sums.start()
    gain = norm_gain_of(few, 0, lead)
    sums.relay()
    output.start()
    y_sums.relay()
    sums.wait()
    gain_grad = jnp.zeros_like(gain)
    for half in range(2):
        result = sums.result(half)
        for index in range(2):
            block = 2 * half + index
            value, gain_part = back_through_norm(res[0, block], error[block], result[index], gain)
            gain_grad = gain_grad + gain_part
            low_grad[block] = value.astype(BF16)
    gradient = Deliver(0, low_grad, first_grad, is_, ig, load.at[10])
    gradient.start()
    mine[1] = few_later[...]
    add_norm_grad(mine.at[0], few_grad, gain_grad, lead)
    few_core = remote(mine, pair, (fs, fr), 0, at_core(1 - core))
    few_core.start()
    few_core.wait()
    mine[...] = mine[...] + pair[...]
    few_y = Everyone(y, at_y, lambda to: mine, lambda me: y_few.at[me], (hs, hr))
    few_y.start()
    y_sums.wait()
    rows = z_blocks.shape[2]
    for z_hi in range(2):
        first = y_sums.result(z_hi).astype(BF16)
        second = middle[z_hi]
        for half in range(2):
            z_blocks[2 * z_hi, half] = first[half * rows : (half + 1) * rows]
            z_blocks[2 * z_hi + 1, half] = second[half * rows : (half + 1) * rows]
    y_sums.finish()
    z_sums = RingScatter(z, at_z, lambda owner, half: z_blocks.at[owner, half], (e0, e1, e2), (zs, zr))
    z_sums.start()
    few_y.wait()
    y_few[y] = mine[...]
    mine[...] = (y_few[0] + y_few[1]) + (y_few[2] + y_few[3])
    few_z = Everyone(z, at_z, lambda to: mine.at[to % 2], lambda me: z_few.at[me], (js, jr))
    few_z.start()
    z_sums.relay()
    few_z.wait()
    z_few[z] = mine[pipe]
    few_sum[...] = (z_few[0] + z_few[1]) + (z_few[2] + z_few[3])
    x_few[x] = few_sum[...]
    few_x = Everyone(x, at_x, lambda to: few_sum, lambda me: x_few.at[me], (ks, kr))
    few_x.start()
    z_sums.wait()
    for half in range(2):
        large[half * rows : (half + 1) * rows, :] = z_sums.result(half)
    z_sums.finish()
    quarter = 2 * rows // 4
    for block in range(4):
        state_parts[0, block] = large[block * quarter : (block + 1) * quarter, state_at : state_at + state_columns]
    state_x = Everyone(x, at_x, lambda to: state_parts.at[0, to], lambda me: state_parts.at[1, me], (ws, wr))
    state_x.start()
    few_x.wait()
    few_shared[...] = (x_few[0] + x_few[1]) + (x_few[2] + x_few[3])
    state_x.wait()
    total_state = state_parts[0, x]
    for step in every:
        total_state = total_state + state_parts[1, (x + step) % 4]
    state_grad[...] = total_state
    keep.wait()
    swap.wait()
    output.wait()
    gradient.wait()
    sums.finish()


def final_call(part, res, few, error, errors, grads, middle, few_grad, few_later, sizes):
    blocks, quarter, width = error.shape
    wide = few.shape[2]
    lead = wide - (width - wide)
    columns = grads.shape[1]
    piece = grads.shape[0] // 16
    state_at, state_columns = sizes
    both = (2,) + few_grad.shape
    delivered = jax.ShapeDtypeStruct((2, blocks, quarter, width), BF16)
    return pl.pallas_call(
        partial(final_kernel, (lead, state_at, state_columns)),
        out_shape=[
            delivered,
            delivered,
            delivered,
            jax.ShapeDtypeStruct((piece, columns), F32),
            jax.ShapeDtypeStruct(few_grad.shape, F32),
            jax.ShapeDtypeStruct(few_grad.shape, F32),
            jax.ShapeDtypeStruct((piece // 4, state_columns), F32),
        ],
        in_specs=[VMEM, VMEM, VMEM, VMEM, ANY, ANY, VMEM, VMEM, VMEM],
        out_specs=[ANY, ANY, ANY, VMEM, VMEM, VMEM, VMEM],
        scratch_shapes=[pltpu.VMEM(error.shape, BF16), pltpu.VMEM(error.shape, BF16)]
        + scatter_buffers(2, quarter, width)
        + core_buffers(piece, columns)
        + scatter_buffers(piece, columns)
        + scatter_buffers(piece // 2, columns)
        + [
            pltpu.VMEM((4, 2, piece // 2, columns), BF16),
            pltpu.VMEM(both, F32),
            pltpu.VMEM(both, F32),
            pltpu.VMEM((4,) + both, F32),
            pltpu.VMEM((4,) + few_grad.shape, F32),
            pltpu.VMEM((4,) + few_grad.shape, F32),
            pltpu.VMEM((2, 4, piece // 4, state_columns), F32),
        ]
        + dma(6) + dma(1) + dma(8) + dma(6) + dma(6) + dma(1) + dma(3) + dma(3) + dma(3) + dma(3)
        + [pltpu.SemaphoreType.DMA((4,)), pltpu.SemaphoreType.DMA((8,))] * 2
        + [pltpu.SemaphoreType.DMA((11,))],
        compiler_params=remote_params(4),
        name="final_sums",
    )(part.reshape(blocks, 4, quarter, width), res, few, error, errors,
      grads.reshape(2, 4, 2, piece, columns), middle, few_grad, few_later)


def body(inputs, out_grad, norm_gain, in_gate_x, in_read_write, in_step, conv_main, conv_state,
         step_bias, log_rate, skip_gain, gate_gain, out_weight):
    _, part, width = inputs.shape
    inner = out_weight.shape[2]
    pair = in_read_write.shape[2]
    heads = step_bias.shape[1]
    whole_inner = inner * lax.axis_size("tensor")
    split = 2 * inner + pair
    wide = inner + pair
    first = lax.axis_index("pipe") == 0
    shard = jnp.concatenate(
        [
            in_gate_x[0, :, 0],
            in_gate_x[0, :, 1],
            in_read_write[0],
            jnp.pad(in_step[0], ((0, 0), (0, LANES - heads))),
            out_weight[0],
        ],
        1,
    )
    rate = -jnp.exp(log_rate[0])
    pad = ((0, 0), (0, LANES - heads))
    skip = jnp.broadcast_to(skip_gain[0][:, None], (heads, inner // heads)).reshape(1, inner)
    few = jnp.concatenate(
        [
            jnp.concatenate([conv_main[0], conv_state[0]], 1),
            jnp.concatenate([gate_gain, jnp.pad(step_bias, pad), jnp.pad(rate[None], pad)], 1),
            jnp.concatenate([skip, norm_gain], 1).reshape(2, wide),
        ],
        0,
    )
    few, weights, errors1, normed, saved, states, res, inverses, scales1, firsts = forward_all(
        inputs, out_grad, shard, few, inner, pair, heads, whole_inner
    )
    weights = weights.reshape(2, width, -1)
    part1, grad1, mixed1, few_grad1 = backward_call(
        1, errors1, scales1, weights, few, saved, states, inner, pair, heads
    )
    large1 = weight_call(1, normed, grad1, errors1, mixed1)
    errors0, scales0, input_grad1, few_grad1, middle = turn_call(
        part1, res, few, errors1, inverses, large1, few_grad1, whole_inner
    )
    rows0 = errors0.reshape(4 * part, width)
    part0, grad0, mixed0, few_grad0 = backward_call(
        0, rows0, scales0, weights, few, saved, states, inner, pair, heads
    )
    large0 = weight_call(0, normed, grad0, rows0, mixed0)
    last_out, first_grad, second_grad, large, few_sum, few_shared, state_grad = final_call(
        part0, res, few, input_grad1, errors0, large0, middle, few_grad0, few_grad1, (2 * inner, pair)
    )
    by_layer = lambda zero, one: jnp.where(
        first, zero.reshape(1, 2, part, width), one.reshape(1, 2, part, width)
    ).astype(F32)
    rates = few_sum[5, inner + LANES : inner + LANES + heads] * rate
    return (
        by_layer(firsts, last_out),
        by_layer(first_grad, second_grad),
        few_shared[6:].reshape(1, 2 * wide)[:, inner:],
        large[:, : 2 * inner].reshape(1, -1, 2, inner),
        state_grad[None],
        large[None, :, split : split + heads],
        few_sum[None, :5, :inner],
        few_shared[None, :5, inner:],
        few_sum[5:6, inner : inner + heads],
        rates[None],
        few_sum[6, :inner].reshape(1, heads, -1).sum(2),
        few_sum[5:6, :inner],
        large[None, :, split + LANES :],
    )


def solution(mesh):
    in_specs = (
        P("dp", "tensor", None),
        P("dp", "tensor", None),
        P("pipe", None),
        P("pipe", "dp", None, "tensor"),
        P("pipe", "dp", None),
        P("pipe", "dp", "tensor"),
        P("pipe", None, "tensor"),
        P("pipe", None, None),
        P("pipe", "tensor"),
        P("pipe", "tensor"),
        P("pipe", "tensor"),
        P("pipe", "tensor"),
        P("pipe", "dp", "tensor"),
    )
    out_specs = (
        P("pipe", "dp", "tensor", None),
        P("pipe", "dp", "tensor", None),
        P("pipe", None),
        P("pipe", "dp", None, "tensor"),
        P("pipe", ("dp", "tensor"), None),
        P("pipe", "dp", "tensor"),
        P("pipe", None, "tensor"),
        P("pipe", None, None),
        P("pipe", "tensor"),
        P("pipe", "tensor"),
        P("pipe", "tensor"),
        P("pipe", "tensor"),
        P("pipe", "dp", "tensor"),
    )
    return jax.shard_map(body, mesh=mesh, in_specs=in_specs, out_specs=out_specs, check_vma=False)
```

time: 359 us -> 302 us (0.84)
  Pallas kernels: 313 us -> 281 us
  between operations: 14.3 us -> 0.79 us
  local copies, waits for them, and re-layouts: 19.2 us -> 11.2 us
    pallas_call x8 -> x4, Pallas kernels: 213 us -> 179 us  [the longest x1 118 us: forward_all(): pl.pallas_call(partial(forward_all_kernel, (inner, pair, heads, lead, who...]
    select_n x4 -> x1, other arithmetic: 6.17 us -> 0.11 us  [body(): jnp.where(first, zero.reshape(1, 2, part, width), one.reshape(1, 2, part,...]
    convert_element_type x0 -> x2, other arithmetic: none -> 4.39 us  [body(): by_layer = lambda zero, one: jnp.where(first, zero.reshape(1, 2, part, wi...]
  transfers between devices with their start and end apart: 1 -> 0, of which waited for: 0 -> 0; matrix products, arithmetic and copies ran while one was open for 0% -> 0% of each run, Pallas kernels for 32% -> 0%
where the time goes in v3:
time: 302 us; the launch traced here: 301 us
  Pallas kernels  281 us (93%)
  local copies, waits for them, and re-layouts  11.2 us (4%)
  other arithmetic  8.34 us (3%)
    pallas_call x1, Pallas kernels, forward_all(): pl.pallas_call(partial(forward_all_kernel, (inner, pair, heads, lead, who...  118 us
    pallas_call x1, Pallas kernels, final_call(): pl.pallas_call(partial(final_kernel, (lead, state_at, state_columns)), ou...  52.8 us
    pallas_call x2, Pallas kernels, backward_call(): pl.pallas_call(partial(backward_kernel, (inner, pair, heads)), grid=(coun...  48.9 us
    pallas_call x1, Pallas kernels, turn_call(): pl.pallas_call(partial(turn_kernel, inner, lead), out_shape=[shape((block...  43.1 us
    pallas_call x2, Pallas kernels, weight_call(): pl.pallas_call(weight_kernel, grid=(width // ROWS,), in_specs=[pl.BlockSp...  18 us

profile of v3, /device:TPU:0, one launch (start us, length us, event | category | flops | bytes accessed | tf_op | source)
XLA Modules:
  0.0 301.0 jit_solution(5784912512107344124)
XLA Ops:
  0.6 1.2 fusion.8
  1.9 0.8 bitcast_dynamic-update-slice_fusion.1
  2.7 0.8 copy.33
  3.5 0.8 bitcast_dynamic-update-slice_fusion.shard
  4.3 0.0 copy-start.3
  4.3 0.7 exponential_negate_fusion
  5.0 0.7 broadcast_in_dim.25
  5.7 0.1 reshape.104
  5.8 0.7 maximum_reduce_fusion
  6.5 0.7 copy.51
  7.2 0.7 copy.50
  7.9 1.3 fusion.3.few_in
  9.2 0.0 copy-done.3
  9.2 117.9 %forward_layers.1 = (f32[2,8,768]{2,1,0:T(8,128)}, bf16[2,16,64,1920]{3,2,1,0:T(8,128)(2,1)}, bf16[1024,1024]{1,0:T(8,128)(2,1)}, bf16[2,1024,1024]{2,1,0:T(8,12...) custom-call(bf16[2,2,128,1024]{3,2,1,0:T(8,128)(2,1)} %bitcast.60, ...), custom_call_target="tpu_custom_call" | custom-call | tf_op jit(solution)/shard_map/forward_layers/pallas_call | solution.py:903
  127.2 24.4 %layer_backward.2 = (bf16[1024,1024]{1,0:T(8,128)(2,1)}, bf16[1024,1408]{1,0:T(8,128)(2,1)}, bf16[1024,512]{1,0:T(8,128)(2,1)}, f32[8,768]{1,0:T(8,128)}) custom-call(bf16[1024,1024]{1,0:T(8,128)(2,1)} %get-tuple-element.44.e_ref.errors_ref.errors_later, f32[4,4,8,128]{3,2,1,0:T(8,128)} %get-tuple-element.45.scales_ref, bf16[2,1024,1920]{2,1,0:T(8,128)(2,1)} %bitcast.51, ...), custom_call_target="tpu_custom_call" | custom-call | tf_op jit(solution)/shard_map/layer_backward/pallas_call | solution.py:217
  151.6 9.0 %weight_gradients.2 = bf16[1024,1920]{1,0:T(8,128)(2,1)} custom-call(bf16[2,1024,1024]{2,1,0:T(8,128)(2,1)} %get-tuple-element.53.rows_ref, bf16[1024,1408]{1,0:T(8,128)(2,1)} %get-tuple-element.54.grad_ref, bf16[1024,1024]{1,0:T(8,128)(2,1)} %get-tuple-element.44.e_ref.errors_ref.errors_later, bf16[1024,512]{1,0:T(8,128)(2,1)} %get-tuple-element.55.mixed_ref), custom_call_target="tpu_custom_call" | custom-call | tf_op jit(solution)/shard_map/weight_gradients/pallas_call | solution.py:262
  160.6 43.1 %between_gradients.1 = (bf16[4,4,64,1024]{3,2,1,0:T(8,128)(2,1)}, f32[4,4,8,128]{3,2,1,0:T(8,128)}, f32[4,64,1024]{2,1,0:T(8,128)}, f32[8,768]{1,0:T(8,128)}, bf16[2,64,1920]{2,1,0:T(8,128)(2,1)}) custom-call(bf16[4,4,64,1024]{3,2,1,0:T(8,128)(2,1)} %bitcast.59, f32[3,4,64,1024]{3,2,1,0:T(8,128)} %get-tuple-element.51.res, ...), custom_call_target="tpu_custom_call" | custom-call | tf_op jit(solution)/shard_map/between_gradients/pallas_call | solution.py:1081
  203.6 24.4 %layer_backward.3 = (bf16[1024,1024]{1,0:T(8,128)(2,1)}, bf16[1024,1408]{1,0:T(8,128)(2,1)}, bf16[1024,512]{1,0:T(8,128)(2,1)}, f32[8,768]{1,0:T(8,128)}) custom-call(bf16[1024,1024]{1,0:T(8,128)(2,1)} %bitcast.53, f32[4,4,8,128]{3,2,1,0:T(8,128)} %get-tuple-element.58.scales_ref, bf16[2,1024,1920]{2,1,0:T(8,128)(2,1)} %bitcast.52, ...), custom_call_target="tpu_custom_call" | custom-call | tf_op jit(solution)/shard_map/layer_backward/pallas_call | solution.py:217
  228.1 9.0 %weight_gradients.3 = bf16[1024,1920]{1,0:T(8,128)(2,1)} custom-call(bf16[2,1024,1024]{2,1,0:T(8,128)(2,1)} %get-tuple-element.53.rows_ref, bf16[1024,1408]{1,0:T(8,128)(2,1)} %get-tuple-element.61.grad_ref, bf16[1024,1024]{1,0:T(8,128)(2,1)} %bitcast.54, bf16[1024,512]{1,0:T(8,128)(2,1)} %get-tuple-element.62.mixed_ref), custom_call_target="tpu_custom_call" | custom-call | tf_op jit(solution)/shard_map/weight_gradients/pallas_call | solution.py:262
  237.1 0.0 copy-start
  237.1 52.8 %final_sums.1 = (bf16[2,4,64,1024]{3,2,1,0:T(8,128)(2,1)}, bf16[2,4,64,1024]{3,2,1,0:T(8,128)(2,1)}, bf16[2,4,64,1024]{3,2,1,0:T(8,128)(2,1)}, f32[64,1920]{1,0:...) custom-call(bf16[4,4,64,1024]{3,2,1,0:T(8,128)(2,1)} %bitcast.58, ...), custom_call_target="tpu_custom_call" | custom-call | tf_op jit(solution)/shard_map/final_sums/pallas_call | solution.py:1214
  289.9 0.0 copy-start.1
  289.9 0.0 copy-start.2
  289.9 0.0 copy-done
  289.9 2.8 bitcast_convert_fusion
  292.8 0.0 copy-done.1
  292.8 0.0 copy-done.2
  292.8 0.0 copy-start.7
  292.8 0.0 copy-start.4
  292.8 0.1 broadcast_select_fusion
  292.9 0.0 copy-start.5
  292.9 0.0 copy-start.8
  292.9 0.0 copy-start.6
  292.9 1.6 convert.3
  294.5 0.0 copy-done.7
  294.5 0.6 slice.52
  295.1 0.0 copy-done.4
  295.1 0.9 reshape.114
  296.1 0.7 copy.34
  296.7 0.0 copy-done.5
  296.7 0.6 copy.35
  297.3 0.6 copy.36
  297.9 0.0 copy-done.8
  297.9 0.5 slice_multiply_fusion
  298.5 0.6 fusion.9
  299.1 0.1 reshape_squeeze.3
  299.1 0.6 reduce_sum.11
  299.8 0.7 slice_bitcast_fusion
  300.4 0.0 copy-done.6
  300.4 0.6 copy.57
  (10 shorter events, 0.1 us)
Async XLA Ops:
  4.3 4.9 %copy-start.3 = (bf16[64,1920]{1,0:T(8,128)(2,1)}, bf16[64,1920]{1,0:T(8,128)(2,1)S(1)}, u32[]{:S(2)}) copy-start(bf16[64,1920]{1,0:T(8,128)(2,1)S(1)} %bitcast_dynamic-update-slice_fusion.shard) | copy-start | bytes 737284
  237.1 52.8 %copy-start = (bf16[2,256,1024]{2,1,0:T(8,128)(2,1)S(1)}, bf16[2,256,1024]{2,1,0:T(8,128)(2,1)}, u32[]{:S(2)}) copy-start(bf16[2,256,1024]{2,1,0:T(8,128)(2,1)} %get-tuple-element.43) | copy-start | bytes 3145732
  289.9 2.9 copy-start.1
  289.9 2.9 copy-start.2
  292.8 1.7 copy-start.7
  292.8 2.3 copy-start.4
  292.9 3.8 %copy-start.5 = (f32[8,768]{1,0:T(8,128)S(1)}, f32[8,768]{1,0:T(8,128)}, u32[]{:S(2)}) copy-start(f32[8,768]{1,0:T(8,128)} %get-tuple-element.72) | copy-start | bytes 73732
  292.9 5.0 %copy-start.8 = (f32[1,8]{1,0:T(1,128)S(1)}, f32[1,8]{1,0:T(1,128)}, u32[]{:S(2)}) copy-start(f32[1,8]{1,0:T(1,128)} %param.27) | copy-start | bytes 100
  292.9 7.5 %copy-start.6 = (f32[16,256]{1,0:T(8,128)S(1)}, f32[16,256]{1,0:T(8,128)}, u32[]{:S(2)}) copy-start(f32[16,256]{1,0:T(8,128)} %get-tuple-element.71) | copy-start | bytes 49156

commit v4 on v3

--- a/solution.py
+++ b/solution.py
@@ -71,126 +71,6 @@
     return delta, log_decay
 
 
-def backward_kernel(sizes, e_ref, scales_ref, w_ref, few_ref, selector_ref,
-                    collector_ref, saved_ref, s_ref,
-                    part_ref, grad_ref, mixed_ref, few_out, state, later, pad):
-    inner, pair, heads = sizes
-    states = pair // 2
-    split = inner + inner + pair
-    conv = inner + pair
-    (z_at, p_at, c_at, raw_at, y_at), _ = columns_of(inner, conv)
-
-    @pl.when(pl.program_id(0) == 0)
-    def _():
-        state[...] = jnp.zeros_like(state)
-        later[...] = jnp.zeros_like(later)
-        pad[ROWS : ROWS + 8, :] = jnp.zeros((8, conv), F32)
-        few_out[...] = jnp.zeros_like(few_out)
-
-    @pl.when(pl.program_id(0) > 0)
-    def _():
-        pad[ROWS : ROWS + 8, :] = pad[0:8, :]
-
-    selector = selector_ref[...]
-    collector = collector_ref[...]
-    bias = few_ref[0, 5:6, inner : inner + LANES]
-    rate = few_ref[0, 5:6, inner + LANES : inner + 2 * LANES]
-    gain = few_ref[0, 5:6, :inner]
-    skip = few_ref[0, 6:7, :inner]
-    mask = (iota((1, LANES), 1) < heads).astype(F32)
-    first = iota((CHUNK, LANES), 1) < LANES // 2
-    later_in = iota((CHUNK, CHUNK), 1) >= iota((CHUNK, CHUNK), 0)
-    last = iota((CHUNK, LANES), 0) == CHUNK - 1
-    quarter = ROWS // 4
-    column = lambda row: jnp.concatenate(
-        [row_to_column(scales_ref[0, owner, row : row + 1, :])[:quarter] for owner in range(4)], 0
-    )
-    inverse = column(0)
-    inner_dot = column(1)
-    mixed_grad = mm(e_ref[...], w_ref[0, :, split + LANES :])
-    for chunk in reversed(range(ROWS // CHUNK)):
-        at = slice(chunk * CHUNK, (chunk + 1) * CHUNK)
-        z = saved_ref[0, at, z_at]
-        y = saved_ref[0, at, y_at]
-        sig = sigmoid(z)
-        act = z * sig
-        g = y * act * inverse[at]
-        mixed_ref[at, :] = (g * gain).astype(BF16)
-        mixed_here = mixed_grad[at]
-        gated_grad = inverse[at] * (mixed_here * gain - g * inner_dot[at])
-        dy = gated_grad * act
-        grad_ref[at, :inner] = (gated_grad * y * (sig * (1.0 + z - act))).astype(BF16)
-        c = saved_ref[0, at, c_at]
-        csig = sigmoid(c)
-        value = c * csig
-        slope = csig * (1.0 + c - value)
-        xs = value[:, :inner]
-        b_low = value[:, inner : inner + states].astype(BF16)
-        c_low = value[:, inner + states :].astype(BF16)
-        raw = saved_ref[0, at, raw_at]
-        delta, log_decay = steps(raw, bias, rate, mask)
-        turned = log_decay.T
-        final = log_decay[CHUNK - 1 : CHUNK, :]
-        wide_delta = spread(delta, selector, heads)
-        scaled = wide_delta * xs
-        scaled_low = scaled.astype(BF16)
-        dy_low = dy.astype(BF16)
-        products = jnp.where(later_in, mm(b_low, c_low, ((1,), (1,))), 0.0)
-        dproducts = jnp.zeros((CHUNK, CHUNK), F32)
-        within = []
-        for two in range(heads // 2):
-            lanes = slice(two * LANES, (two + 1) * LANES)
-            parts = []
-            for odd in range(2):
-                h = 2 * two + odd
-                mine = first if odd == 0 else ~first
-                decay = jnp.exp(jnp.minimum(turned[h : h + 1, :] - log_decay[:, h : h + 1], 0.0))
-                parts.append(mm((products * decay).astype(BF16), dy_low[:, lanes]))
-                own = jnp.where(mine, scaled_low[:, lanes], jnp.zeros((), BF16))
-                dproducts = dproducts + decay * mm(own, dy_low[:, lanes], ((1,), (1,)))
-            within.append(jnp.where(first, parts[0], parts[1]))
-        dproducts = jnp.where(later_in, dproducts, 0.0).astype(BF16)
-        old = s_ref[0, chunk]
-        old_low = old.astype(BF16)
-        dstate = state[...]
-        dstate_low = dstate.astype(BF16)
-        to_end = spread(jnp.exp(final - log_decay) * mask, selector, heads)
-        from_start = (spread(jnp.exp(log_decay) * mask, selector, heads) * dy).astype(BF16)
-        dscaled = jnp.concatenate(within, 1) + to_end * mm(b_low, dstate_low)
-        dc_state = mm(from_start, old_low, ((1,), (1,))) + mm(dproducts, b_low, ((0,), (0,)))
-        db_state = mm((to_end * scaled).astype(BF16), dstate_low, ((1,), (1,))) + mm(dproducts, c_low)
-        carry = jnp.broadcast_to(jnp.sum(later[...] * dstate, 0, keepdims=True), (8, inner))
-        carry = per_head(carry, collector)[0:1]
-        keep = spread(jnp.broadcast_to(jnp.exp(final) * mask, (8, LANES)), selector, heads)[0:1]
-        state[...] = keep * dstate + mm(c_low, from_start, ((0,), (0,)))
-        later[...] = old
-        flow = dy_low.astype(F32) * (y - skip * xs) - scaled_low.astype(F32) * dscaled
-        dlog = per_head(flow, collector) + jnp.where(last, carry, 0.0)
-        tri = (iota((CHUNK, CHUNK), 1) >= iota((CHUNK, CHUNK), 0)).astype(F32)
-        dstep = mm_exact(tri, dlog)
-        ddelta = per_head(xs * dscaled, collector) + rate * dstep
-        draw = ddelta * sigmoid(raw + bias) * mask
-        few_out[5:6, inner : inner + LANES] += jnp.sum(draw, 0, keepdims=True)
-        few_out[5:6, inner + LANES : inner + 2 * LANES] += jnp.sum(delta * dstep, 0, keepdims=True)
-        few_out[5:6, :inner] += jnp.sum(mixed_here * g, 0, keepdims=True)
-        few_out[6:7, :inner] += jnp.sum(dy * xs, 0, keepdims=True)
-        dxs = wide_delta * dscaled + skip * dy
-        pad[at, :] = jnp.concatenate([dxs, db_state, dc_state], 1) * slope
-        grad_ref[at, split:] = draw.astype(BF16)
-    for chunk in range(ROWS // CHUNK):
-        at = slice(chunk * CHUNK, (chunk + 1) * CHUNK)
-        p = saved_ref[0, at, p_at]
-        total = jnp.zeros((CHUNK, conv), F32)
-        for tap in range(4):
-            begin = chunk * CHUNK + 3 - tap
-            shifted = pad[begin : begin + CHUNK, :]
-            total = total + few_ref[0, tap : tap + 1, :] * shifted
-            few_out[tap : tap + 1, :] += jnp.sum(p * shifted, 0, keepdims=True)
-        few_out[4:5, :] += jnp.sum(pad[at, :], 0, keepdims=True)
-        grad_ref[at, inner:split] = total.astype(BF16)
-    part_ref[...] = mm(grad_ref[...], w_ref[0, :, : split + LANES], ((1,), (1,))).astype(part_ref.dtype)
-
-
 def constants(inner, heads):
     width = inner // heads
     lane = np.arange(LANES)[:, None]
@@ -198,81 +78,6 @@
     selector = ((lane % heads == channel) & (lane < 2 * heads)).astype(np.float32)
     collector = (lane == channel).astype(np.float32).T
     return jnp.asarray(selector, BF16), jnp.asarray(collector, BF16)
-
-
-def whole(array):
-    return pl.BlockSpec(array.shape, lambda i: (0,) * array.ndim)
-
-
-def backward_call(layer, e, scales, w, few, saved, states, inner, pair, heads):
-    length, width = e.shape
-    count = length // ROWS
-    conv = inner + pair
-    split = inner + conv
-    selector, collector = constants(inner, heads)
-    by_rows = lambda columns: pl.BlockSpec((ROWS, columns), lambda i: (count - 1 - i, 0))
-    of_layer = lambda array: pl.BlockSpec((1,) + array.shape[1:], lambda i: (layer, 0, 0))
-    chunks = ROWS // CHUNK
-    out = lambda columns, kind=F32: jax.ShapeDtypeStruct((length, columns), kind)
-    return pl.pallas_call(
-        partial(backward_kernel, (inner, pair, heads)),
-        grid=(count,),
-        in_specs=[
-            by_rows(width),
-            pl.BlockSpec((1,) + scales.shape[1:], lambda i: (count - 1 - i, 0, 0, 0)),
-            of_layer(w),
-            of_layer(few),
-            whole(selector),
-            whole(collector),
-            pl.BlockSpec((1, ROWS, saved.shape[2]), lambda i: (layer, count - 1 - i, 0)),
-            pl.BlockSpec((1, chunks) + states.shape[2:], lambda i: (layer, count - 1 - i, 0, 0)),
-        ],
-        out_specs=[
-            by_rows(width),
-            by_rows(split + LANES),
-            by_rows(inner),
-            pl.BlockSpec((8, conv), lambda i: (0, 0)),
-        ],
-        out_shape=[
-            out(width, BF16),
-            out(split + LANES, BF16),
-            out(inner, BF16),
-            jax.ShapeDtypeStruct((8, conv), F32),
-        ],
-        scratch_shapes=[
-            pltpu.VMEM((pair // 2, inner), F32),
-            pltpu.VMEM((pair // 2, inner), F32),
-            pltpu.VMEM((ROWS + 8, conv), F32),
-        ],
-        compiler_params=pltpu.CompilerParams(vmem_limit_bytes=56 * 2**20),
-        name="layer_backward",
-    )(e, scales, w, few, selector, collector, saved, states)
-
-
-def weight_kernel(rows_ref, grad_ref, errors_ref, mixed_ref, out_ref):
-    columns = grad_ref.shape[1]
-    turn = ((0,), (0,))
-    out_ref[:, :columns] = mm(rows_ref[0], grad_ref[...], turn).astype(out_ref.dtype)
-    out_ref[:, columns:] = mm(errors_ref[...], mixed_ref[...], turn).astype(out_ref.dtype)
-
-
-def weight_call(layer, normed, grad, errors, mixed):
-    length, width = errors.shape
-    columns = grad.shape[1] + mixed.shape[1]
-    return pl.pallas_call(
-        weight_kernel,
-        grid=(width // ROWS,),
-        in_specs=[
-            pl.BlockSpec((1, length, ROWS), lambda i: (layer, 0, i)),
-            whole(grad),
-            pl.BlockSpec((length, ROWS), lambda i: (0, i)),
-            whole(mixed),
-        ],
-        out_specs=pl.BlockSpec((ROWS, columns), lambda i: (i, 0)),
-        out_shape=jax.ShapeDtypeStruct((width, columns), BF16),
-        compiler_params=pltpu.CompilerParams(vmem_limit_bytes=56 * 2**20),
-        name="weight_gradients",
-    )(normed, grad, errors, mixed)
 
 
 MESH = pl.DeviceIdType.MESH
@@ -451,52 +256,6 @@
     return pltpu.CompilerParams(
         collective_id=collective_id, has_side_effects=True, vmem_limit_bytes=56 * 2**20
     )
-
-
-class CoreSum:
-    def __init__(self, grads, kept, arrived, total, sems, load):
-        _, _, core, _ = place()
-        self.kept, self.arrived, self.total = kept, arrived, total
-        self.pieces = [(y, half) for y in range(4) for half in range(2)]
-        self.copies, self.reads = [], []
-        for index, (y, half) in enumerate(self.pieces):
-            target = arrived.at[y, half]
-            self.copies.append(remote(grads.at[half, y, 1 - core], target, sems, index, at_core(1 - core)))
-            self.reads.append(pltpu.make_async_copy(grads.at[half, y, core], kept.at[y, half], load.at[index]))
-
-    def start(self):
-        for copy, read in zip(self.copies, self.reads):
-            copy.start()
-            read.start()
-
-    def finish(self):
-        for copy, read, (y, half) in zip(self.copies, self.reads, self.pieces):
-            read.wait()
-            copy.wait_recv()
-            value = self.kept[y, half].astype(F32) + self.arrived[y, half].astype(F32)
-            self.total[y, half] = value.astype(BF16)
-        for copy in self.copies:
-            copy.wait_send()
-
-
-def core_buffers(rows, columns):
-    return [pltpu.VMEM((4, 2, rows, columns), BF16)] * 3
-
-
-def back_through_norm(value, grad_out, summed, gain):
-    scale = norm_scale(value)
-    unit = value * scale
-    scaled = summed * gain
-    mean = jnp.mean(scaled * unit, -1, keepdims=True)
-    return grad_out + scale * (scaled - unit * mean), jnp.sum(summed * unit, 0, keepdims=True)
-
-
-def add_norm_grad(target, source, gain_grad, lead):
-    wide = target.shape[1]
-    first = wide - lead
-    target[...] = source[...]
-    target[6:7, lead:] = gain_grad[:, :first]
-    target[7:8, :] = gain_grad[:, first:]
 
 
 def owned(block, x, rows):
@@ -634,7 +393,7 @@
 
 
 def forward_all_kernel(sizes, inputs, out_grad, shard, few_in, selector,
-                       few_both, weights, errors, normed, saved, states, res, inverses, scales, firsts,
+                       few_both, weights, errors, normed, saved, states, res, inverses, scales, firsts, last_low,
                        hidden, w_held, part, relays, sums, arrived, squares, others, stage, state_stage, norm_stage,
                        error_rows, own_scales, state, pad, spread_weights, few,
                        xs, xr, xl, es, er, el, zs, zr, zl, ys, yr, yl, cs, cr, y1s, y1r, y1l, c1s, c1r,
@@ -741,16 +500,17 @@
         job.wait()
         branch = column * job.result()
         value = res[layer, block] + branch
-        res[layer + 1, block] = value
         job.finish()
 
         @pl.when(layer == 0)
         def _():
+            res[1, block] = value
             hidden[1, owned(block, x, quarter)] = value.astype(BF16)
             gather_of(block).start()
 
         @pl.when(layer == 1)
         def _():
+            last_low[block] = value.astype(BF16)
             dots = jnp.sum(error_rows[block].astype(F32) * branch, -1, keepdims=True) / whole_inner
             own_scales[block] = jnp.zeros((8, LANES), F32)
             own_scales[block, 0:1, :] = inverse
@@ -909,13 +669,14 @@
             shape((2, length, width), BF16),
             shape((2, length, saved_columns), F32),
             shape((2, length // CHUNK, pair // 2, inner), F32),
-            shape((3, 4, quarter, width), F32),
+            shape((2, 4, quarter, width), F32),
             shape((2, 4, 8, LANES), F32),
             shape((4, 4, 8, LANES), F32),
             shape((2, part, width), BF16),
+            shape((4, quarter, width), BF16),
         ],
         in_specs=[ANY, ANY, ANY, VMEM, VMEM],
-        out_specs=[VMEM, ANY, ANY, ANY, ANY, ANY, VMEM, VMEM, ANY, ANY],
+        out_specs=[VMEM, ANY, ANY, ANY, ANY, ANY, VMEM, VMEM, ANY, ANY, VMEM],
         scratch_shapes=[
             pltpu.VMEM((2, length, width), BF16),
             pltpu.VMEM((2, 16 * rows, columns), BF16),
@@ -952,209 +713,423 @@
 
 class Deliver:
     def __init__(self, layer, source, target, sends, recvs, local):
-        z, _, _, x = place()
+        self.layer, self.source, self.target = layer, source, target
+        self.sends, self.recvs, self.local_sem = sends, recvs, local
+        z, _, _, self.x = place()
         self.pipe = z % 2
         self.here = self.pipe == layer
-        self.copies = [
-            pltpu.make_async_remote_copy(
-                src_ref=source.at[(x + step) % 4],
-                dst_ref=target.at[self.pipe, x],
-                send_sem=sends.at[step],
-                recv_sem=recvs.at[self.pipe * 4 + step],
-                device_id={"pipe": layer, "tensor": (x + step) % 4},
-                device_id_type=MESH,
-            )
-            for step in range(4)
-        ]
-        self.arrivals = [
-            pltpu.make_async_remote_copy(
-                src_ref=source.at[x],
-                dst_ref=target.at[1 - self.pipe, x],
-                send_sem=sends.at[step],
-                recv_sem=recvs.at[(1 - self.pipe) * 4 + step],
-                device_id={"pipe": 1 - self.pipe, "tensor": x},
-                device_id_type=MESH,
-            )
-            for step in range(4)
-        ]
-        self.local = pltpu.make_async_copy(source.at[x], target.at[self.pipe, x], local)
+
+    def copy(self, step, pipe, device_pipe, block):
+        return pltpu.make_async_remote_copy(
+            src_ref=self.source.at[block],
+            dst_ref=self.target.at[pipe, self.x],
+            send_sem=self.sends.at[step],
+            recv_sem=self.recvs.at[pipe * 4 + step],
+            device_id={"pipe": device_pipe, "tensor": block},
+            device_id_type=MESH,
+        )
+
+    def out(self, step):
+        return self.copy(step, self.pipe, self.layer, (self.x + step) % 4)
+
+    def local(self):
+        return pltpu.make_async_copy(self.source.at[self.x], self.target.at[self.pipe, self.x], self.local_sem)
 
     def start(self):
-        for copy in self.copies[1:]:
-            copy.start()
+        for step in (1, 2, 3):
+            self.out(step).start()
 
         @pl.when(self.here)
         def _():
-            self.local.start()
+            self.local().start()
 
         @pl.when(jnp.logical_not(self.here))
         def _():
-            self.copies[0].start()
+            self.out(0).start()
 
     def wait(self):
-        for copy in self.copies[1:]:
-            copy.wait_send()
+        for step in (1, 2, 3):
+            self.out(step).wait_send()
 
         @pl.when(self.here)
         def _():
-            self.local.wait()
-            for copy in self.copies[1:] + self.arrivals:
-                copy.wait_recv()
+            self.local().wait()
+            for step in (1, 2, 3):
+                self.out(step).wait_recv()
+            for step in range(4):
+                self.copy(step, 1 - self.pipe, 1 - self.pipe, self.x).wait_recv()
 
         @pl.when(jnp.logical_not(self.here))
         def _():
-            self.copies[0].wait_send()
+            self.out(0).wait_send()
 
 
 def both_pipes(x, pipe):
     return [{"pipe": 1 - pipe, "tensor": (x + step) % 4} for step in range(4)]
 
 
-def turn_kernel(inner, lead, part, res, few, errors_later, inverses, grads, few_grad,
-                errors, scales, input_grad, few_total, middle,
-                raw, own, sent, b0, b1, b2, kept, arrived, total, d0, d1, d2,
-                xs, xr, gs, gr, gl, ts, tr, cs, cr, ys, yr, load):
-    z, y, core, x = place()
+class CoreSum:
+    def __init__(self, grads, arrived, sems):
+        _, _, core, _ = place()
+        self.grads, self.arrived, self.core = grads, arrived, core
+        self.pieces = [(y, half) for y in range(4) for half in range(2)]
+        self.sems = sems
+
+    def copy(self, index):
+        y, half = self.pieces[index]
+        source = self.grads.at[half, y, 1 - self.core]
+        return remote(source, self.arrived.at[y, half], self.sems, index, at_core(1 - self.core))
+
+    def start(self):
+        for index in range(8):
+            self.copy(index).start()
+
+    def finish(self):
+        for index, (y, half) in enumerate(self.pieces):
+            self.copy(index).wait_recv()
+            value = self.grads[half, y, self.core].astype(F32) + self.arrived[y, half].astype(F32)
+            self.grads[half, y, self.core] = value.astype(BF16)
+        for index in range(8):
+            self.copy(index).wait_send()
+
+
+def back_through_norm(value, grad_out, summed, gain):
+    scale = norm_scale(value)
+    unit = value * scale
+    scaled = summed * gain
+    mean = jnp.mean(scaled * unit, -1, keepdims=True)
+    return grad_out + scale * (scaled - unit * mean), jnp.sum(summed * unit, 0, keepdims=True)
+
+
+def backward_block(sizes, first_block, e, scales, w, few, selector, collector, saved, states,
+                   part, grad, mixed, few_out, state, later, pad):
+    inner, pair, heads = sizes
+    states_count = pair // 2
+    split = inner + inner + pair
+    conv = inner + pair
     quarter = ROWS // 4
-    reads = [
-        pltpu.make_async_copy(errors_later.at[owned(block, x, quarter)], raw.at[block], load.at[8 + block])
-        for block in range(4)
-    ]
-    for read in reads:
-        read.start()
-    greet(*around(x, at_x, (1, 2, 3)), *around(y, at_y), at_core(1 - core))
-    two = lambda half: pl.ds(2 * half, 2)
-    sums = RingScatter(x, at_x, lambda owner, half: part.at[two(half), owner], (b0, b1, b2), (xs, xr))
-    sums.start()
-    cores = CoreSum(grads, kept, arrived, total, (cs, cr), load)
-    cores.start()
-    cores.finish()
-    y_sums = RingScatter(y, at_y, lambda owner, half: total.at[owner, half], (d0, d1, d2), (ys, yr))
-    y_sums.start()
-    for read in reads:
-        read.wait()
-    gain = norm_gain_of(few, 1, lead)
-    sums.relay()
-    y_sums.relay()
-    sums.wait()
-    gain_grad = jnp.zeros_like(gain)
-    own[...] = jnp.zeros_like(own)
-    for half in range(2):
-        result = sums.result(half)
-        for index in range(2):
-            block = 2 * half + index
-            value, gain_part = back_through_norm(res[1, block], raw[block].astype(F32), result[index], gain)
-            gain_grad = gain_grad + gain_part
-            input_grad[block] = value
-            low = value.astype(BF16)
-            sent[block] = low
-            branch = res[1, block] - res[0, block]
-            dots = jnp.sum(low.astype(F32) * branch, -1, keepdims=True) / inner
-            own[block, 0:1, :] = inverses[0, block, 0:1, :]
-            own[block, 1:2, 0:quarter] = column_to_row(dots)
-    x_ring = RingGather(x, at_x, lambda half: sent.at[two(half)], lambda origin, half: errors.at[two(half), origin], (gs, gr, gl))
-    x_ring.start()
-    tell = Everyone(x, at_x, lambda to: own, lambda me: scales.at[pl.ds(0, 4), me], (ts, tr))
-    tell.start()
-    keep = pltpu.make_async_copy(own, scales.at[pl.ds(0, 4), x], load.at[12])
-    keep.start()
-    add_norm_grad(few_total, few_grad, gain_grad, lead)
-    y_sums.wait()
-    for half in range(2):
-        middle[half] = y_sums.result(half).astype(BF16)
-    y_sums.finish()
-    x_ring.relay()
-    keep.wait()
-    tell.wait()
-    x_ring.wait(2, 3, 4, 5)
-    x_ring.finish()
-    sums.finish()
-
-
-def turn_call(part, res, few, errors, inverses, grads, few_grad, inner):
-    _, blocks, quarter, width = res.shape
-    lead = few.shape[2] - (width - few.shape[2])
-    columns = grads.shape[1]
-    piece = grads.shape[0] // 16
-    owned_rows = (blocks, quarter, width)
-    shape = jax.ShapeDtypeStruct
-    return pl.pallas_call(
-        partial(turn_kernel, inner, lead),
-        out_shape=[
-            shape((blocks, 4, quarter, width), BF16),
-            shape((blocks, 4, 8, LANES), F32),
-            shape(owned_rows, F32),
-            shape(few_grad.shape, F32),
-            shape((2, piece, columns), BF16),
-        ],
-        in_specs=[VMEM, VMEM, VMEM, ANY, VMEM, ANY, VMEM],
-        out_specs=[ANY, ANY, VMEM, VMEM, VMEM],
-        scratch_shapes=[
-            pltpu.VMEM(owned_rows, BF16),
-            pltpu.VMEM((blocks, 8, LANES), F32),
-            pltpu.VMEM(owned_rows, BF16),
-        ]
-        + scatter_buffers(2, quarter, width)
-        + core_buffers(piece, columns)
-        + scatter_buffers(piece, columns)
-        + dma(6) + gather_sems() + dma(3) + dma(8) + dma(6)
-        + [pltpu.SemaphoreType.DMA((13,))],
-        compiler_params=remote_params(3),
-        name="between_gradients",
-    )(part.reshape(blocks, 4, quarter, width), res, few, errors, inverses,
-      grads.reshape(2, 4, 2, piece, columns), few_grad)
-
-
-def final_kernel(sizes, part, res, few, error, errors, grads, middle, few_grad, few_later,
-                 last_out, first_grad, second_grad, large, few_sum, few_shared, state_grad,
-                 low_out, low_grad, b0, b1, b2, kept, arrived, total, d0, d1, d2, e0, e1, e2, z_blocks,
-                 mine, pair, y_few, z_few, x_few, state_parts,
-                 xs, xr, ps, pr, cs, cr, ys, yr, zs, zr, fs, fr, hs, hr, js, jr, ks, kr, ws, wr,
-                 os, og, is_, ig, load):
-    lead, state_at, state_columns = sizes
+    (z_at, p_at, c_at, raw_at, y_at), _ = columns_of(inner, conv)
+
+    @pl.when(first_block)
+    def _():
+        state[...] = jnp.zeros_like(state)
+        later[...] = jnp.zeros_like(later)
+        pad[ROWS : ROWS + 8, :] = jnp.zeros((8, conv), F32)
+
+    @pl.when(jnp.logical_not(first_block))
+    def _():
+        pad[ROWS : ROWS + 8, :] = pad[0:8, :]
+
+    bias = few[5:6, inner : inner + LANES]
+    rate = few[5:6, inner + LANES : inner + 2 * LANES]
+    gain = few[5:6, :inner]
+    skip = few[6:7, :inner]
+    mask = (iota((1, LANES), 1) < heads).astype(F32)
+    first = iota((CHUNK, LANES), 1) < LANES // 2
+    later_in = iota((CHUNK, CHUNK), 1) >= iota((CHUNK, CHUNK), 0)
+    last = iota((CHUNK, LANES), 0) == CHUNK - 1
+    tri = later_in.astype(F32)
+    column = lambda row: jnp.concatenate(
+        [row_to_column(scales[owner, row : row + 1, :])[:quarter] for owner in range(4)], 0
+    )
+    inverse = column(0)
+    inner_dot = column(1)
+    mixed_grad = mm(e, w[:, split + LANES :])
+    for chunk in reversed(range(ROWS // CHUNK)):
+        at = slice(chunk * CHUNK, (chunk + 1) * CHUNK)
+        z = saved[at, z_at]
+        y = saved[at, y_at]
+        sig = sigmoid(z)
+        act = z * sig
+        g = y * act * inverse[at]
+        mixed[at, :] = (g * gain).astype(BF16)
+        mixed_here = mixed_grad[at]
+        gated_grad = inverse[at] * (mixed_here * gain - g * inner_dot[at])
+        dy = gated_grad * act
+        grad[at, :inner] = (gated_grad * y * (sig * (1.0 + z - act))).astype(BF16)
+        c = saved[at, c_at]
+        csig = sigmoid(c)
+        value = c * csig
+        slope = csig * (1.0 + c - value)
+        xs = value[:, :inner]
+        b_low = value[:, inner : inner + states_count].astype(BF16)
+        c_low = value[:, inner + states_count :].astype(BF16)
+        raw = saved[at, raw_at]
+        delta, log_decay = steps(raw, bias, rate, mask)
+        turned = log_decay.T
+        final = log_decay[CHUNK - 1 : CHUNK, :]
+        wide_delta = spread(delta, selector, heads)
+        scaled = wide_delta * xs
+        scaled_low = scaled.astype(BF16)
+        dy_low = dy.astype(BF16)
+        products = jnp.where(later_in, mm(b_low, c_low, ((1,), (1,))), 0.0)
+        dproducts = jnp.zeros((CHUNK, CHUNK), F32)
+        within = []
+        for two in range(heads // 2):
+            lanes = slice(two * LANES, (two + 1) * LANES)
+            parts = []
+            for odd in range(2):
+                h = 2 * two + odd
+                mine = first if odd == 0 else ~first
+                decay = jnp.exp(jnp.minimum(turned[h : h + 1, :] - log_decay[:, h : h + 1], 0.0))
+                parts.append(mm((products * decay).astype(BF16), dy_low[:, lanes]))
+                own = jnp.where(mine, scaled_low[:, lanes], jnp.zeros((), BF16))
+                dproducts = dproducts + decay * mm(own, dy_low[:, lanes], ((1,), (1,)))
+            within.append(jnp.where(first, parts[0], parts[1]))
+        dproducts = jnp.where(later_in, dproducts, 0.0).astype(BF16)
+        old = states[chunk]
+        old_low = old.astype(BF16)
+        dstate = state[...]
+        dstate_low = dstate.astype(BF16)
+        to_end = spread(jnp.exp(final - log_decay) * mask, selector, heads)
+        from_start = (spread(jnp.exp(log_decay) * mask, selector, heads) * dy).astype(BF16)
+        dscaled = jnp.concatenate(within, 1) + to_end * mm(b_low, dstate_low)
+        dc_state = mm(from_start, old_low, ((1,), (1,))) + mm(dproducts, b_low, ((0,), (0,)))
+        db_state = mm((to_end * scaled).astype(BF16), dstate_low, ((1,), (1,))) + mm(dproducts, c_low)
+        carry = jnp.broadcast_to(jnp.sum(later[...] * dstate, 0, keepdims=True), (8, inner))
+        carry = per_head(carry, collector)[0:1]
+        keep = spread(jnp.broadcast_to(jnp.exp(final) * mask, (8, LANES)), selector, heads)[0:1]
+        state[...] = keep * dstate + mm(c_low, from_start, ((0,), (0,)))
+        later[...] = old
+        flow = dy_low.astype(F32) * (y - skip * xs) - scaled_low.astype(F32) * dscaled
+        dlog = per_head(flow, collector) + jnp.where(last, carry, 0.0)
+        dstep = mm_exact(tri, dlog)
+        ddelta = per_head(xs * dscaled, collector) + rate * dstep
+        draw = ddelta * sigmoid(raw + bias) * mask
+        few_out[5:6, inner : inner + LANES] += jnp.sum(draw, 0, keepdims=True)
+        few_out[5:6, inner + LANES : inner + 2 * LANES] += jnp.sum(delta * dstep, 0, keepdims=True)
+        few_out[5:6, :inner] += jnp.sum(mixed_here * g, 0, keepdims=True)
+        few_out[6:7, :inner] += jnp.sum(dy * xs, 0, keepdims=True)
+        dxs = wide_delta * dscaled + skip * dy
+        pad[at, :] = jnp.concatenate([dxs, db_state, dc_state], 1) * slope
+        grad[at, split:] = draw.astype(BF16)
+    for chunk in range(ROWS // CHUNK):
+        at = slice(chunk * CHUNK, (chunk + 1) * CHUNK)
+        p = saved[at, p_at]
+        total = jnp.zeros((CHUNK, conv), F32)
+        for tap in range(4):
+            begin = chunk * CHUNK + 3 - tap
+            shifted = pad[begin : begin + CHUNK, :]
+            total = total + few[tap : tap + 1, :] * shifted
+            few_out[tap : tap + 1, :] += jnp.sum(p * shifted, 0, keepdims=True)
+        few_out[4:5, :] += jnp.sum(pad[at, :], 0, keepdims=True)
+        grad[at, inner:split] = total.astype(BF16)
+    part[...] = mm(grad[...], w[:, : split + LANES], ((1,), (1,))).astype(BF16)
+
+
+def backward_all_kernel(sizes, errors_later, scales_later, weights, few, selector, collector, normed, saved, states,
+                        res, inverses, last_low,
+                        last_out, first_grad, second_grad, large, few_sum, few_shared, state_grad,
+                        errors, scales, w_held, part, relays, sums, arrived, stage, state_stage, norm_stage,
+                        grad, mixed, own_scales, own_grad, low_grad, few_grad, norm_grad, total, low_total,
+                        core1, core0, u0, u1, u2, v0, v1, v2, e0, e1, e2, middle, z_blocks,
+                        pair_few, y_few, z_few, x_few, state_parts, state, later, pad,
+                        rs, rr, gs, gr, ss, sr, c1s, c1r, y1s, y1r, c0s, c0r, y0s, y0r, zs, zr,
+                        ps, pr, fs, fr, hs, hr, js, jr, ks, kr, ws, wr, os, og, is_, ig, loads, load):
+    inner, pair, heads, lead, whole_inner = sizes
+    layer_sizes = (inner, pair, heads)
     z, y, core, x = place()
     pipe = z % 2
     every = (1, 2, 3)
-    for block in range(4):
-        low_out[block] = res[2, block].astype(BF16)
+    quarter = ROWS // 4
+    split = 2 * inner + pair
+
+    def at_step(op):
+        return 1 - op // 4, 3 - op % 4
+
+    def loads_of(op):
+        layer, block = at_step(op)
+        slot = op % 2
+        at = pl.ds(pl.multiple_of(block * ROWS, ROWS), ROWS)
+        count = ROWS // CHUNK
+        return [
+            pltpu.make_async_copy(saved.at[layer, at], stage.at[slot], loads.at[0, slot]),
+            pltpu.make_async_copy(states.at[layer, pl.ds(block * count, count)], state_stage.at[slot], loads.at[1, slot]),
+            pltpu.make_async_copy(normed.at[layer, at], norm_stage.at[slot], loads.at[2, slot]),
+        ]
+
+    def weight_load(layer):
+        return pltpu.make_async_copy(weights.at[layer], w_held.at[layer], load.at[layer])
+
+    error_load = pltpu.make_async_copy(errors_later, errors.at[1], load.at[2])
+    error_load.start()
+    weight_load(1).start()
+    for copy in loads_of(0):
+        copy.start()
+    weight_load(0).start()
     greet(*around(x, at_x, every), *around(y, at_y, every), *around(z, at_z, every), at_core(1 - core),
           *both_pipes(x, pipe))
-    two = lambda half: pl.ds(2 * half, 2)
-    sums = RingScatter(x, at_x, lambda owner, half: part.at[two(half), owner], (b0, b1, b2), (xs, xr))
-    sums.start()
-    cores = CoreSum(grads, kept, arrived, total, (cs, cr), load)
+    output = Deliver(1, last_low, last_out, os, og, load.at[3])
+    output.start()
+    scales[1] = scales_later[...]
+    few_grad[...] = jnp.zeros_like(few_grad)
+    norm_grad[...] = jnp.zeros_like(norm_grad)
+    own_scales[...] = jnp.zeros_like(own_scales)
+    total[...] = jnp.zeros_like(total)
+    error_load.wait()
+    for block in range(4):
+        own_grad[block] = errors[1, owned(block, x, quarter)].astype(F32)
+    weight_load(1).wait()
+
+    def sums_of(op):
+        rows = lambda owner, half: part.at[
+            op % 4, pl.ds(pl.multiple_of(owner * quarter + half * (quarter // 2), quarter // 2), quarter // 2)
+        ]
+        return BlockSums(x, rows, relays, sums, arrived, (rs, rr), op)
+
+    def gather_of(block):
+        place_of = lambda origin, half: errors.at[
+            0, pl.ds(pl.multiple_of(block * ROWS + origin * quarter + half * (quarter // 2), quarter // 2), quarter // 2)
+        ]
+        return RingGather(x, at_x, lambda half: place_of(x, half), place_of, (gs.at[block], gr.at[block]), local=False)
+
+    def scales_of(block):
+        return to_everyone(x, at_x, lambda to: own_scales.at[block], lambda me: scales.at[0, block, me], (ss, sr), block)
+
+    def core_sum(layer):
+        arrived_core, sems = ((core0, (c0s, c0r)), (core1, (c1s, c1r)))[layer]
+        return CoreSum(low_total, arrived_core, sems)
+
+    def y_sum(layer):
+        buffers, sems = (((v0, v1, v2), (y0s, y0r)), ((u0, u1, u2), (y1s, y1r)))[layer]
+        return RingScatter(y, at_y, lambda owner, half: low_total.at[half, owner, core], buffers, sems)
+
+    def finish_sums(op):
+        layer, block = at_step(op)
+        job = sums_of(op)
+        job.wait()
+        gain = jnp.concatenate([few[layer, 6:7, lead:], few[layer, 7:8, :]], 1)
+        value, gain_part = back_through_norm(res[layer, block], own_grad[block], job.result(), gain)
+        own_grad[block] = value
+        norm_grad[layer, 0:1, :] += gain_part
+        low = value.astype(BF16)
+        job.finish()
+
+        @pl.when(layer == 1)
+        def _():
+            errors[0, owned(block, x, quarter)] = low
+            gather_of(block).start()
+            dots = jnp.sum(low.astype(F32) * (res[1, block] - res[0, block]), -1, keepdims=True) / whole_inner
+            own_scales[block, 0:1, :] = inverses[0, block, 0:1, :]
+            own_scales[block, 1:2, 0:quarter] = column_to_row(dots)
+            scales[0, block, x] = own_scales[block]
+            scales_of(block).start()
+
+        @pl.when(layer == 0)
+        def _():
+            low_grad[block] = low
+
+    def flush():
+        piece = total.shape[0] // 16
+        for index in range(16):
+            z_hi, y_at, core_at = index // 8, (index // 2) % 4, index % 2
+            low_total[z_hi, y_at, core_at] = total[index * piece : (index + 1) * piece, :].astype(BF16)
+
+    own_block = errors.at[0, pl.ds(pl.multiple_of(x * ROWS, ROWS), ROWS)]
+    second_copy = pltpu.make_async_copy(own_block, second_grad.at[pipe], load.at[4])
+    swap = remote(own_block, second_grad.at[pipe], (ps, pr), 0, at_pipe(1 - pipe))
+
+    def step(op, carry):
+        layer, block = at_step(op)
+        slot = op % 2
+
+        @pl.when(layer == 0)
+        def _():
+            job = gather_of(block)
+            job.wait(2, 3, 4, 5)
+            job.finish()
+            scales_of(block).wait()
+
+        @pl.when(op == 4)
+        def _():
+            weight_load(0).wait()
+
+        @pl.when(op == 7)
+        def _():
+            second_copy.start()
+            swap.start()
+
+        for copy in loads_of(op):
+            copy.wait()
+
+        @pl.when(op < 7)
+        def _():
+            for copy in loads_of(op + 1):
+                copy.start()
+
+        at = pl.ds(pl.multiple_of(block * ROWS, ROWS), ROWS)
+        e = errors[layer, at]
+        backward_block(layer_sizes, block == 3, e, scales.at[layer, block], w_held.at[layer], few.at[layer],
+                       selector[...], collector[...], stage.at[slot], state_stage.at[slot],
+                       part.at[op % 4], grad, mixed, few_grad.at[layer], state, later, pad)
+        sums_of(op).start()
+
+        @pl.when((op >= 3) & (op < 7))
+        def _():
+            gather_of(6 - op).relay()
+
+        @pl.when(op >= 2)
+        def _():
+            finish_sums(op - 2)
+
+        @pl.when(op >= 1)
+        def _():
+            sums_of(op - 1).relay()
+
+        @pl.when(op == 4)
+        def _():
+            core_sum(1).finish()
+            y_sum(1).start()
+
+        @pl.when(op == 5)
+        def _():
+            y_sum(1).relay()
+
+        @pl.when(op == 6)
+        def _():
+            job = y_sum(1)
+            job.wait()
+            for half in range(2):
+                middle[half] = job.result(half).astype(BF16)
+            job.finish()
+
+        turn = ((0,), (0,))
+        wide = split + LANES
+        for index in range(total.shape[0] // ROWS):
+            rows = slice(index * ROWS, (index + 1) * ROWS)
+            total[rows, :wide] += mm(norm_stage[slot, :, rows], grad[...], turn)
+            total[rows, wide:] += mm(errors[layer, at, rows], mixed[...], turn)
+
+        @pl.when(op == 3)
+        def _():
+            flush()
+            core_sum(1).start()
+            total[...] = jnp.zeros_like(total)
+
+        return carry
+
+    lax.fori_loop(0, 8, step, 0)
+    flush()
+    cores = core_sum(0)
     cores.start()
-    own_block = errors.at[x]
-    keep = pltpu.make_async_copy(own_block, second_grad.at[pipe], load.at[8])
-    keep.start()
-    swap = remote(own_block, second_grad.at[pipe], (ps, pr), 0, at_pipe(1 - pipe))
-    swap.start()
-    output = Deliver(1, low_out, last_out, os, og, load.at[9])
+    finish_sums(6)
+    sums_of(7).relay()
     cores.finish()
-    y_sums = RingScatter(y, at_y, lambda owner, half: total.at[owner, half], (d0, d1, d2), (ys, yr))
+    y_sums = y_sum(0)
     y_sums.start()
-    gain = norm_gain_of(few, 0, lead)
-    sums.relay()
-    output.start()
-    y_sums.relay()
-    sums.wait()
-    gain_grad = jnp.zeros_like(gain)
-    for half in range(2):
-        result = sums.result(half)
-        for index in range(2):
-            block = 2 * half + index
-            value, gain_part = back_through_norm(res[0, block], error[block], result[index], gain)
-            gain_grad = gain_grad + gain_part
-            low_grad[block] = value.astype(BF16)
-    gradient = Deliver(0, low_grad, first_grad, is_, ig, load.at[10])
+    finish_sums(7)
+    gradient = Deliver(0, low_grad, first_grad, is_, ig, load.at[5])
     gradient.start()
-    mine[1] = few_later[...]
-    add_norm_grad(mine.at[0], few_grad, gain_grad, lead)
-    few_core = remote(mine, pair, (fs, fr), 0, at_core(1 - core))
+    for layer in range(2):
+        width = few_grad.shape[2] - lead
+        few_grad[layer, 6:7, lead:] = norm_grad[layer, 0:1, :width]
+        few_grad[layer, 7:8, :] = norm_grad[layer, 0:1, width:]
+    few_core = remote(few_grad, pair_few, (fs, fr), 0, at_core(1 - core))
     few_core.start()
     few_core.wait()
-    mine[...] = mine[...] + pair[...]
-    few_y = Everyone(y, at_y, lambda to: mine, lambda me: y_few.at[me], (hs, hr))
+    y_sums.relay()
+    few_grad[...] = few_grad[...] + pair_few[...]
+    few_y = Everyone(y, at_y, lambda to: few_grad, lambda me: y_few.at[me], (hs, hr))
     few_y.start()
     y_sums.wait()
     rows = z_blocks.shape[2]
@@ -1164,17 +1139,17 @@
         for half in range(2):
             z_blocks[2 * z_hi, half] = first[half * rows : (half + 1) * rows]
             z_blocks[2 * z_hi + 1, half] = second[half * rows : (half + 1) * rows]
-    y_sums.finish()
     z_sums = RingScatter(z, at_z, lambda owner, half: z_blocks.at[owner, half], (e0, e1, e2), (zs, zr))
     z_sums.start()
+    y_sums.finish()
     few_y.wait()
-    y_few[y] = mine[...]
-    mine[...] = (y_few[0] + y_few[1]) + (y_few[2] + y_few[3])
-    few_z = Everyone(z, at_z, lambda to: mine.at[to % 2], lambda me: z_few.at[me], (js, jr))
+    y_few[y] = few_grad[...]
+    few_grad[...] = (y_few[0] + y_few[1]) + (y_few[2] + y_few[3])
+    few_z = Everyone(z, at_z, lambda to: few_grad.at[to % 2], lambda me: z_few.at[me], (js, jr))
     few_z.start()
     z_sums.relay()
     few_z.wait()
-    z_few[z] = mine[pipe]
+    z_few[z] = few_grad[pipe]
     few_sum[...] = (z_few[0] + z_few[1]) + (z_few[2] + z_few[3])
     x_few[x] = few_sum[...]
     few_x = Everyone(x, at_x, lambda to: few_sum, lambda me: x_few.at[me], (ks, kr))
@@ -1182,69 +1157,99 @@
     z_sums.wait()
     for half in range(2):
         large[half * rows : (half + 1) * rows, :] = z_sums.result(half)
-    z_sums.finish()
-    quarter = 2 * rows // 4
+    state_rows = 2 * rows // 4
     for block in range(4):
-        state_parts[0, block] = large[block * quarter : (block + 1) * quarter, state_at : state_at + state_columns]
+        state_parts[0, block] = large[block * state_rows : (block + 1) * state_rows, 2 * inner : split]
     state_x = Everyone(x, at_x, lambda to: state_parts.at[0, to], lambda me: state_parts.at[1, me], (ws, wr))
     state_x.start()
+    z_sums.finish()
     few_x.wait()
     few_shared[...] = (x_few[0] + x_few[1]) + (x_few[2] + x_few[3])
     state_x.wait()
     total_state = state_parts[0, x]
-    for step in every:
-        total_state = total_state + state_parts[1, (x + step) % 4]
+    for step_at in every:
+        total_state = total_state + state_parts[1, (x + step_at) % 4]
     state_grad[...] = total_state
-    keep.wait()
+    second_copy.wait()
     swap.wait()
     output.wait()
     gradient.wait()
-    sums.finish()
-
-
-def final_call(part, res, few, error, errors, grads, middle, few_grad, few_later, sizes):
-    blocks, quarter, width = error.shape
-    wide = few.shape[2]
-    lead = wide - (width - wide)
-    columns = grads.shape[1]
-    piece = grads.shape[0] // 16
-    state_at, state_columns = sizes
-    both = (2,) + few_grad.shape
-    delivered = jax.ShapeDtypeStruct((2, blocks, quarter, width), BF16)
+
+
+def backward_all(errors, scales, weights, few, normed, saved, states, res, inverses, last_low,
+                 inner, pair, heads, whole_inner):
+    length, width = errors.shape
+    _, blocks, quarter, _ = res.shape
+    conv = inner + pair
+    lead = conv - (width - conv)
+    split = 2 * inner + pair
+    columns = weights.shape[2]
+    piece = weights.shape[1] // 16
+    chunks = ROWS // CHUNK
+    selector, collector = constants(inner, heads)
+    shape = jax.ShapeDtypeStruct
+    delivered = shape((2, blocks, quarter, width), BF16)
+    few_shape = few.shape[1:]
+    half = (quarter // 2, width)
+    semaphores = lambda *count: [pltpu.SemaphoreType.DMA(count)] * 2
     return pl.pallas_call(
-        partial(final_kernel, (lead, state_at, state_columns)),
+        partial(backward_all_kernel, (inner, pair, heads, lead, whole_inner)),
         out_shape=[
             delivered,
             delivered,
-            delivered,
-            jax.ShapeDtypeStruct((piece, columns), F32),
-            jax.ShapeDtypeStruct(few_grad.shape, F32),
-            jax.ShapeDtypeStruct(few_grad.shape, F32),
-            jax.ShapeDtypeStruct((piece // 4, state_columns), F32),
+            shape((2, blocks * quarter, width), BF16),
+            shape((piece, columns), F32),
+            shape(few_shape, F32),
+            shape(few_shape, F32),
+            shape((piece // 4, pair), F32),
         ],
-        in_specs=[VMEM, VMEM, VMEM, VMEM, ANY, ANY, VMEM, VMEM, VMEM],
+        in_specs=[ANY, VMEM, ANY, VMEM, VMEM, VMEM, ANY, ANY, ANY, VMEM, VMEM, ANY],
         out_specs=[ANY, ANY, ANY, VMEM, VMEM, VMEM, VMEM],
-        scratch_shapes=[pltpu.VMEM(error.shape, BF16), pltpu.VMEM(error.shape, BF16)]
-        + scatter_buffers(2, quarter, width)
-        + core_buffers(piece, columns)
-        + scatter_buffers(piece, columns)
+        scratch_shapes=[
+            pltpu.VMEM((2, length, width), BF16),
+            pltpu.VMEM((2, blocks, 4, 8, LANES), F32),
+            pltpu.VMEM(weights.shape, BF16),
+            pltpu.VMEM((4, ROWS, width), BF16),
+            pltpu.VMEM((8, 2) + half, BF16),
+            pltpu.VMEM((8, 2) + half, BF16),
+            pltpu.VMEM((8, 2, 2) + half, BF16),
+            pltpu.VMEM((2, ROWS, saved.shape[2]), F32),
+            pltpu.VMEM((2, chunks, pair // 2, inner), F32),
+            pltpu.VMEM((2, ROWS, width), BF16),
+            pltpu.VMEM((ROWS, split + LANES), BF16),
+            pltpu.VMEM((ROWS, inner), BF16),
+            pltpu.VMEM((blocks, 8, LANES), F32),
+            pltpu.VMEM((blocks, quarter, width), F32),
+            pltpu.VMEM((blocks, quarter, width), BF16),
+            pltpu.VMEM((2,) + few_shape, F32),
+            pltpu.VMEM((2, 8, width), F32),
+            pltpu.VMEM((width, columns), F32),
+            pltpu.VMEM((2, 4, 2, piece, columns), BF16),
+            pltpu.VMEM((4, 2, piece, columns), BF16),
+            pltpu.VMEM((4, 2, piece, columns), BF16),
+        ]
+        + scatter_buffers(piece, columns) * 2
         + scatter_buffers(piece // 2, columns)
         + [
+            pltpu.VMEM((2, piece, columns), BF16),
             pltpu.VMEM((4, 2, piece // 2, columns), BF16),
-            pltpu.VMEM(both, F32),
-            pltpu.VMEM(both, F32),
-            pltpu.VMEM((4,) + both, F32),
-            pltpu.VMEM((4,) + few_grad.shape, F32),
-            pltpu.VMEM((4,) + few_grad.shape, F32),
-            pltpu.VMEM((2, 4, piece // 4, state_columns), F32),
+            pltpu.VMEM((2,) + few_shape, F32),
+            pltpu.VMEM((4, 2) + few_shape, F32),
+            pltpu.VMEM((4,) + few_shape, F32),
+            pltpu.VMEM((4,) + few_shape, F32),
+            pltpu.VMEM((2, 4, piece // 4, pair), F32),
+            pltpu.VMEM((pair // 2, inner), F32),
+            pltpu.VMEM((pair // 2, inner), F32),
+            pltpu.VMEM((ROWS + 8, conv), F32),
         ]
-        + dma(6) + dma(1) + dma(8) + dma(6) + dma(6) + dma(1) + dma(3) + dma(3) + dma(3) + dma(3)
+        + semaphores(8, 6) + semaphores(4, 6) + semaphores(4, 3)
+        + dma(8) + dma(6) + dma(8) + dma(6) + dma(6)
+        + dma(1) + dma(1) + dma(3) + dma(3) + dma(3) + dma(3)
         + [pltpu.SemaphoreType.DMA((4,)), pltpu.SemaphoreType.DMA((8,))] * 2
-        + [pltpu.SemaphoreType.DMA((11,))],
-        compiler_params=remote_params(4),
-        name="final_sums",
-    )(part.reshape(blocks, 4, quarter, width), res, few, error, errors,
-      grads.reshape(2, 4, 2, piece, columns), middle, few_grad, few_later)
+        + [pltpu.SemaphoreType.DMA((3, 2)), pltpu.SemaphoreType.DMA((6,))],
+        compiler_params=pltpu.CompilerParams(collective_id=1, has_side_effects=True, vmem_limit_bytes=62 * 2**20),
+        name="backward_layers",
+    )(errors, scales, weights, few, selector, collector, normed, saved, states, res, inverses, last_low)
 
 
 def body(inputs, out_grad, norm_gain, in_gate_x, in_read_write, in_step, conv_main, conv_state,
@@ -1278,24 +1283,13 @@
         ],
         0,
     )
-    few, weights, errors1, normed, saved, states, res, inverses, scales1, firsts = forward_all(
+    few, weights, errors, normed, saved, states, res, inverses, scales, firsts, last_low = forward_all(
         inputs, out_grad, shard, few, inner, pair, heads, whole_inner
     )
     weights = weights.reshape(2, width, -1)
-    part1, grad1, mixed1, few_grad1 = backward_call(
-        1, errors1, scales1, weights, few, saved, states, inner, pair, heads
-    )
-    large1 = weight_call(1, normed, grad1, errors1, mixed1)
-    errors0, scales0, input_grad1, few_grad1, middle = turn_call(
-        part1, res, few, errors1, inverses, large1, few_grad1, whole_inner
-    )
-    rows0 = errors0.reshape(4 * part, width)
-    part0, grad0, mixed0, few_grad0 = backward_call(
-        0, rows0, scales0, weights, few, saved, states, inner, pair, heads
-    )
-    large0 = weight_call(0, normed, grad0, rows0, mixed0)
-    last_out, first_grad, second_grad, large, few_sum, few_shared, state_grad = final_call(
-        part0, res, few, input_grad1, errors0, large0, middle, few_grad0, few_grad1, (2 * inner, pair)
+    last_out, first_grad, second_grad, large, few_sum, few_shared, state_grad = backward_all(
+        errors, scales, weights, few, normed, saved, states, res, inverses, last_low,
+        inner, pair, heads, whole_inner
     )
     by_layer = lambda zero, one: jnp.where(
         first, zero.reshape(1, 2, part, width), one.reshape(1, 2, part, width)

time: 302 us -> 255 us (0.84)
  Pallas kernels: 281 us -> 235 us
    pallas_call x6 -> x1, Pallas kernels: 163 us -> 117 us  [backward_all(): pl.pallas_call(partial(backward_all_kernel, (inner, pair, heads, lead, wh...]
where the time goes in v4:
time: 255 us
  Pallas kernels  235 us (92%)
  local copies, waits for them, and re-layouts  11.2 us (4%)
  other arithmetic  7.72 us (3%)
    pallas_call x1, Pallas kernels, forward_all(): pl.pallas_call(partial(forward_all_kernel, (inner, pair, heads, lead, who...  118 us
    pallas_call x1, Pallas kernels, backward_all(): pl.pallas_call(partial(backward_all_kernel, (inner, pair, heads, lead, wh...  117 us
    unnamed x27, local copies, waits for them, and re-layouts  5.5 us

profile of v4, /device:TPU:0, one launch (start us, length us, event | category | flops | bytes accessed | tf_op | source)
XLA Modules:
  0.0 254.5 jit_solution(14399813770120208901)
XLA Ops:
  0.6 1.2 fusion.8
  1.9 0.8 bitcast_dynamic-update-slice_fusion.1
  2.7 0.8 copy.31
  3.5 0.8 bitcast_dynamic-update-slice_fusion.shard
  4.3 0.0 copy-start.1
  4.3 0.7 broadcast_in_dim.25
  5.0 0.1 reshape.67
  5.1 0.7 maximum_reduce_fusion
  5.8 0.7 copy.48
  6.5 0.7 copy.49
  7.2 0.7 exponential_negate_fusion
  7.9 1.3 fusion.3.few_in
  9.2 0.0 copy-done.1
  9.2 117.9 %forward_layers.1 = (f32[2,8,768]{2,1,0:T(8,128)}, bf16[2,16,64,1920]{3,2,1,0:T(8,128)(2,1)}, bf16[1024,1024]{1,0:T(8,128)(2,1)}, bf16[2,1024,1024]{2,1,0:T(8,12...) custom-call(bf16[2,2,128,1024]{3,2,1,0:T(8,128)(2,1)} %bitcast.52, ...), custom_call_target="tpu_custom_call" | custom-call | tf_op jit(solution)/shard_map/forward_layers/pallas_call | solution.py:663
  127.1 0.0 copy-start
  127.1 116.9 %backward_layers.1 = (bf16[2,4,64,1024]{3,2,1,0:T(8,128)(2,1)}, bf16[2,4,64,1024]{3,2,1,0:T(8,128)(2,1)}, bf16[2,256,1024]{2,1,0:T(8,128)(2,1)}, f32[64,1920]{1,...) custom-call(bf16[1024,1024]{1,0:T(8,128)(2,1)} %get-tuple-element.32.errors_later, ...), custom_call_target="tpu_custom_call" | custom-call | tf_op jit(solution)/shard_map/backward_layers/pallas_call | solution.py:1195
  244.0 0.0 copy-done
  244.1 0.0 copy-start.2
  244.1 0.0 copy-start.3
  244.1 0.0 copy-start.5
  244.1 0.0 copy-start.6
  244.1 0.0 copy-start.4
  244.1 3.9 %bitcast_convert_fusion = (f32[1,2,256,1024]{3,2,1,0:T(8,128)}, f32[1,2,256,1024]{3,2,1,0:T(8,128)}) fusion(bf16[2,256,1024]{2,1,0:T(8,128)(2,1)} %get-tuple-element.44, bf16[2,4,64,1024]{3,2,1,0:T(8,128)(2,1)} %get-tuple-element.43, pred[]{:T(512)S(6)} %eq.3, bf16[2,256,1024]{2,1,0:T(8,128)(2,1)S(1)} %copy-done, bf16[2,4,64,1024]{3,2,1,0:T(8,128)(2,1)} %get-tuple-element.42), kind=kLoop, calls=%fused_computation | loop fusion | flops 2097152 | bytes 8388609 | tf_op jit(solution)/shard_map/convert_element_type | solution.py:1296
  248.0 0.0 copy-done.2
  248.0 0.9 reshape.73
  248.9 0.7 slice_bitcast_fusion
  249.6 0.7 copy.32
  250.3 0.0 copy-done.3
  250.3 0.6 copy.33
  250.9 0.0 copy-done.5
  250.9 0.6 slice.52
  251.5 0.6 copy.34
  252.1 0.6 fusion.9
  252.7 0.1 reshape_squeeze.3
  252.8 0.6 reduce_sum.11
  253.4 0.0 copy-done.6
  253.4 0.5 slice_multiply_fusion
  253.9 0.0 copy-done.4
  253.9 0.6 copy.55
  (10 shorter events, 0.1 us)
Async XLA Ops:
  4.3 4.9 %copy-start.1 = (bf16[64,1920]{1,0:T(8,128)(2,1)}, bf16[64,1920]{1,0:T(8,128)(2,1)S(1)}, u32[]{:S(2)}) copy-start(bf16[64,1920]{1,0:T(8,128)(2,1)S(1)} %bitcast_dynamic-update-slice_fusion.shard) | copy-start | bytes 737284
  127.1 117.0 %copy-start = (bf16[2,256,1024]{2,1,0:T(8,128)(2,1)S(1)}, bf16[2,256,1024]{2,1,0:T(8,128)(2,1)}, u32[]{:S(2)}) copy-start(bf16[2,256,1024]{2,1,0:T(8,128)(2,1)} %get-tuple-element.31) | copy-start | bytes 3145732
  244.1 3.9 %copy-start.2 = (f32[64,1920]{1,0:T(8,128)S(1)}, f32[64,1920]{1,0:T(8,128)}, u32[]{:S(2)}) copy-start(f32[64,1920]{1,0:T(8,128)} %get-tuple-element.46) | copy-start | bytes 1474564
  244.1 6.2 %copy-start.3 = (f32[8,768]{1,0:T(8,128)S(1)}, f32[8,768]{1,0:T(8,128)}, u32[]{:S(2)}) copy-start(f32[8,768]{1,0:T(8,128)} %get-tuple-element.48) | copy-start | bytes 73732
  244.1 6.8 %copy-start.5 = (f32[8,768]{1,0:T(8,128)S(1)}, f32[8,768]{1,0:T(8,128)}, u32[]{:S(2)}) copy-start(f32[8,768]{1,0:T(8,128)} %get-tuple-element.45) | copy-start | bytes 73732
  244.1 9.3 %copy-start.6 = (f32[1,8]{1,0:T(1,128)S(1)}, f32[1,8]{1,0:T(1,128)}, u32[]{:S(2)}) copy-start(f32[1,8]{1,0:T(1,128)} %param.25) | copy-start | bytes 100
  244.1 9.8 %copy-start.4 = (f32[16,256]{1,0:T(8,128)S(1)}, f32[16,256]{1,0:T(8,128)}, u32[]{:S(2)}) copy-start(f32[16,256]{1,0:T(8,128)} %get-tuple-element.47) | copy-start | bytes 49156

commit v5 on v4

--- a/solution.py
+++ b/solution.py
@@ -153,10 +153,13 @@
         ]
 
     def start(self):
-        for copy in self.copies[:4]:
+        for copy in self.copies[:4] + self.local:
             copy.start()
-        for copy in self.local:
-            copy.start()
+
+    def start_half(self, half):
+        for index in ((0, 3), (1, 2))[half]:
+            self.copies[index].start()
+        self.local[half].start()
 
     def relay(self):
         for index in range(2):
@@ -167,18 +170,25 @@
         for index in indices:
             self.copies[index].wait_recv()
 
-    def finish(self):
+    def wait_local(self):
         for copy in self.local:
             copy.wait()
+
+    def wait_sends(self):
         for copy in self.copies:
             copy.wait_send()
 
+    def finish(self):
+        self.wait_local()
+        self.wait_sends()
+
 
 class RingScatter:
-    def __init__(self, me, device, piece, buffers, sems):
+    def __init__(self, me, device, piece, buffers, sems, near=None):
         self.me, self.right, self.left = me, (me + 1) % 4, (me + 3) % 4
         across = (me + 2) % 4
-        self.piece, self.buffers = piece, buffers
+        self.buffers = buffers
+        self.near = near or [piece(me, 0), piece(me, 1), piece(self.right, 0), piece(self.left, 1)]
         relays, sums, arrived = buffers
         to_right, to_left = device(self.right), device(self.left)
         self.copies = [
@@ -196,9 +206,9 @@
 
     def relay(self):
         relays, sums, _ = self.buffers
-        for half, block in ((0, self.right), (1, self.left)):
+        for half in range(2):
             self.copies[half].wait_recv()
-            total = relays[half].astype(F32) + self.piece(block, half)[...].astype(F32)
+            total = relays[half].astype(F32) + self.near[2 + half][...].astype(F32)
             sums[half] = total.astype(sums.dtype)
             self.copies[4 + half].start()
 
@@ -208,7 +218,7 @@
 
     def result(self, half):
         arrived = self.buffers[2]
-        mine = self.piece(self.me, half)[...].astype(F32)
+        mine = self.near[half][...].astype(F32)
         return mine + arrived[0, half].astype(F32) + arrived[1, half].astype(F32)
 
     def finish(self):
@@ -274,8 +284,8 @@
             remote(piece(across, 1), relays.at[op, 1], at_op, 1, to_left),
             remote(piece(self.right, 1), arrived.at[op, 0, 1], at_op, 2, to_right),
             remote(piece(self.left, 0), arrived.at[op, 1, 0], at_op, 3, to_left),
-            remote(sums.at[op, 0], arrived.at[op, 0, 0], at_op, 4, to_right),
-            remote(sums.at[op, 1], arrived.at[op, 1, 1], at_op, 5, to_left),
+            remote(sums.at[op % 2, 0], arrived.at[op, 0, 0], at_op, 4, to_right),
+            remote(sums.at[op % 2, 1], arrived.at[op, 1, 1], at_op, 5, to_left),
         ]
         self.op = op
 
@@ -287,7 +297,7 @@
         for half, block in ((0, self.right), (1, self.left)):
             self.copies[half].wait_recv()
             total = self.relays[self.op, half].astype(F32) + self.piece(block, half)[...].astype(F32)
-            self.sums[self.op, half] = total.astype(BF16)
+            self.sums[self.op % 2, half] = total.astype(BF16)
             self.copies[4 + half].start()
 
     def wait(self):
@@ -316,16 +326,17 @@
 
 
 def columns_of(inner, conv):
-    ends = np.cumsum([0, inner, conv, conv, LANES, inner])
+    ends = np.cumsum([0, inner, conv, LANES, inner])
     return [slice(int(begin), int(end)) for begin, end in zip(ends[:-1], ends[1:])], int(ends[-1])
 
 
-def forward_block(sizes, first_block, rows, w, few, selector, save, states, part, squares, state, pad):
+def forward_block(sizes, first_block, last_layer, rows, e, w_in, w_out, few, selector, save, save_p, states, part,
+                  squares, mixed, state, pad, serve):
     inner, pair, heads = sizes
     states_count = pair // 2
     split = inner + inner + pair
     conv = inner + pair
-    (z_at, p_at, c_at, raw_at, y_at), _ = columns_of(inner, conv)
+    (z_at, c_at, raw_at, y_at), _ = columns_of(inner, conv)
 
     @pl.when(first_block)
     def _():
@@ -336,9 +347,9 @@
     def _():
         pad[0:8, :] = pad[ROWS : ROWS + 8, :]
 
-    projected = mm(rows, w[:, : split + LANES])
+    projected = mm(rows, w_in)
     save[:, z_at] = projected[:, :inner]
-    save[:, p_at] = projected[:, inner:split]
+    save_p[...] = projected[:, inner:split].astype(BF16)
     pad[8 : ROWS + 8, :] = projected[:, inner:split]
     save[:, raw_at] = projected[:, split:]
     bias = few[5:6, inner : inner + LANES]
@@ -388,93 +399,182 @@
         for piece in range(CHUNK // owner_rows):
             row = column_to_row(total[piece * owner_rows : (piece + 1) * owner_rows])
             squares[chunk * (CHUNK // owner_rows) + piece, 0:1, 0:owner_rows] = row
-        mixed = (gated * gain).astype(BF16)
-        part[at, :] = mm(mixed, w[:, split + LANES :], ((1,), (1,))).astype(BF16)
-
-
-def forward_all_kernel(sizes, inputs, out_grad, shard, few_in, selector,
-                       few_both, weights, errors, normed, saved, states, res, inverses, scales, firsts, last_low,
-                       hidden, w_held, part, relays, sums, arrived, squares, others, stage, state_stage, norm_stage,
-                       error_rows, own_scales, state, pad, spread_weights, few,
+        mixed[at, :] = (gated * gain).astype(BF16)
+        if chunk == 0:
+            serve()
+    part[...] = mm(mixed[...], w_out(), ((1,), (1,))).astype(BF16)
+
+    @pl.when(last_layer)
+    def _():
+        total = jnp.sum(mm(e[...], w_out()) * mixed[...].astype(F32), 1, keepdims=True)
+        for piece in range(4):
+            squares[piece, 1:2, 0:owner_rows] = column_to_row(total[piece * owner_rows : (piece + 1) * owner_rows])
+
+
+class HandedRing:
+    def __init__(self, me, device, source, slot, sems, core_sems):
+        _, _, core, _ = place()
+        self.slot = lambda origin, half: slot(origin, half, core)
+        self.ring = RingGather(me, device, source, self.slot, sems)
+        self.pieces = [(source(half), self.slot(me, half), 6 + half) for half in range(2)]
+        for index in range(6):
+            held = self.slot(*self.ring.origins[index])
+            self.pieces.append((held, held, index))
+        self.core_sems, self.device = core_sems, at_core(1 - core)
+
+    def hand(self, at):
+        source, target, index = self.pieces[at]
+        return remote(source, target, self.core_sems, index, self.device)
+
+    def start_half(self, half):
+        self.ring.start_half(half)
+        self.hand(half).start()
+
+    def start(self):
+        for half in range(2):
+            self.start_half(half)
+
+    def relay(self):
+        self.ring.relay()
+        for index in range(2):
+            self.hand(2 + index).start()
+
+    def finish(self):
+        for index in range(2, 6):
+            self.ring.wait(index)
+            self.hand(2 + index).start()
+        self.ring.finish()
+        for at in range(8):
+            self.hand(at).wait()
+
+
+def gather_parameters(sizes, few, shard, gate_x, read_write, step, main, of_state, bias, log_rate, skip, gate, norm):
+    inner, pair, heads, lead = sizes
+    width = inner // heads
+    few[...] = jnp.zeros_like(few)
+    for tap in range(5):
+        few[tap : tap + 1, :inner] = main[tap]
+        few[tap : tap + 1, inner:] = of_state[tap]
+    few[5:6, :inner] = gate[...]
+    few[5:6, inner : inner + heads] = bias[...]
+    few[5:6, inner + LANES : inner + LANES + heads] = -jnp.exp(log_rate[...])
+    for head in range(heads):
+        few[6:7, head * width : (head + 1) * width] = jnp.broadcast_to(skip[0:1, head : head + 1], (1, width))
+    first = few.shape[1] - lead
+    few[6:7, lead:] = norm[:, :first]
+    few[7:8, :] = norm[:, first:]
+    split = 2 * inner + pair
+    both = gate_x[...]
+    for index in range(2):
+        shard[:, index * inner : (index + 1) * inner] = both[:, index, :]
+    shard[:, 2 * inner : split] = read_write[0]
+    same = (iota((heads, LANES), 0) == iota((heads, LANES), 1)).astype(BF16)
+    shard[:, split:] = mm(step[0], same, ((0,), (0,))).astype(BF16)
+
+
+def forward_all_kernel(sizes, inputs, out_grad, shard_out, gate_x, read_write, step_in, main, of_state, bias, log_rate,
+                       skip, gate, norm, selector,
+                       few_both, weights_in, weights_out, errors_out, normed, saved, saved_p, states, res, inverses, scales,
+                       firsts, last_part,
+                       hidden, w_in, w_out, errors, part, relays, sums, arrived, squares, others, stage, p_stage, state_stage,
+                       norm_stage, mixed, state, pad, shard_in, z_weights, y_weights, few,
                        xs, xr, xl, es, er, el, zs, zr, zl, ys, yr, yl, cs, cr, y1s, y1r, y1l, c1s, c1r,
-                       fs, fr, rs, rr, gs, gr, gl, qs, qr, ss, sr, ps, pr, outs, load):
+                       bs, br, bl, os, og, ol, c2s, c2r, fs, fr, rs, rr, gs, gr, qs, qr, outs, load):
     inner, pair, heads, lead, whole_inner = sizes
     layer_sizes = (inner, pair, heads)
     z, y, core, x = place()
     pipe = z % 2
     quarter = ROWS // 4
-    few[pipe] = few_in[...]
+    gather_parameters((inner, pair, heads, lead), few.at[pipe], shard_in, gate_x, read_write, step_in, main, of_state,
+                      bias, log_rate, skip, gate, norm)
     squares[...] = jnp.zeros_like(squares)
     greet(*around(x, at_x, (1, 2, 3)), *around(y, at_y), *around(z, at_z), at_core(1 - core), at_pipe(1 - pipe))
     few_swap = remote(few.at[pipe], few.at[pipe], (fs, fr), 0, at_pipe(1 - pipe))
     few_swap.start()
-    piece = spread_weights.shape[1]
-    shard_rows = lambda half: pl.ds(half * (piece // 2), piece // 2)
-    z_slot = lambda origin, half: spread_weights.at[(origin % 2) * 2 + origin // 2, shard_rows(half)]
-    z_ring = RingGather(z, at_z, lambda half: shard.at[shard_rows(half)], z_slot, (zs, zr, zl))
+    piece = shard_in.shape[0]
+    by_half = lambda half: pl.ds(half * (piece // 2), piece // 2)
+    z_ring = RingGather(z, at_z, lambda half: shard_in.at[by_half(half)],
+                        lambda origin, half: z_weights.at[origin, by_half(half)], (zs, zr, zl))
     z_ring.start()
+    y_ring = RingGather(y, at_y, lambda half: shard_out.at[by_half(half)],
+                        lambda origin, half: y_weights.at[origin, by_half(half)], (bs, br, bl))
+    y_ring.start()
     block_rows = lambda origin, half: pl.ds(pl.multiple_of(origin * ROWS + half * (ROWS // 2), ROWS // 2), ROWS // 2)
     x_ring = RingGather(x, at_x, lambda half: inputs.at[pipe, half],
                         lambda origin, half: hidden.at[0, block_rows(origin, half)], (xs, xr, xl))
     x_ring.start()
     e_ring = RingGather(x, at_x, lambda half: out_grad.at[pipe, half],
                         lambda origin, half: errors.at[block_rows(origin, half)], (es, er, el))
-    weight_rings = []
-    for layer, sems, core_sems in ((0, (ys, yr, yl), (cs, cr)), (1, (y1s, y1r, y1l), (c1s, c1r))):
-        weight_rings.append(
-            WeightRows(
-                lambda half, layer=layer: spread_weights.at[2 * layer + half],
-                lambda origin, half, core, layer=layer: weights.at[layer, (half * 4 + origin) * 2 + core],
-                sems,
-                core_sems,
-            )
+
+    def in_ring(layer, sems, core_sems):
+        away = pipe * (1 - layer) + (1 - pipe) * layer
+        from_z = lambda half: (z + 3 * away + 2 * half) % 4
+        return HandedRing(
+            y, at_y, lambda half: z_weights.at[from_z(half)],
+            lambda origin, half, core: w_in.at[layer, from_z(half) // 2, origin, core], sems, core_sems,
         )
+
+    rings = [in_ring(0, (ys, yr, yl), (cs, cr)), in_ring(1, (y1s, y1r, y1l), (c1s, c1r))]
+    out_ring = HandedRing(
+        z, at_z, lambda half: y_weights.at[pl.ds(2 * half, 2)],
+        lambda origin, half, core: w_out.at[origin % 2, origin // 2, pl.ds(2 * half, 2), core],
+        (os, og, ol), (c2s, c2r),
+    )
+    z_ring.wait_local()
+
+    @pl.when(pipe == 0)
+    def _():
+        rings[0].start_half(0)
+
+    y_ring.relay()
     z_ring.relay()
-    z_ring.wait(2, 3, 4, 5)
-    z_ring.finish()
-    weight_rings[0].start()
+    z_ring.wait(2)
+
+    @pl.when(pipe == 1)
+    def _():
+        rings[0].start_half(0)
+
+    z_ring.wait(3)
+
+    @pl.when(pipe == 1)
+    def _():
+        rings[0].start_half(1)
+
+    y_ring.wait(2, 3, 4, 5)
+    y_ring.wait_local()
+    out_ring.start()
+    z_ring.wait(4, 5)
+
+    @pl.when(pipe == 0)
+    def _():
+        rings[0].start_half(1)
+
     x_ring.relay()
     e_ring.start()
-    weight_rings[0].relay()
+    out_ring.relay()
+    rings[0].relay()
+    z_ring.wait_sends()
+    y_ring.wait_sends()
     few_swap.wait()
     few_both[...] = few[...]
     x_ring.wait(2, 3, 4, 5)
     x_ring.finish()
     for block in range(4):
         res[0, block] = hidden[0, owned(block, x, quarter)].astype(F32)
-    weight_rings[0].finish()
-    weight_rings[1].start()
-    w_loads = [
-        [
-            pltpu.make_async_copy(
-                weights.at[layer, index],
-                w_held.at[layer, pl.ds(index * piece, piece)],
-                load.at[layer * 16 + index],
-            )
-            for index in range(16)
-        ]
-        for layer in range(2)
-    ]
-    for copy in w_loads[0]:
-        copy.start()
-    for copy in w_loads[0]:
-        copy.wait()
-
+    rings[0].finish()
+    rings[1].start()
     def sums_of(op):
         rows = lambda owner, half: part.at[op, pl.ds(pl.multiple_of(owner * quarter + half * (quarter // 2), quarter // 2), quarter // 2)]
         return BlockSums(x, rows, relays, sums, arrived, (rs, rr), op)
 
     def squares_of(op):
-        return to_everyone(x, at_x, lambda to: squares.at[op, to], lambda me: others.at[op, me], (qs, qr), op)
+        return to_everyone(x, at_x, lambda to: squares.at[op], lambda me: others.at[op, me], (qs, qr), op)
 
     def gather_of(block):
         place_of = lambda origin, half: hidden.at[
             1, pl.ds(pl.multiple_of(block * ROWS + origin * quarter + half * (quarter // 2), quarter // 2), quarter // 2)
         ]
-        return RingGather(x, at_x, lambda half: place_of(x, half), place_of, (gs.at[block], gr.at[block], gl), local=False)
-
-    def scales_of(block):
-        return to_everyone(x, at_x, lambda to: own_scales.at[block], lambda me: scales.at[block, me], (ss, sr), block)
+        return RingGather(x, at_x, lambda half: place_of(x, half), place_of, (gs.at[block], gr.at[block]), local=False)
 
     def outs_of(op):
         layer, block = op // 4, op % 4
@@ -485,173 +585,142 @@
             pltpu.make_async_copy(stage.at[slot], saved.at[layer, at], outs.at[0, slot]),
             pltpu.make_async_copy(state_stage.at[slot], states.at[layer, pl.ds(block * count, count)], outs.at[1, slot]),
             pltpu.make_async_copy(norm_stage.at[slot], normed.at[layer, at], outs.at[2, slot]),
+            pltpu.make_async_copy(p_stage.at[slot], saved_p.at[layer, at], outs.at[3, slot]),
         ]
 
-    def finish_sums(op):
-        layer, block = op // 4, op % 4
-        job = sums_of(op)
-        squares_of(op).wait()
-        total = squares[op, x, 0:1, :]
-        for step in (1, 2, 3):
-            total = total + others[op, (x + step) % 4, 0:1, :]
-        inverse = lax.rsqrt(total / whole_inner + EPS)
-        inverses[layer, block] = jnp.broadcast_to(inverse, (8, LANES))
+    def row_sums(op, owner):
+        total = others[op, 0, owner, 0:2, :]
+        for device in (1, 2, 3):
+            total = total + others[op, device, owner, 0:2, :]
+        return lax.rsqrt(total[0:1] / whole_inner + EPS), total[1:2]
+
+    def finish_sums(block):
+        job = sums_of(block)
+        squares_of(block).wait()
+        others[block, x] = squares[block]
+        inverse, _ = row_sums(block, x)
+        inverses[block] = jnp.broadcast_to(inverse, (8, LANES))
         column = row_to_column(inverse)[:quarter]
         job.wait()
-        branch = column * job.result()
-        value = res[layer, block] + branch
+        value = res[0, block] + column * job.result()
         job.finish()
-
-        @pl.when(layer == 0)
-        def _():
-            res[1, block] = value
-            hidden[1, owned(block, x, quarter)] = value.astype(BF16)
-            gather_of(block).start()
-
-        @pl.when(layer == 1)
-        def _():
-            last_low[block] = value.astype(BF16)
-            dots = jnp.sum(error_rows[block].astype(F32) * branch, -1, keepdims=True) / whole_inner
-            own_scales[block] = jnp.zeros((8, LANES), F32)
-            own_scales[block, 0:1, :] = inverse
-            own_scales[block, 1:2, 0:quarter] = column_to_row(dots)
-            scales_of(block).start()
-
-    error_loads = [
-        pltpu.make_async_copy(errors.at[owned(block, x, quarter)], error_rows.at[block], load.at[32 + block])
-        for block in range(4)
+        res[1, block] = value
+        hidden[1, owned(block, x, quarter)] = value.astype(BF16)
+        gather_of(block).start()
+
+    def finish_scales(block):
+        squares_of(4 + block).wait()
+        others[4 + block, x] = squares[4 + block]
+        for owner in range(4):
+            inverse, dots = row_sums(4 + block, owner)
+            scales[block, owner, 0:1, :] = inverse
+            scales[block, owner, 1:2, :] = dots * inverse / whole_inner
+
+    own_block = hidden.at[1, pl.ds(pl.multiple_of(x * ROWS, ROWS), ROWS)]
+    ends = [
+        pltpu.make_async_copy(w_in.at[0], weights_in.at[0], load.at[0]),
+        pltpu.make_async_copy(w_in.at[1], weights_in.at[1], load.at[1]),
+        pltpu.make_async_copy(w_out, weights_out, load.at[2]),
+        pltpu.make_async_copy(errors, errors_out, load.at[3]),
+        pltpu.make_async_copy(own_block, firsts, load.at[4]),
     ]
-    own_block = hidden.at[1, pl.ds(pl.multiple_of(x * ROWS, ROWS), ROWS)]
-    first_copy = pltpu.make_async_copy(own_block, firsts.at[pipe], load.at[36])
-    swap = remote(own_block, firsts.at[pipe], (ps, pr), 0, at_pipe(1 - pipe))
+
+    def part_copy(block):
+        at = pl.ds(pl.multiple_of(block * ROWS, ROWS), ROWS)
+        return pltpu.make_async_copy(part.at[4 + block], last_part.at[at], load.at[5 + block])
 
     def step(op, carry):
         layer, block = op // 4, op % 4
 
-        @pl.when(op < 8)
-        def _():
-            @pl.when(layer == 1)
+        @pl.when(layer == 1)
+        def _():
+            job = gather_of(block)
+            job.wait(2, 3, 4, 5)
+            job.finish()
+
+        @pl.when(op == 7)
+        def _():
+            ends[4].start()
+
+        @pl.when(op >= 2)
+        def _():
+            for copy in outs_of(op - 2):
+                copy.wait()
+
+        def serve():
+            @pl.when(op == 0)
             def _():
-                job = gather_of(block)
-                job.wait(2, 3, 4, 5)
-                job.finish()
-
-            @pl.when(op == 7)
+                out_ring.finish()
+
+            @pl.when(op == 1)
             def _():
-                first_copy.start()
-                swap.start()
-
-            @pl.when(op >= 2)
+                e_ring.relay()
+                rings[1].relay()
+
+            @pl.when((op >= 1) & (op < 5))
             def _():
-                for copy in outs_of(op - 2):
-                    copy.wait()
-
-            slot = op % 2
-            at = pl.ds(pl.multiple_of(block * ROWS, ROWS), ROWS)
-            value = hidden[layer, at].astype(F32)
-            gain = jnp.concatenate([few[layer, 6:7, lead:], few[layer, 7:8, :]], 1)
-            norm_stage[slot] = (value * norm_scale(value) * gain).astype(BF16)
-            forward_block(layer_sizes, block == 0, norm_stage[slot], w_held.at[layer], few.at[layer], selector[...],
-                          stage.at[slot], state_stage.at[slot], part.at[op], squares.at[op], state, pad)
-            for copy in outs_of(op):
-                copy.start()
-
-        @pl.when(op == 0)
-        def _():
-            e_ring.relay()
-
-        @pl.when(op == 1)
-        def _():
-            weight_rings[1].relay()
-
-        @pl.when(op == 2)
-        def _():
-            e_ring.wait(2, 3, 4, 5)
-            e_ring.finish()
-            for copy in error_loads:
-                copy.start()
-
-        @pl.when(op == 3)
-        def _():
-            weight_rings[1].finish()
-            for copy in w_loads[1]:
-                copy.start()
-            for copy in error_loads:
-                copy.wait()
-
-        @pl.when((op >= 3) & (op < 7))
-        def _():
-            gather_of(op - 3).relay()
-
-        @pl.when(op >= 2)
-        def _():
-            finish_sums(op - 2)
-
-        @pl.when((op >= 1) & (op < 9))
-        def _():
-            sums_of(op - 1).relay()
-
-        @pl.when(op < 8)
+                sums_of(op - 1).relay()
+
+            @pl.when((op >= 2) & (op < 6))
+            def _():
+                gather_of(op - 2).relay()
+
+            @pl.when(op == 3)
+            def _():
+                e_ring.wait(2, 3, 4, 5)
+                e_ring.finish()
+                rings[1].finish()
+                for copy in ends[:4]:
+                    copy.start()
+
+            @pl.when(op >= 5)
+            def _():
+                finish_scales(op - 5)
+
+        slot = op % 2
+        at = pl.ds(pl.multiple_of(block * ROWS, ROWS), ROWS)
+        value = hidden[layer, at].astype(F32)
+        gain = jnp.concatenate([few[layer, 6:7, lead:], few[layer, 7:8, :]], 1)
+        norm_stage[slot] = (value * norm_scale(value) * gain).astype(BF16)
+        width = value.shape[1]
+        forward_block(layer_sizes, block == 0, layer == 1, norm_stage[slot], errors.at[at],
+                      w_in[layer].reshape(width, -1), lambda: w_out[layer].reshape(width, -1), few.at[layer], selector[...],
+                      stage.at[slot], p_stage.at[slot], state_stage.at[slot], part.at[op], squares.at[op], mixed, state, pad, serve)
+        for copy in outs_of(op):
+            copy.start()
+        squares_of(op).start()
+
+        @pl.when(op < 4)
         def _():
             sums_of(op).start()
-            squares_of(op).start()
-
-        @pl.when(op == 3)
-        def _():
-            for copy in w_loads[1]:
-                copy.wait()
+
+        @pl.when(op >= 4)
+        def _():
+            part_copy(op - 4).start()
+
+        @pl.when((op >= 1) & (op < 5))
+        def _():
+            finish_sums(op - 1)
 
         return carry
 
-    lax.fori_loop(0, 10, step, 0)
+    lax.fori_loop(0, 8, step, 0)
+    finish_scales(3)
     for op in (6, 7):
         for copy in outs_of(op):
             copy.wait()
-    keep = [pltpu.make_async_copy(own_scales.at[block], scales.at[block, x], load.at[37 + block]) for block in range(4)]
-    for copy in keep:
-        copy.start()
+    for copy in ends:
+        copy.wait()
     for block in range(4):
-        scales_of(block).wait()
-    for copy in keep:
-        copy.wait()
-    first_copy.wait()
-    swap.wait()
-
-
-class WeightRows:
-    def __init__(self, source, slot, sems, core_sems):
-        _, y, core, _ = place()
-        self.core_sems, self.device = core_sems, at_core(1 - core)
-        self.slot = lambda origin, half: slot(origin, half, core)
-        self.ring = RingGather(y, at_y, source, self.slot, sems)
-        self.hand = [remote(source(half), self.slot(y, half), core_sems, 6 + half, self.device) for half in range(2)]
-        for index in range(6):
-            held = self.slot(*self.ring.origins[index])
-            self.hand.append(remote(held, held, core_sems, index, self.device))
-
-    def start(self):
-        self.ring.start()
-        for copy in self.hand[:2]:
-            copy.start()
-
-    def relay(self):
-        self.ring.relay()
-        for index in range(2):
-            self.hand[2 + index].start()
-
-    def finish(self):
-        for index in range(2, 6):
-            self.ring.wait(index)
-            self.hand[2 + index].start()
-        self.ring.finish()
-        for copy in self.hand:
-            copy.wait()
-
-
-def forward_all(inputs, out_grad, shard, few, inner, pair, heads, whole_inner):
+        part_copy(block).wait()
+
+
+def forward_all(inputs, out_grad, shard_out, gate_x, read_write, step, main, of_state, bias, log_rate, skip, gate, norm,
+                inner, pair, heads, whole_inner):
     _, part, width = inputs.shape
-    rows, columns = shard.shape
+    rows = shard_out.shape[0]
     conv = inner + pair
+    columns = inner + conv + LANES
     lead = conv - (width - conv)
     length = 4 * part
     _, saved_columns = columns_of(inner, conv)
@@ -660,55 +729,62 @@
     selector, _ = constants(inner, heads)
     half = (2, 2, part // 2, width)
     shape = jax.ShapeDtypeStruct
+    w_in = (2, 2, 4, 2, rows, columns)
+    w_out = (2, 2, 4, 2, rows, inner)
+    semaphores = lambda *count: [pltpu.SemaphoreType.DMA(count)] * 2
     return pl.pallas_call(
         partial(forward_all_kernel, (inner, pair, heads, lead, whole_inner)),
         out_shape=[
-            shape((2,) + few.shape, F32),
-            shape((2, 16, rows, columns), BF16),
+            shape((2, 8, conv), F32),
+            shape(w_in, BF16),
+            shape(w_out, BF16),
             shape((length, width), BF16),
             shape((2, length, width), BF16),
             shape((2, length, saved_columns), F32),
+            shape((2, length, conv), BF16),
             shape((2, length // CHUNK, pair // 2, inner), F32),
             shape((2, 4, quarter, width), F32),
-            shape((2, 4, 8, LANES), F32),
+            shape((4, 8, LANES), F32),
             shape((4, 4, 8, LANES), F32),
-            shape((2, part, width), BF16),
-            shape((4, quarter, width), BF16),
+            shape((part, width), BF16),
+            shape((length, width), BF16),
         ],
-        in_specs=[ANY, ANY, ANY, VMEM, VMEM],
-        out_specs=[VMEM, ANY, ANY, ANY, ANY, ANY, VMEM, VMEM, ANY, ANY, VMEM],
+        in_specs=[ANY, ANY, ANY] + [VMEM] * 11,
+        out_specs=[VMEM, ANY, ANY, ANY, ANY, ANY, ANY, ANY, VMEM, VMEM, VMEM, ANY, ANY],
         scratch_shapes=[
             pltpu.VMEM((2, length, width), BF16),
-            pltpu.VMEM((2, 16 * rows, columns), BF16),
+            pltpu.VMEM(w_in, BF16),
+            pltpu.VMEM(w_out, BF16),
+            pltpu.VMEM((length, width), BF16),
             pltpu.VMEM((8, ROWS, width), BF16),
-            pltpu.VMEM((8, 2, quarter // 2, width), BF16),
-            pltpu.VMEM((8, 2, quarter // 2, width), BF16),
-            pltpu.VMEM((8, 2, 2, quarter // 2, width), BF16),
+            pltpu.VMEM((4, 2, quarter // 2, width), BF16),
+            pltpu.VMEM((4, 2, quarter // 2, width), BF16),
+            pltpu.VMEM((4, 2, 2, quarter // 2, width), BF16),
             pltpu.VMEM((8, 4, 8, LANES), F32),
-            pltpu.VMEM((8, 4, 8, LANES), F32),
+            pltpu.VMEM((8, 4, 4, 8, LANES), F32),
             pltpu.VMEM((2, ROWS, saved_columns), F32),
+            pltpu.VMEM((2, ROWS, conv), BF16),
             pltpu.VMEM((2, chunks, pair // 2, inner), F32),
             pltpu.VMEM((2, ROWS, width), BF16),
-            pltpu.VMEM((4, quarter, width), BF16),
-            pltpu.VMEM((4, 8, LANES), F32),
+            pltpu.VMEM((ROWS, inner), BF16),
             pltpu.VMEM((pair // 2, inner), F32),
             pltpu.VMEM((ROWS + 8, conv), F32),
+            pltpu.VMEM((rows, columns), BF16),
             pltpu.VMEM((4, rows, columns), BF16),
-            pltpu.VMEM((2,) + few.shape, F32),
+            pltpu.VMEM((4, rows, inner), BF16),
+            pltpu.VMEM((2, 8, conv), F32),
         ]
         + gather_sems() * 3
         + (gather_sems() + dma(8)) * 2
+        + gather_sems()
+        + gather_sems() + dma(8)
         + dma(1)
-        + [pltpu.SemaphoreType.DMA((8, 6))] * 2
-        + [pltpu.SemaphoreType.DMA((4, 6))] * 2
-        + [pltpu.SemaphoreType.DMA((2,))]
-        + [pltpu.SemaphoreType.DMA((8, 3))] * 2
-        + [pltpu.SemaphoreType.DMA((4, 3))] * 2
-        + dma(1)
-        + [pltpu.SemaphoreType.DMA((3, 2)), pltpu.SemaphoreType.DMA((41,))],
+        + semaphores(4, 6) + semaphores(4, 6) + semaphores(8, 3)
+        + [pltpu.SemaphoreType.DMA((4, 2)), pltpu.SemaphoreType.DMA((9,))],
         compiler_params=remote_params(0),
         name="forward_layers",
-    )(inputs.reshape(half), out_grad.reshape(half), shard, few, selector)
+    )(inputs.reshape(half), out_grad.reshape(half), shard_out, gate_x, read_write, step, main, of_state, bias, log_rate,
+      skip, gate, norm, selector)
 
 
 class Deliver:
@@ -801,14 +877,14 @@
     return grad_out + scale * (scaled - unit * mean), jnp.sum(summed * unit, 0, keepdims=True)
 
 
-def backward_block(sizes, first_block, e, scales, w, few, selector, collector, saved, states,
-                   part, grad, mixed, few_out, state, later, pad):
+def backward_block(sizes, first_block, e, scales, w_in, w_out, few, selector, collector, saved, saved_p, states,
+                   part, grad, mixed, few_out, state, later, pad, serve):
     inner, pair, heads = sizes
     states_count = pair // 2
     split = inner + inner + pair
     conv = inner + pair
     quarter = ROWS // 4
-    (z_at, p_at, c_at, raw_at, y_at), _ = columns_of(inner, conv)
+    (z_at, c_at, raw_at, y_at), _ = columns_of(inner, conv)
 
     @pl.when(first_block)
     def _():
@@ -834,7 +910,7 @@
     )
     inverse = column(0)
     inner_dot = column(1)
-    mixed_grad = mm(e, w[:, split + LANES :])
+    mixed_grad = mm(e, w_out)
     for chunk in reversed(range(ROWS // CHUNK)):
         at = slice(chunk * CHUNK, (chunk + 1) * CHUNK)
         z = saved[at, z_at]
@@ -903,9 +979,11 @@
         dxs = wide_delta * dscaled + skip * dy
         pad[at, :] = jnp.concatenate([dxs, db_state, dc_state], 1) * slope
         grad[at, split:] = draw.astype(BF16)
+        if chunk == ROWS // CHUNK - 1:
+            serve()
     for chunk in range(ROWS // CHUNK):
         at = slice(chunk * CHUNK, (chunk + 1) * CHUNK)
-        p = saved[at, p_at]
+        p = saved_p[at, :].astype(F32)
         total = jnp.zeros((CHUNK, conv), F32)
         for tap in range(4):
             begin = chunk * CHUNK + 3 - tap
@@ -914,18 +992,68 @@
             few_out[tap : tap + 1, :] += jnp.sum(p * shifted, 0, keepdims=True)
         few_out[4:5, :] += jnp.sum(pad[at, :], 0, keepdims=True)
         grad[at, inner:split] = total.astype(BF16)
-    part[...] = mm(grad[...], w[:, : split + LANES], ((1,), (1,))).astype(BF16)
-
-
-def backward_all_kernel(sizes, errors_later, scales_later, weights, few, selector, collector, normed, saved, states,
-                        res, inverses, last_low,
-                        last_out, first_grad, second_grad, large, few_sum, few_shared, state_grad,
-                        errors, scales, w_held, part, relays, sums, arrived, stage, state_stage, norm_stage,
-                        grad, mixed, own_scales, own_grad, low_grad, few_grad, norm_grad, total, low_total,
-                        core1, core0, u0, u1, u2, v0, v1, v2, e0, e1, e2, middle, z_blocks,
-                        pair_few, y_few, z_few, x_few, state_parts, state, later, pad,
-                        rs, rr, gs, gr, ss, sr, c1s, c1r, y1s, y1r, c0s, c0r, y0s, y0r, zs, zr,
-                        ps, pr, fs, fr, hs, hr, js, jr, ks, kr, ws, wr, os, og, is_, ig, loads, load):
+    part[...] = mm(grad[...], w_in, ((1,), (1,))).astype(BF16)
+
+
+class WeightParts:
+    def __init__(self, refs):
+        (self.columns, self.low, self.core, self.y, self.z, self.middle, self.z_blocks, self.core_sems, self.y_sems,
+         self.z_sems) = refs
+
+    @staticmethod
+    def scratch(piece, columns):
+        grads = pltpu.VMEM((4, 2, piece, columns), BF16)
+        return [
+            [
+                pltpu.VMEM((2, 4, 2, piece, columns), BF16),
+                grads,
+                scatter_buffers(piece, columns),
+                scatter_buffers(piece // 2, columns),
+                pltpu.VMEM((2, piece, columns), BF16),
+                pltpu.VMEM((4, 2, piece // 2, columns), BF16),
+            ],
+            [[dma(8), dma(8)], [dma(6), dma(6)], dma(6)],
+        ]
+
+    def flush(self, total):
+        piece = total.shape[0] // 16
+        for index in range(16):
+            z_hi, y_at, core_at = index // 8, (index // 2) % 4, index % 2
+            self.low[z_hi, y_at, core_at] = total[index * piece : (index + 1) * piece, self.columns].astype(BF16)
+
+    def core_sum(self, layer):
+        return CoreSum(self.low, self.core, self.core_sems[layer])
+
+    def y_sum(self, layer):
+        _, y, core, _ = place()
+        return RingScatter(y, at_y, lambda owner, half: self.low.at[half, owner, core], self.y, self.y_sems[layer])
+
+    def z_sum(self):
+        z, _, _, _ = place()
+        return RingScatter(z, at_z, lambda owner, half: self.z_blocks.at[owner, half], self.z, self.z_sems)
+
+    def to_z(self, sums):
+        rows = self.z_blocks.shape[2]
+        for z_hi in range(2):
+            first = sums.result(z_hi).astype(BF16)
+            second = self.middle[z_hi]
+            for half in range(2):
+                self.z_blocks[2 * z_hi, half] = first[half * rows : (half + 1) * rows]
+                self.z_blocks[2 * z_hi + 1, half] = second[half * rows : (half + 1) * rows]
+
+
+def flat(tree):
+    return jax.tree.leaves(tree)
+
+
+def backward_all_kernel(sizes, errors_later, scales_later, weights_in, weights_out, few, selector, collector, normed,
+                        saved, saved_p, states, res, inverses, first_own, last_part,
+                        firsts, last_out, first_grad, second_grad, large, few_sum, few_shared, state_grad,
+                        errors, scales, w_in, w_out, part, relays, sums, arrived, stage, p_stage, state_stage,
+                        norm_stage, e_stage, grad, mixed, own_scales, own_grad, low_grad, few_grad, norm_grad, total,
+                        t0, t1, t2, last_held, first_rows, pair_few, y_few, z_few, x_few, state_parts, state, later, pad,
+                        rs, rr, gs, gr, ss, sr, ts, tr, ls, lr, ps, pr, fs, fr, hs, hr, js, jr, ks, kr, ws, wr, is_, ig,
+                        loads, load, core_free, y_free, *rest):
     inner, pair, heads, lead, whole_inner = sizes
     layer_sizes = (inner, pair, heads)
     z, y, core, x = place()
@@ -933,6 +1061,14 @@
     every = (1, 2, 3)
     quarter = ROWS // 4
     split = 2 * inner + pair
+    ends = (slice(2 * inner, total.shape[1]), slice(0, 2 * inner))
+    layout = [WeightParts.scratch(total.shape[0] // 16, at.stop - at.start) for at in ends]
+    refs = iter(rest)
+    memory = [jax.tree.map(lambda _: next(refs), of_part[0]) for of_part in layout]
+    signals = [jax.tree.map(lambda _: next(refs), of_part[1]) for of_part in layout]
+    parts = [WeightParts([at] + held + sems) for at, held, sems in zip(ends, memory, signals)]
+
+    block_rows = lambda owner, half: pl.ds(pl.multiple_of(owner * ROWS + half * (ROWS // 2), ROWS // 2), ROWS // 2)
 
     def at_step(op):
         return 1 - op // 4, 3 - op % 4
@@ -946,53 +1082,70 @@
             pltpu.make_async_copy(saved.at[layer, at], stage.at[slot], loads.at[0, slot]),
             pltpu.make_async_copy(states.at[layer, pl.ds(block * count, count)], state_stage.at[slot], loads.at[1, slot]),
             pltpu.make_async_copy(normed.at[layer, at], norm_stage.at[slot], loads.at[2, slot]),
+            pltpu.make_async_copy(saved_p.at[layer, at], p_stage.at[slot], loads.at[3, slot]),
         ]
 
-    def weight_load(layer):
-        return pltpu.make_async_copy(weights.at[layer], w_held.at[layer], load.at[layer])
-
-    error_load = pltpu.make_async_copy(errors_later, errors.at[1], load.at[2])
-    error_load.start()
-    weight_load(1).start()
-    for copy in loads_of(0):
+    def weight_loads(layer):
+        return [
+            pltpu.make_async_copy(weights_in.at[layer], w_in.at[layer], load.at[layer]),
+            pltpu.make_async_copy(weights_out.at[layer], w_out.at[layer], load.at[6 + layer]),
+        ]
+
+    def error_load(op):
+        _, block = at_step(op)
+        at = pl.ds(pl.multiple_of(block * ROWS, ROWS), ROWS)
+        return pltpu.make_async_copy(errors_later.at[at], e_stage.at[op % 2], loads.at[4, op % 2])
+
+    own_loads = [
+        pltpu.make_async_copy(errors_later.at[owned(block, x, quarter)], low_grad.at[block], load.at[9 + block])
+        for block in range(4)
+    ]
+    sum_loads = [
+        pltpu.make_async_copy(last_part.at[block_rows(owner, half)], last_held.at[index], load.at[13 + index])
+        for index, (owner, half) in enumerate(((x, 0), (x, 1), ((x + 1) % 4, 0), ((x + 3) % 4, 1)))
+    ]
+    error_load(0).start()
+    for copy in weight_loads(1) + loads_of(0):
         copy.start()
-    weight_load(0).start()
+    first_load = pltpu.make_async_copy(first_own, first_rows, load.at[8])
+    first_load.start()
+    for copy in own_loads + sum_loads + weight_loads(0):
+        copy.start()
     greet(*around(x, at_x, every), *around(y, at_y, every), *around(z, at_z, every), at_core(1 - core),
           *both_pipes(x, pipe))
-    output = Deliver(1, last_low, last_out, os, og, load.at[3])
-    output.start()
+    last_sums = RingScatter(x, at_x, lambda owner, half: last_part.at[block_rows(owner, half)], (t0, t1, t2), (ts, tr),
+                            [last_held.at[index] for index in range(4)])
+    first_copy = pltpu.make_async_copy(first_own, firsts.at[pipe], load.at[2])
+    first_swap = remote(first_own, firsts.at[pipe], (ps, pr), 1, at_pipe(1 - pipe))
+    first_copy.start()
+    first_swap.start()
     scales[1] = scales_later[...]
     few_grad[...] = jnp.zeros_like(few_grad)
     norm_grad[...] = jnp.zeros_like(norm_grad)
     own_scales[...] = jnp.zeros_like(own_scales)
     total[...] = jnp.zeros_like(total)
-    error_load.wait()
-    for block in range(4):
-        own_grad[block] = errors[1, owned(block, x, quarter)].astype(F32)
-    weight_load(1).wait()
+    for block, copy in enumerate(own_loads):
+        copy.wait()
+        own_grad[block] = low_grad[block].astype(F32)
+    for copy in sum_loads:
+        copy.wait()
+    for copy in weight_loads(1):
+        copy.wait()
 
     def sums_of(op):
         rows = lambda owner, half: part.at[
-            op % 4, pl.ds(pl.multiple_of(owner * quarter + half * (quarter // 2), quarter // 2), quarter // 2)
+            op % 3, pl.ds(pl.multiple_of(owner * quarter + half * (quarter // 2), quarter // 2), quarter // 2)
         ]
         return BlockSums(x, rows, relays, sums, arrived, (rs, rr), op)
 
     def gather_of(block):
         place_of = lambda origin, half: errors.at[
-            0, pl.ds(pl.multiple_of(block * ROWS + origin * quarter + half * (quarter // 2), quarter // 2), quarter // 2)
+            pl.ds(pl.multiple_of(block * ROWS + origin * quarter + half * (quarter // 2), quarter // 2), quarter // 2)
         ]
         return RingGather(x, at_x, lambda half: place_of(x, half), place_of, (gs.at[block], gr.at[block]), local=False)
 
     def scales_of(block):
         return to_everyone(x, at_x, lambda to: own_scales.at[block], lambda me: scales.at[0, block, me], (ss, sr), block)
-
-    def core_sum(layer):
-        arrived_core, sems = ((core0, (c0s, c0r)), (core1, (c1s, c1r)))[layer]
-        return CoreSum(low_total, arrived_core, sems)
-
-    def y_sum(layer):
-        buffers, sems = (((v0, v1, v2), (y0s, y0r)), ((u0, u1, u2), (y1s, y1r)))[layer]
-        return RingScatter(y, at_y, lambda owner, half: low_total.at[half, owner, core], buffers, sems)
 
     def finish_sums(op):
         layer, block = at_step(op)
@@ -1007,10 +1160,10 @@
 
         @pl.when(layer == 1)
         def _():
-            errors[0, owned(block, x, quarter)] = low
+            errors[owned(block, x, quarter)] = low
             gather_of(block).start()
             dots = jnp.sum(low.astype(F32) * (res[1, block] - res[0, block]), -1, keepdims=True) / whole_inner
-            own_scales[block, 0:1, :] = inverses[0, block, 0:1, :]
+            own_scales[block, 0:1, :] = inverses[block, 0:1, :]
             own_scales[block, 1:2, 0:quarter] = column_to_row(dots)
             scales[0, block, x] = own_scales[block]
             scales_of(block).start()
@@ -1019,15 +1172,25 @@
         def _():
             low_grad[block] = low
 
-    def flush():
-        piece = total.shape[0] // 16
-        for index in range(16):
-            z_hi, y_at, core_at = index // 8, (index // 2) % 4, index % 2
-            low_total[z_hi, y_at, core_at] = total[index * piece : (index + 1) * piece, :].astype(BF16)
-
-    own_block = errors.at[0, pl.ds(pl.multiple_of(x * ROWS, ROWS), ROWS)]
+    own_block = errors.at[pl.ds(pl.multiple_of(x * ROWS, ROWS), ROWS)]
     second_copy = pltpu.make_async_copy(own_block, second_grad.at[pipe], load.at[4])
     swap = remote(own_block, second_grad.at[pipe], (ps, pr), 0, at_pipe(1 - pipe))
+
+    last_copy = pltpu.make_async_copy(first_rows, last_out.at[pipe], load.at[3])
+    last_swap = remote(first_rows, last_out.at[pipe], (ls, lr), 0, at_pipe(1 - pipe))
+
+    def finish_last():
+        last_sums.wait()
+        first_load.wait()
+        column = jnp.concatenate(
+            [row_to_column(scales_later[x, owner, 0:1, :])[:quarter] for owner in range(4)], 0
+        )
+        for half in range(2):
+            at = slice(half * (ROWS // 2), (half + 1) * (ROWS // 2))
+            first_rows[at, :] = (first_rows[at, :].astype(F32) + column[at] * last_sums.result(half)).astype(BF16)
+        last_sums.finish()
+        last_copy.start()
+        last_swap.start()
 
     def step(op, carry):
         layer, block = at_step(op)
@@ -1042,7 +1205,8 @@
 
         @pl.when(op == 4)
         def _():
-            weight_load(0).wait()
+            for copy in weight_loads(0):
+                copy.wait()
 
         @pl.when(op == 7)
         def _():
@@ -1058,65 +1222,91 @@
                 copy.start()
 
         at = pl.ds(pl.multiple_of(block * ROWS, ROWS), ROWS)
-        e = errors[layer, at]
-        backward_block(layer_sizes, block == 3, e, scales.at[layer, block], w_held.at[layer], few.at[layer],
-                       selector[...], collector[...], stage.at[slot], state_stage.at[slot],
-                       part.at[op % 4], grad, mixed, few_grad.at[layer], state, later, pad)
+
+        @pl.when(layer == 0)
+        def _():
+            e_stage[slot] = errors[at]
+
+        @pl.when(layer == 1)
+        def _():
+            error_load(op).wait()
+
+        @pl.when(op < 3)
+        def _():
+            error_load(op + 1).start()
+
+        e = e_stage[slot]
+        def serve():
+            @pl.when(op >= 1)
+            def _():
+                sums_of(op - 1).relay()
+
+            @pl.when((op >= 2) & (op < 6))
+            def _():
+                gather_of(5 - op).relay()
+
+            @pl.when(op == 4)
+            def _():
+                for of_part in parts:
+                    of_part.core_sum(1).finish()
+                    of_part.y_sum(1).start()
+                pl.semaphore_signal(core_free, inc=1, device_id=at_core(1 - core), device_id_type=MESH)
+
+            @pl.when(op == 5)
+            def _():
+                for of_part in parts:
+                    of_part.y_sum(1).relay()
+
+            @pl.when(op == 6)
+            def _():
+                for of_part in parts:
+                    job = of_part.y_sum(1)
+                    job.wait()
+                    for half in range(2):
+                        of_part.middle[half] = job.result(half).astype(BF16)
+                    job.finish()
+                for device in around(y, at_y):
+                    pl.semaphore_signal(y_free, inc=1, device_id=device, device_id_type=MESH)
+
+        backward_block(layer_sizes, block == 3, e, scales.at[layer, block], w_in[layer].reshape(e.shape[1], -1),
+                       w_out[layer].reshape(e.shape[1], -1), few.at[layer],
+                       selector[...], collector[...], stage.at[slot], p_stage.at[slot], state_stage.at[slot],
+                       part.at[op % 3], grad, mixed, few_grad.at[layer], state, later, pad, serve)
         sums_of(op).start()
 
-        @pl.when((op >= 3) & (op < 7))
-        def _():
-            gather_of(6 - op).relay()
-
-        @pl.when(op >= 2)
-        def _():
-            finish_sums(op - 2)
-
         @pl.when(op >= 1)
         def _():
-            sums_of(op - 1).relay()
-
-        @pl.when(op == 4)
-        def _():
-            core_sum(1).finish()
-            y_sum(1).start()
-
-        @pl.when(op == 5)
-        def _():
-            y_sum(1).relay()
-
-        @pl.when(op == 6)
-        def _():
-            job = y_sum(1)
-            job.wait()
-            for half in range(2):
-                middle[half] = job.result(half).astype(BF16)
-            job.finish()
+            finish_sums(op - 1)
 
         turn = ((0,), (0,))
         wide = split + LANES
         for index in range(total.shape[0] // ROWS):
             rows = slice(index * ROWS, (index + 1) * ROWS)
             total[rows, :wide] += mm(norm_stage[slot, :, rows], grad[...], turn)
-            total[rows, wide:] += mm(errors[layer, at, rows], mixed[...], turn)
+            total[rows, wide:] += mm(e_stage[slot, :, rows], mixed[...], turn)
 
         @pl.when(op == 3)
         def _():
-            flush()
-            core_sum(1).start()
+            for of_part in parts:
+                of_part.flush(total)
+                of_part.core_sum(1).start()
             total[...] = jnp.zeros_like(total)
 
         return carry
 
     lax.fori_loop(0, 8, step, 0)
-    flush()
-    cores = core_sum(0)
-    cores.start()
-    finish_sums(6)
+    pl.semaphore_wait(core_free, 1)
+    for of_part in parts:
+        of_part.flush(total)
+        of_part.core_sum(0).start()
+    pl.semaphore_wait(y_free, 2)
+    last_sums.start()
     sums_of(7).relay()
-    cores.finish()
-    y_sums = y_sum(0)
-    y_sums.start()
+    y_sums = [of_part.y_sum(0) for of_part in parts]
+    z_sums = [of_part.z_sum() for of_part in parts]
+    for of_part, job in zip(parts, y_sums):
+        of_part.core_sum(0).finish()
+        job.start()
     finish_sums(7)
     gradient = Deliver(0, low_grad, first_grad, is_, ig, load.at[5])
     gradient.start()
@@ -1126,43 +1316,41 @@
         few_grad[layer, 7:8, :] = norm_grad[layer, 0:1, width:]
     few_core = remote(few_grad, pair_few, (fs, fr), 0, at_core(1 - core))
     few_core.start()
+    y_sums[0].relay()
     few_core.wait()
-    y_sums.relay()
     few_grad[...] = few_grad[...] + pair_few[...]
     few_y = Everyone(y, at_y, lambda to: few_grad, lambda me: y_few.at[me], (hs, hr))
     few_y.start()
-    y_sums.wait()
-    rows = z_blocks.shape[2]
-    for z_hi in range(2):
-        first = y_sums.result(z_hi).astype(BF16)
-        second = middle[z_hi]
-        for half in range(2):
-            z_blocks[2 * z_hi, half] = first[half * rows : (half + 1) * rows]
-            z_blocks[2 * z_hi + 1, half] = second[half * rows : (half + 1) * rows]
-    z_sums = RingScatter(z, at_z, lambda owner, half: z_blocks.at[owner, half], (e0, e1, e2), (zs, zr))
-    z_sums.start()
-    y_sums.finish()
+    last_sums.relay()
+    y_sums[0].wait()
+    parts[0].to_z(y_sums[0])
+    z_sums[0].start()
+    y_sums[1].relay()
     few_y.wait()
     y_few[y] = few_grad[...]
     few_grad[...] = (y_few[0] + y_few[1]) + (y_few[2] + y_few[3])
     few_z = Everyone(z, at_z, lambda to: few_grad.at[to % 2], lambda me: z_few.at[me], (js, jr))
     few_z.start()
-    z_sums.relay()
+    z_sums[0].relay()
     few_z.wait()
     z_few[z] = few_grad[pipe]
     few_sum[...] = (z_few[0] + z_few[1]) + (z_few[2] + z_few[3])
     x_few[x] = few_sum[...]
     few_x = Everyone(x, at_x, lambda to: few_sum, lambda me: x_few.at[me], (ks, kr))
     few_x.start()
-    z_sums.wait()
+    finish_last()
+    z_sums[0].wait()
+    rows = parts[0].z_blocks.shape[2]
     for half in range(2):
-        large[half * rows : (half + 1) * rows, :] = z_sums.result(half)
+        large[half * rows : (half + 1) * rows, ends[0]] = z_sums[0].result(half)
     state_rows = 2 * rows // 4
     for block in range(4):
         state_parts[0, block] = large[block * state_rows : (block + 1) * state_rows, 2 * inner : split]
     state_x = Everyone(x, at_x, lambda to: state_parts.at[0, to], lambda me: state_parts.at[1, me], (ws, wr))
     state_x.start()
-    z_sums.finish()
+    y_sums[1].wait()
+    parts[1].to_z(y_sums[1])
+    z_sums[1].start()
     few_x.wait()
     few_shared[...] = (x_few[0] + x_few[1]) + (x_few[2] + x_few[3])
     state_x.wait()
@@ -1170,21 +1358,31 @@
     for step_at in every:
         total_state = total_state + state_parts[1, (x + step_at) % 4]
     state_grad[...] = total_state
+    z_sums[1].relay()
     second_copy.wait()
     swap.wait()
-    output.wait()
+    first_copy.wait()
+    first_swap.wait()
+    last_copy.wait()
+    last_swap.wait()
     gradient.wait()
-
-
-def backward_all(errors, scales, weights, few, normed, saved, states, res, inverses, last_low,
+    z_sums[1].wait()
+    for half in range(2):
+        large[half * rows : (half + 1) * rows, ends[1]] = z_sums[1].result(half)
+    for job in y_sums + z_sums:
+        job.finish()
+
+
+def backward_all(errors, scales, weights_in, weights_out, few, normed, saved, saved_p, states, res, inverses, first_own, last_part,
                  inner, pair, heads, whole_inner):
     length, width = errors.shape
     _, blocks, quarter, _ = res.shape
     conv = inner + pair
     lead = conv - (width - conv)
     split = 2 * inner + pair
-    columns = weights.shape[2]
-    piece = weights.shape[1] // 16
+    piece = weights_in.shape[4]
+    layout = [WeightParts.scratch(piece, pair + LANES + inner), WeightParts.scratch(piece, 2 * inner)]
+    columns = weights_in.shape[5] + inner
     chunks = ROWS // CHUNK
     selector, collector = constants(inner, heads)
     shape = jax.ShapeDtypeStruct
@@ -1195,7 +1393,8 @@
     return pl.pallas_call(
         partial(backward_all_kernel, (inner, pair, heads, lead, whole_inner)),
         out_shape=[
-            delivered,
+            shape((2, blocks * quarter, width), BF16),
+            shape((2, blocks * quarter, width), BF16),
             delivered,
             shape((2, blocks * quarter, width), BF16),
             shape((piece, columns), F32),
@@ -1203,18 +1402,21 @@
             shape(few_shape, F32),
             shape((piece // 4, pair), F32),
         ],
-        in_specs=[ANY, VMEM, ANY, VMEM, VMEM, VMEM, ANY, ANY, ANY, VMEM, VMEM, ANY],
-        out_specs=[ANY, ANY, ANY, VMEM, VMEM, VMEM, VMEM],
+        in_specs=[ANY, VMEM, ANY, ANY, VMEM, VMEM, VMEM, ANY, ANY, ANY, ANY, VMEM, VMEM, ANY, ANY],
+        out_specs=[ANY, ANY, ANY, ANY, VMEM, VMEM, VMEM, VMEM],
         scratch_shapes=[
-            pltpu.VMEM((2, length, width), BF16),
+            pltpu.VMEM((length, width), BF16),
             pltpu.VMEM((2, blocks, 4, 8, LANES), F32),
-            pltpu.VMEM(weights.shape, BF16),
-            pltpu.VMEM((4, ROWS, width), BF16),
+            pltpu.VMEM(weights_in.shape, BF16),
+            pltpu.VMEM(weights_out.shape, BF16),
+            pltpu.VMEM((3, ROWS, width), BF16),
             pltpu.VMEM((8, 2) + half, BF16),
-            pltpu.VMEM((8, 2) + half, BF16),
+            pltpu.VMEM((2, 2) + half, BF16),
             pltpu.VMEM((8, 2, 2) + half, BF16),
             pltpu.VMEM((2, ROWS, saved.shape[2]), F32),
+            pltpu.VMEM((2, ROWS, conv), BF16),
             pltpu.VMEM((2, chunks, pair // 2, inner), F32),
+            pltpu.VMEM((2, ROWS, width), BF16),
             pltpu.VMEM((2, ROWS, width), BF16),
             pltpu.VMEM((ROWS, split + LANES), BF16),
             pltpu.VMEM((ROWS, inner), BF16),
@@ -1224,15 +1426,11 @@
             pltpu.VMEM((2,) + few_shape, F32),
             pltpu.VMEM((2, 8, width), F32),
             pltpu.VMEM((width, columns), F32),
-            pltpu.VMEM((2, 4, 2, piece, columns), BF16),
-            pltpu.VMEM((4, 2, piece, columns), BF16),
-            pltpu.VMEM((4, 2, piece, columns), BF16),
         ]
-        + scatter_buffers(piece, columns) * 2
-        + scatter_buffers(piece // 2, columns)
+        + scatter_buffers(ROWS // 2, width)
         + [
-            pltpu.VMEM((2, piece, columns), BF16),
-            pltpu.VMEM((4, 2, piece // 2, columns), BF16),
+            pltpu.VMEM((4, ROWS // 2, width), BF16),
+            pltpu.VMEM((ROWS, width), BF16),
             pltpu.VMEM((2,) + few_shape, F32),
             pltpu.VMEM((4, 2) + few_shape, F32),
             pltpu.VMEM((4,) + few_shape, F32),
@@ -1243,73 +1441,109 @@
             pltpu.VMEM((ROWS + 8, conv), F32),
         ]
         + semaphores(8, 6) + semaphores(4, 6) + semaphores(4, 3)
-        + dma(8) + dma(6) + dma(8) + dma(6) + dma(6)
-        + dma(1) + dma(1) + dma(3) + dma(3) + dma(3) + dma(3)
-        + [pltpu.SemaphoreType.DMA((4,)), pltpu.SemaphoreType.DMA((8,))] * 2
-        + [pltpu.SemaphoreType.DMA((3, 2)), pltpu.SemaphoreType.DMA((6,))],
+        + dma(6) + dma(1) + dma(2) + dma(1) + dma(3) + dma(3) + dma(3) + dma(3)
+        + [pltpu.SemaphoreType.DMA((4,)), pltpu.SemaphoreType.DMA((8,))]
+        + [pltpu.SemaphoreType.DMA((5, 2)), pltpu.SemaphoreType.DMA((17,))]
+        + [pltpu.SemaphoreType.REGULAR, pltpu.SemaphoreType.REGULAR]
+        + flat([of_part[0] for of_part in layout])
+        + flat([of_part[1] for of_part in layout]),
         compiler_params=pltpu.CompilerParams(collective_id=1, has_side_effects=True, vmem_limit_bytes=62 * 2**20),
         name="backward_layers",
-    )(errors, scales, weights, few, selector, collector, normed, saved, states, res, inverses, last_low)
+    )(errors, scales, weights_in, weights_out, few, selector, collector, normed, saved, saved_p, states, res, inverses,
+      first_own, last_part)
+
+
+def finish_kernel(sizes, firsts, last_out, first_grad, second_grad, large, few_sum, few_shared, state_grad, few,
+                  activations, input_grads, norm, gate_x, read_write, step, main, of_state, bias, rates, skip, gate,
+                  out_weight):
+    inner, pair, heads, lead = sizes
+    first = lax.axis_index("pipe") == 0
+    activations[0] = jnp.where(first, firsts[...], last_out[...]).astype(F32)
+    input_grads[0] = jnp.where(first, first_grad[...], second_grad[...]).astype(F32)
+    split = 2 * inner + pair
+
+    @pl.when(pl.program_id(0) == 0)
+    def _():
+        norm[:, : few_shared.shape[1] - lead] = few_shared[6:7, lead:]
+        norm[:, few_shared.shape[1] - lead :] = few_shared[7:8, :]
+        for index in range(2):
+            gate_x[0, :, index, :] = large[:, index * inner : (index + 1) * inner]
+        read_write[0] = state_grad[...]
+        step[0] = mm_exact((iota((heads, LANES), 0) == iota((heads, LANES), 1)).astype(F32),
+                           large[:, split : split + LANES], ((1,), (1,)))
+        for tap in range(5):
+            main[tap] = few_sum[tap : tap + 1, :inner]
+            of_state[tap] = few_shared[tap : tap + 1, inner:]
+        bias[...] = few_sum[5:6, inner : inner + heads]
+        rate = jnp.where(first, few[0, 5:6, inner + LANES :], few[1, 5:6, inner + LANES :])
+        rates[...] = (few_sum[5:6, inner + LANES :] * rate)[:, :heads]
+        width = inner // heads
+        skip[...] = jnp.concatenate(
+            [jnp.sum(few_sum[6:7, head * width : (head + 1) * width], 1, keepdims=True) for head in range(heads)], 1
+        )
+        gate[...] = few_sum[5:6, :inner]
+        out_weight[0] = large[:, split + LANES :]
+
+
+def finish_call(firsts, last_out, first_grad, second_grad, large, few_sum, few_shared, state_grad, few, inner, pair, heads):
+    two, part, width = firsts.shape
+    conv = few.shape[2]
+    lead = conv - (width - conv)
+    rows = part // 4
+    piece = large.shape[0]
+    by_rows = pl.BlockSpec((two, rows, width), lambda i: (0, i, 0))
+    out_rows = pl.BlockSpec((1, two, rows, width), lambda i: (0, 0, i, 0))
+    shape = lambda *sizes: jax.ShapeDtypeStruct(sizes, F32)
+    small = [
+        shape(1, width),
+        shape(1, piece, 2, inner),
+        shape(1, piece // 4, pair),
+        shape(1, heads, piece),
+        shape(5, 1, inner),
+        shape(5, 1, pair),
+        shape(1, heads),
+        shape(1, heads),
+        shape(1, heads),
+        shape(1, inner),
+        shape(1, piece, inner),
+    ]
+    return pl.pallas_call(
+        partial(finish_kernel, (inner, pair, heads, lead)),
+        grid=(4,),
+        in_specs=[by_rows] * 4 + [whole(item) for item in (large, few_sum, few_shared, state_grad, few)],
+        out_specs=[out_rows] * 2 + [whole(item) for item in small],
+        out_shape=[shape(1, two, part, width)] * 2 + small,
+        compiler_params=pltpu.CompilerParams(vmem_limit_bytes=60 * 2**20),
+        name="outputs",
+    )(firsts, last_out, first_grad.reshape(firsts.shape), second_grad, large, few_sum, few_shared, state_grad, few)
+
+
+def whole(array):
+    rank = len(array.shape)
+    return pl.BlockSpec(array.shape, lambda i: (0,) * rank)
 
 
 def body(inputs, out_grad, norm_gain, in_gate_x, in_read_write, in_step, conv_main, conv_state,
          step_bias, log_rate, skip_gain, gate_gain, out_weight):
-    _, part, width = inputs.shape
     inner = out_weight.shape[2]
     pair = in_read_write.shape[2]
     heads = step_bias.shape[1]
     whole_inner = inner * lax.axis_size("tensor")
-    split = 2 * inner + pair
-    wide = inner + pair
-    first = lax.axis_index("pipe") == 0
-    shard = jnp.concatenate(
-        [
-            in_gate_x[0, :, 0],
-            in_gate_x[0, :, 1],
-            in_read_write[0],
-            jnp.pad(in_step[0], ((0, 0), (0, LANES - heads))),
-            out_weight[0],
-        ],
-        1,
+    few, weights_in, weights_out, errors, normed, saved, saved_p, states, res, inverses, scales, first_own, last_part = (
+        forward_all(
+            inputs, out_grad, out_weight[0], in_gate_x[0], in_read_write, in_step.transpose(0, 2, 1),
+            conv_main.transpose(1, 0, 2), conv_state.transpose(1, 0, 2), step_bias, log_rate, skip_gain, gate_gain, norm_gain, inner, pair, heads, whole_inner
+        )
     )
-    rate = -jnp.exp(log_rate[0])
-    pad = ((0, 0), (0, LANES - heads))
-    skip = jnp.broadcast_to(skip_gain[0][:, None], (heads, inner // heads)).reshape(1, inner)
-    few = jnp.concatenate(
-        [
-            jnp.concatenate([conv_main[0], conv_state[0]], 1),
-            jnp.concatenate([gate_gain, jnp.pad(step_bias, pad), jnp.pad(rate[None], pad)], 1),
-            jnp.concatenate([skip, norm_gain], 1).reshape(2, wide),
-        ],
-        0,
-    )
-    few, weights, errors, normed, saved, states, res, inverses, scales, firsts, last_low = forward_all(
-        inputs, out_grad, shard, few, inner, pair, heads, whole_inner
-    )
-    weights = weights.reshape(2, width, -1)
-    last_out, first_grad, second_grad, large, few_sum, few_shared, state_grad = backward_all(
-        errors, scales, weights, few, normed, saved, states, res, inverses, last_low,
+    firsts, last_out, first_grad, second_grad, large, few_sum, few_shared, state_grad = backward_all(
+        errors, scales, weights_in, weights_out, few, normed, saved, saved_p, states, res, inverses, first_own, last_part,
         inner, pair, heads, whole_inner
     )
-    by_layer = lambda zero, one: jnp.where(
-        first, zero.reshape(1, 2, part, width), one.reshape(1, 2, part, width)
-    ).astype(F32)
-    rates = few_sum[5, inner + LANES : inner + LANES + heads] * rate
-    return (
-        by_layer(firsts, last_out),
-        by_layer(first_grad, second_grad),
-        few_shared[6:].reshape(1, 2 * wide)[:, inner:],
-        large[:, : 2 * inner].reshape(1, -1, 2, inner),
-        state_grad[None],
-        large[None, :, split : split + heads],
-        few_sum[None, :5, :inner],
-        few_shared[None, :5, inner:],
-        few_sum[5:6, inner : inner + heads],
-        rates[None],
-        few_sum[6, :inner].reshape(1, heads, -1).sum(2),
-        few_sum[5:6, :inner],
-        large[None, :, split + LANES :],
+    outputs = finish_call(
+        firsts, last_out, first_grad, second_grad, large, few_sum, few_shared, state_grad, few, inner, pair, heads
     )
+    turned = [item.transpose(axes) for item, axes in zip(outputs[5:8], ((0, 2, 1), (1, 0, 2), (1, 0, 2)))]
+    return (*outputs[:5], *turned, *outputs[8:])
 
 
 def solution(mesh):

time: 255 us -> 238 us (0.933)
  local copies, waits for them, and re-layouts: 11.2 us -> 0 us
  other arithmetic: 7.72 us -> 0 us
    pallas_call x1, Pallas kernels: 118 us -> 103 us  [forward_all(): pl.pallas_call(partial(forward_all_kernel, (inner, pair, heads, lead, who...]
    pallas_call x1, Pallas kernels: 117 us -> 129 us  [backward_all(): pl.pallas_call(partial(backward_all_kernel, (inner, pair, heads, lead, wh...]
    unnamed x27 -> x0, local copies, waits for them, and re-layouts: 5.5 us -> none
    pallas_call x0 -> x1, Pallas kernels: none -> 5.27 us  [finish_call(): pl.pallas_call(partial(finish_kernel, (inner, pair, heads, lead)), grid=(...]
    convert_element_type x1 -> x0, other arithmetic: 3.88 us -> none  [body(): by_layer = lambda zero, one: jnp.where(first, zero.reshape(1, 2, part, wi...]
where the time goes in v5:
time: 238 us
  Pallas kernels  237 us (100%)
    pallas_call x1, Pallas kernels, backward_all(): pl.pallas_call(partial(backward_all_kernel, (inner, pair, heads, lead, wh...  129 us
    pallas_call x1, Pallas kernels, forward_all(): pl.pallas_call(partial(forward_all_kernel, (inner, pair, heads, lead, who...  103 us
    pallas_call x1, Pallas kernels, finish_call(): pl.pallas_call(partial(finish_kernel, (inner, pair, heads, lead)), grid=(...  5.27 us

profile of v5, /device:TPU:0, one launch (start us, length us, event | category | flops | bytes accessed | tf_op | source)
XLA Modules:
  0.0 238.1 jit_solution(2454440270639155727)
XLA Ops:
  0.6 102.9 %forward_layers.1 = (f32[2,8,768]{2,1,0:T(8,128)}, bf16[2,2,4,2,64,1408]{5,4,3,2,1,0:T(8,128)(2,1)}, bf16[2,2,4,2,64,512]{5,4,3,2,1,0:T(8,128)(2,1)}, bf16[1024,...) custom-call(bf16[2,2,128,1024]{3,2,1,0:T(8,128)(2,1)} %bitcast.11, ...), custom_call_target="tpu_custom_call" | custom-call | tf_op jit(solution)/shard_map/forward_layers/pallas_call | solution.py:735
  103.6 129.1 %backward_layers.1 = (bf16[2,256,1024]{2,1,0:T(8,128)(2,1)}, bf16[2,256,1024]{2,1,0:T(8,128)(2,1)}, bf16[2,4,64,1024]{3,2,1,0:T(8,128)(2,1)}, bf16[2,256,1024]{2...) custom-call(bf16[1024,1024]{1,0:T(8,128)(2,1)} %get-tuple-element.47.errors_la, ...), custom_call_target="tpu_custom_call" | custom-call | tf_op jit(solution)/shard_map/backward_layers/pallas_call | solution.py:1393
  232.6 5.3 %outputs.1 = (f32[1,2,256,1024]{3,2,1,0:T(8,128)}, f32[1,2,256,1024]{3,2,1,0:T(8,128)}, f32[1,1024]{1,0:T(1,128)}, f32[1,64,2,512]{3,2,1,0:T(2,128)}, f32[1,16,2...) custom-call(bf16[2,256,1024]{2,1,0:T(8,128)(2,1)} %get-tuple-element, ...), custom_call_target="tpu_custom_call" | custom-call | tf_op jit(solution)/shard_map/outputs/pallas_call | solution.py:1510

commit v6 on v5

--- a/solution.py
+++ b/solution.py
@@ -273,10 +273,11 @@
 
 
 class BlockSums:
-    def __init__(self, x, piece, relays, sums, arrived, sems, op):
+    def __init__(self, x, piece, relays, sums, arrived, sems, op, near=None):
         self.right, self.left, self.me = (x + 1) % 4, (x + 3) % 4, x
         across = (x + 2) % 4
-        self.piece, self.relays, self.sums, self.arrived = piece, relays, sums, arrived
+        self.relays, self.sums, self.arrived = relays, sums, arrived
+        self.near = near or [piece(x, 0), piece(x, 1), piece(self.right, 0), piece(self.left, 1)]
         at_op = [sem.at[op] for sem in sems]
         to_right, to_left = at_x(self.right), at_x(self.left)
         self.copies = [
@@ -294,9 +295,9 @@
             copy.start()
 
     def relay(self):
-        for half, block in ((0, self.right), (1, self.left)):
+        for half in range(2):
             self.copies[half].wait_recv()
-            total = self.relays[self.op, half].astype(F32) + self.piece(block, half)[...].astype(F32)
+            total = self.relays[self.op, half].astype(F32) + self.near[2 + half][...].astype(F32)
             self.sums[self.op % 2, half] = total.astype(BF16)
             self.copies[4 + half].start()
 
@@ -307,7 +308,7 @@
     def result(self):
         return jnp.concatenate(
             [
-                self.piece(self.me, half)[...].astype(F32)
+                self.near[half][...].astype(F32)
                 + self.arrived[self.op, 0, half].astype(F32)
                 + self.arrived[self.op, 1, half].astype(F32)
                 for half in range(2)
@@ -785,63 +786,6 @@
         name="forward_layers",
     )(inputs.reshape(half), out_grad.reshape(half), shard_out, gate_x, read_write, step, main, of_state, bias, log_rate,
       skip, gate, norm, selector)
-
-
-class Deliver:
-    def __init__(self, layer, source, target, sends, recvs, local):
-        self.layer, self.source, self.target = layer, source, target
-        self.sends, self.recvs, self.local_sem = sends, recvs, local
-        z, _, _, self.x = place()
-        self.pipe = z % 2
-        self.here = self.pipe == layer
-
-    def copy(self, step, pipe, device_pipe, block):
-        return pltpu.make_async_remote_copy(
-            src_ref=self.source.at[block],
-            dst_ref=self.target.at[pipe, self.x],
-            send_sem=self.sends.at[step],
-            recv_sem=self.recvs.at[pipe * 4 + step],
-            device_id={"pipe": device_pipe, "tensor": block},
-            device_id_type=MESH,
-        )
-
-    def out(self, step):
-        return self.copy(step, self.pipe, self.layer, (self.x + step) % 4)
-
-    def local(self):
-        return pltpu.make_async_copy(self.source.at[self.x], self.target.at[self.pipe, self.x], self.local_sem)
-
-    def start(self):
-        for step in (1, 2, 3):
-            self.out(step).start()
-
-        @pl.when(self.here)
-        def _():
-            self.local().start()
-
-        @pl.when(jnp.logical_not(self.here))
-        def _():
-            self.out(0).start()
-
-    def wait(self):
-        for step in (1, 2, 3):
-            self.out(step).wait_send()
-
-        @pl.when(self.here)
-        def _():
-            self.local().wait()
-            for step in (1, 2, 3):
-                self.out(step).wait_recv()
-            for step in range(4):
-                self.copy(step, 1 - self.pipe, 1 - self.pipe, self.x).wait_recv()
-
-        @pl.when(jnp.logical_not(self.here))
-        def _():
-            self.out(0).wait_send()
-
-
-def both_pipes(x, pipe):
-    return [{"pipe": 1 - pipe, "tensor": (x + step) % 4} for step in range(4)]
 
 
 class CoreSum:
@@ -1012,7 +956,7 @@
                 pltpu.VMEM((2, piece, columns), BF16),
                 pltpu.VMEM((4, 2, piece // 2, columns), BF16),
             ],
-            [[dma(8), dma(8)], [dma(6), dma(6)], dma(6)],
+            [[pltpu.SemaphoreType.DMA((2, 8))] * 2, [dma(6), dma(6)], dma(6)],
         ]
 
     def flush(self, total):
@@ -1022,7 +966,7 @@
             self.low[z_hi, y_at, core_at] = total[index * piece : (index + 1) * piece, self.columns].astype(BF16)
 
     def core_sum(self, layer):
-        return CoreSum(self.low, self.core, self.core_sems[layer])
+        return CoreSum(self.low, self.core, [sem.at[layer] for sem in self.core_sems])
 
     def y_sum(self, layer):
         _, y, core, _ = place()
@@ -1042,6 +986,18 @@
                 self.z_blocks[2 * z_hi + 1, half] = second[half * rows : (half + 1) * rows]
 
 
+def mix_rows(sizes, scales, few, saved, mixed):
+    inner, pair, _ = sizes
+    (z_at, _, _, y_at), _ = columns_of(inner, inner + pair)
+    quarter = ROWS // 4
+    inverse = jnp.concatenate([row_to_column(scales[owner, 0:1, :])[:quarter] for owner in range(4)], 0)
+    for chunk in range(ROWS // CHUNK):
+        at = slice(chunk * CHUNK, (chunk + 1) * CHUNK)
+        z = saved[at, z_at]
+        g = saved[at, y_at] * (z * sigmoid(z)) * inverse[at]
+        mixed[at, :] = (g * few[5:6, :inner]).astype(BF16)
+
+
 def flat(tree):
     return jax.tree.leaves(tree)
 
@@ -1050,9 +1006,9 @@
                         saved, saved_p, states, res, inverses, first_own, last_part,
                         firsts, last_out, first_grad, second_grad, large, few_sum, few_shared, state_grad,
                         errors, scales, w_in, w_out, part, relays, sums, arrived, stage, p_stage, state_stage,
-                        norm_stage, e_stage, grad, mixed, own_scales, own_grad, low_grad, few_grad, norm_grad, total,
+                        norm_stage, e_stage, grad, mixed, own_scales, own_grad, both_grad, few_grad, norm_grad, total,
                         t0, t1, t2, last_held, first_rows, pair_few, y_few, z_few, x_few, state_parts, state, later, pad,
-                        rs, rr, gs, gr, ss, sr, ts, tr, ls, lr, ps, pr, fs, fr, hs, hr, js, jr, ks, kr, ws, wr, is_, ig,
+                        rs, rr, gs, gr, ss, sr, ts, tr, ls, lr, ps, pr, fs, fr, hs, hr, js, jr, ks, kr, ws, wr, is_, ig, ds, dr,
                         loads, load, core_free, y_free, *rest):
     inner, pair, heads, lead, whole_inner = sizes
     layer_sizes = (inner, pair, heads)
@@ -1061,7 +1017,9 @@
     every = (1, 2, 3)
     quarter = ROWS // 4
     split = 2 * inner + pair
-    ends = (slice(2 * inner, total.shape[1]), slice(0, 2 * inner))
+    wide = split + LANES
+    middle_at = inner + pair
+    ends = (slice(wide, total.shape[1]), slice(middle_at, wide), slice(0, middle_at))
     layout = [WeightParts.scratch(total.shape[0] // 16, at.stop - at.start) for at in ends]
     refs = iter(rest)
     memory = [jax.tree.map(lambda _: next(refs), of_part[0]) for of_part in layout]
@@ -1097,11 +1055,15 @@
         return pltpu.make_async_copy(errors_later.at[at], e_stage.at[op % 2], loads.at[4, op % 2])
 
     own_loads = [
-        pltpu.make_async_copy(errors_later.at[owned(block, x, quarter)], low_grad.at[block], load.at[9 + block])
+        pltpu.make_async_copy(errors_later.at[owned(block, x, quarter)], both_grad.at[pipe, block], load.at[9 + block])
         for block in range(4)
     ]
+    last_rows = lambda piece, owner, half: last_part.at[
+        pl.ds(pl.multiple_of(owner * ROWS + piece * quarter + half * (quarter // 2), quarter // 2), quarter // 2)
+    ]
     sum_loads = [
-        pltpu.make_async_copy(last_part.at[block_rows(owner, half)], last_held.at[index], load.at[13 + index])
+        pltpu.make_async_copy(last_rows(piece, owner, half), last_held.at[piece, index], load.at[13 + 4 * piece + index])
+        for piece in range(4)
         for index, (owner, half) in enumerate(((x, 0), (x, 1), ((x + 1) % 4, 0), ((x + 3) % 4, 1)))
     ]
     error_load(0).start()
@@ -1111,10 +1073,12 @@
     first_load.start()
     for copy in own_loads + sum_loads + weight_loads(0):
         copy.start()
-    greet(*around(x, at_x, every), *around(y, at_y, every), *around(z, at_z, every), at_core(1 - core),
-          *both_pipes(x, pipe))
-    last_sums = RingScatter(x, at_x, lambda owner, half: last_part.at[block_rows(owner, half)], (t0, t1, t2), (ts, tr),
-                            [last_held.at[index] for index in range(4)])
+    greet(*around(x, at_x, every), *around(y, at_y, every), *around(z, at_z, every), at_core(1 - core))
+
+    def last_sums(piece):
+        return BlockSums(x, lambda owner, half: last_rows(piece, owner, half), t0, t1, t2, (ts, tr), piece,
+                         [last_held.at[piece, index] for index in range(4)])
+
     first_copy = pltpu.make_async_copy(first_own, firsts.at[pipe], load.at[2])
     first_swap = remote(first_own, firsts.at[pipe], (ps, pr), 1, at_pipe(1 - pipe))
     first_copy.start()
@@ -1126,7 +1090,7 @@
     total[...] = jnp.zeros_like(total)
     for block, copy in enumerate(own_loads):
         copy.wait()
-        own_grad[block] = low_grad[block].astype(F32)
+        own_grad[block] = both_grad[pipe, block].astype(F32)
     for copy in sum_loads:
         copy.wait()
     for copy in weight_loads(1):
@@ -1146,6 +1110,10 @@
 
     def scales_of(block):
         return to_everyone(x, at_x, lambda to: own_scales.at[block], lambda me: scales.at[0, block, me], (ss, sr), block)
+
+    def hand_over(block):
+        mine = both_grad.at[pipe, block]
+        return remote(mine, mine, (is_, ig), block, at_pipe(1 - pipe))
 
     def finish_sums(op):
         layer, block = at_step(op)
@@ -1170,27 +1138,29 @@
 
         @pl.when(layer == 0)
         def _():
-            low_grad[block] = low
+            both_grad[pipe, block] = low
+            hand_over(block).start()
 
     own_block = errors.at[pl.ds(pl.multiple_of(x * ROWS, ROWS), ROWS)]
     second_copy = pltpu.make_async_copy(own_block, second_grad.at[pipe], load.at[4])
     swap = remote(own_block, second_grad.at[pipe], (ps, pr), 0, at_pipe(1 - pipe))
 
-    last_copy = pltpu.make_async_copy(first_rows, last_out.at[pipe], load.at[3])
-    last_swap = remote(first_rows, last_out.at[pipe], (ls, lr), 0, at_pipe(1 - pipe))
-
-    def finish_last():
-        last_sums.wait()
-        first_load.wait()
-        column = jnp.concatenate(
-            [row_to_column(scales_later[x, owner, 0:1, :])[:quarter] for owner in range(4)], 0
-        )
-        for half in range(2):
-            at = slice(half * (ROWS // 2), (half + 1) * (ROWS // 2))
-            first_rows[at, :] = (first_rows[at, :].astype(F32) + column[at] * last_sums.result(half)).astype(BF16)
-        last_sums.finish()
-        last_copy.start()
-        last_swap.start()
+    def last_copies(piece):
+        at = pl.ds(pl.multiple_of(piece * quarter, quarter), quarter)
+        return [
+            pltpu.make_async_copy(first_rows.at[at], last_out.at[pipe, at], load.at[29 + piece]),
+            remote(first_rows.at[at], last_out.at[pipe, at], (ls, lr), piece, at_pipe(1 - pipe)),
+        ]
+
+    def finish_last(piece):
+        job = last_sums(piece)
+        job.wait()
+        column = row_to_column(scales_later[x, piece, 0:1, :])[:quarter]
+        at = pl.ds(pl.multiple_of(piece * quarter, quarter), quarter)
+        first_rows[at] = (first_rows[at].astype(F32) + column * job.result()).astype(BF16)
+        job.finish()
+        for copy in last_copies(piece):
+            copy.start()
 
     def step(op, carry):
         layer, block = at_step(op)
@@ -1208,7 +1178,7 @@
             for copy in weight_loads(0):
                 copy.wait()
 
-        @pl.when(op == 7)
+        @pl.when((layer == 0) & (block == x))
         def _():
             second_copy.start()
             swap.start()
@@ -1245,8 +1215,16 @@
             def _():
                 gather_of(5 - op).relay()
 
+            @pl.when(op == 7)
+            def _():
+                last_sums(0).relay()
+                parts[0].core_sum(0).finish()
+                pl.semaphore_wait(y_free, 2)
+                parts[0].y_sum(0).start()
+
             @pl.when(op == 4)
             def _():
+                first_load.wait()
                 for of_part in parts:
                     of_part.core_sum(1).finish()
                     of_part.y_sum(1).start()
@@ -1268,6 +1246,24 @@
                 for device in around(y, at_y):
                     pl.semaphore_signal(y_free, inc=1, device_id=device, device_id_type=MESH)
 
+        turn = ((0,), (0,))
+
+        def add_out():
+            for index in range(total.shape[0] // ROWS):
+                rows = slice(index * ROWS, (index + 1) * ROWS)
+                total[rows, wide:] += mm(e_stage[slot, :, rows], mixed[...], turn)
+
+        def send_on(of_part):
+            of_part.flush(total)
+            of_part.core_sum(layer).start()
+
+        @pl.when(op == 7)
+        def _():
+            mix_rows(layer_sizes, scales.at[layer, block], few.at[layer], stage.at[slot], mixed)
+            add_out()
+            pl.semaphore_wait(core_free, 1)
+            send_on(parts[0])
+
         backward_block(layer_sizes, block == 3, e, scales.at[layer, block], w_in[layer].reshape(e.shape[1], -1),
                        w_out[layer].reshape(e.shape[1], -1), few.at[layer],
                        selector[...], collector[...], stage.at[slot], p_stage.at[slot], state_stage.at[slot],
@@ -1278,79 +1274,118 @@
         def _():
             finish_sums(op - 1)
 
-        turn = ((0,), (0,))
-        wide = split + LANES
+        @pl.when(op >= 6)
+        def _():
+            last_sums(op - 6).start()
+
+        @pl.when(op < 7)
+        def _():
+            add_out()
+
         for index in range(total.shape[0] // ROWS):
             rows = slice(index * ROWS, (index + 1) * ROWS)
-            total[rows, :wide] += mm(norm_stage[slot, :, rows], grad[...], turn)
-            total[rows, wide:] += mm(e_stage[slot, :, rows], mixed[...], turn)
+            total[rows, middle_at:wide] += mm(norm_stage[slot, :, rows], grad[:, middle_at:], turn)
 
         @pl.when(op == 3)
         def _():
-            for of_part in parts:
-                of_part.flush(total)
-                of_part.core_sum(1).start()
+            send_on(parts[0])
+
+        @pl.when(block == 0)
+        def _():
+            send_on(parts[1])
+
+        for index in range(total.shape[0] // ROWS):
+            rows = slice(index * ROWS, (index + 1) * ROWS)
+            total[rows, :middle_at] += mm(norm_stage[slot, :, rows], grad[:, :middle_at], turn)
+
+        @pl.when(block == 0)
+        def _():
+            send_on(parts[2])
+
+        @pl.when(op == 3)
+        def _():
             total[...] = jnp.zeros_like(total)
 
         return carry
 
     lax.fori_loop(0, 8, step, 0)
-    pl.semaphore_wait(core_free, 1)
-    for of_part in parts:
-        of_part.flush(total)
-        of_part.core_sum(0).start()
-    pl.semaphore_wait(y_free, 2)
-    last_sums.start()
     sums_of(7).relay()
+    last_sums(1).relay()
+    last_sums(2).start()
+    last_sums(3).start()
     y_sums = [of_part.y_sum(0) for of_part in parts]
     z_sums = [of_part.z_sum() for of_part in parts]
-    for of_part, job in zip(parts, y_sums):
+    for of_part, job in zip(parts[1:], y_sums[1:]):
         of_part.core_sum(0).finish()
         job.start()
+    y_sums[0].relay()
     finish_sums(7)
-    gradient = Deliver(0, low_grad, first_grad, is_, ig, load.at[5])
-    gradient.start()
     for layer in range(2):
         width = few_grad.shape[2] - lead
         few_grad[layer, 6:7, lead:] = norm_grad[layer, 0:1, :width]
         few_grad[layer, 7:8, :] = norm_grad[layer, 0:1, width:]
     few_core = remote(few_grad, pair_few, (fs, fr), 0, at_core(1 - core))
     few_core.start()
-    y_sums[0].relay()
+    y_sums[0].wait()
+    parts[0].to_z(y_sums[0])
+    z_sums[0].start()
+    y_sums[1].relay()
+    y_sums[2].relay()
     few_core.wait()
     few_grad[...] = few_grad[...] + pair_few[...]
     few_y = Everyone(y, at_y, lambda to: few_grad, lambda me: y_few.at[me], (hs, hr))
     few_y.start()
-    last_sums.relay()
-    y_sums[0].wait()
-    parts[0].to_z(y_sums[0])
-    z_sums[0].start()
-    y_sums[1].relay()
+    for block in range(4):
+        hand_over(block).wait()
+    deliveries = [
+        Everyone(x, at_x, lambda to, sequence=sequence: both_grad.at[sequence, to],
+                 lambda me, sequence=sequence: first_grad.at[sequence, me], [sem.at[sequence] for sem in (ds, dr)])
+        for sequence in range(2)
+    ]
+    kept = [pltpu.make_async_copy(both_grad.at[sequence, x], first_grad.at[sequence, x], load.at[5 + 28 * sequence])
+            for sequence in range(2)]
+    for copy in deliveries + kept:
+        copy.start()
+    finish_last(0)
+    last_sums(2).relay()
+    finish_last(1)
+    z_sums[0].relay()
+    y_sums[1].wait()
+    parts[1].to_z(y_sums[1])
+    z_sums[1].start()
+    last_sums(3).relay()
+    finish_last(2)
     few_y.wait()
     y_few[y] = few_grad[...]
     few_grad[...] = (y_few[0] + y_few[1]) + (y_few[2] + y_few[3])
     few_z = Everyone(z, at_z, lambda to: few_grad.at[to % 2], lambda me: z_few.at[me], (js, jr))
     few_z.start()
-    z_sums[0].relay()
+    y_sums[2].wait()
+    parts[2].to_z(y_sums[2])
+    z_sums[2].start()
+    z_sums[1].relay()
+    finish_last(3)
     few_z.wait()
     z_few[z] = few_grad[pipe]
     few_sum[...] = (z_few[0] + z_few[1]) + (z_few[2] + z_few[3])
     x_few[x] = few_sum[...]
     few_x = Everyone(x, at_x, lambda to: few_sum, lambda me: x_few.at[me], (ks, kr))
     few_x.start()
-    finish_last()
-    z_sums[0].wait()
     rows = parts[0].z_blocks.shape[2]
-    for half in range(2):
-        large[half * rows : (half + 1) * rows, ends[0]] = z_sums[0].result(half)
+
+    def keep(at):
+        z_sums[at].wait()
+        for half in range(2):
+            large[half * rows : (half + 1) * rows, ends[at]] = z_sums[at].result(half)
+
+    keep(0)
+    z_sums[2].relay()
+    keep(1)
     state_rows = 2 * rows // 4
     for block in range(4):
         state_parts[0, block] = large[block * state_rows : (block + 1) * state_rows, 2 * inner : split]
     state_x = Everyone(x, at_x, lambda to: state_parts.at[0, to], lambda me: state_parts.at[1, me], (ws, wr))
     state_x.start()
-    y_sums[1].wait()
-    parts[1].to_z(y_sums[1])
-    z_sums[1].start()
     few_x.wait()
     few_shared[...] = (x_few[0] + x_few[1]) + (x_few[2] + x_few[3])
     state_x.wait()
@@ -1358,17 +1393,16 @@
     for step_at in every:
         total_state = total_state + state_parts[1, (x + step_at) % 4]
     state_grad[...] = total_state
-    z_sums[1].relay()
+    keep(2)
     second_copy.wait()
     swap.wait()
     first_copy.wait()
     first_swap.wait()
-    last_copy.wait()
-    last_swap.wait()
-    gradient.wait()
-    z_sums[1].wait()
-    for half in range(2):
-        large[half * rows : (half + 1) * rows, ends[1]] = z_sums[1].result(half)
+    for piece in range(4):
+        for copy in last_copies(piece):
+            copy.wait()
+    for copy in deliveries + kept:
+        copy.wait()
     for job in y_sums + z_sums:
         job.finish()
 
@@ -1381,7 +1415,7 @@
     lead = conv - (width - conv)
     split = 2 * inner + pair
     piece = weights_in.shape[4]
-    layout = [WeightParts.scratch(piece, pair + LANES + inner), WeightParts.scratch(piece, 2 * inner)]
+    layout = [WeightParts.scratch(piece, columns) for columns in (inner, inner + LANES, inner + pair)]
     columns = weights_in.shape[5] + inner
     chunks = ROWS // CHUNK
     selector, collector = constants(inner, heads)
@@ -1422,14 +1456,16 @@
             pltpu.VMEM((ROWS, inner), BF16),
             pltpu.VMEM((blocks, 8, LANES), F32),
             pltpu.VMEM((blocks, quarter, width), F32),
-            pltpu.VMEM((blocks, quarter, width), BF16),
+            pltpu.VMEM((2, blocks, quarter, width), BF16),
             pltpu.VMEM((2,) + few_shape, F32),
             pltpu.VMEM((2, 8, width), F32),
             pltpu.VMEM((width, columns), F32),
         ]
-        + scatter_buffers(ROWS // 2, width)
         + [
-            pltpu.VMEM((4, ROWS // 2, width), BF16),
+            pltpu.VMEM((4, 2) + half, BF16),
+            pltpu.VMEM((2, 2) + half, BF16),
+            pltpu.VMEM((4, 2, 2) + half, BF16),
+            pltpu.VMEM((4, 4) + half, BF16),
             pltpu.VMEM((ROWS, width), BF16),
             pltpu.VMEM((2,) + few_shape, F32),
             pltpu.VMEM((4, 2) + few_shape, F32),
@@ -1441,9 +1477,9 @@
             pltpu.VMEM((ROWS + 8, conv), F32),
         ]
         + semaphores(8, 6) + semaphores(4, 6) + semaphores(4, 3)
-        + dma(6) + dma(1) + dma(2) + dma(1) + dma(3) + dma(3) + dma(3) + dma(3)
-        + [pltpu.SemaphoreType.DMA((4,)), pltpu.SemaphoreType.DMA((8,))]
-        + [pltpu.SemaphoreType.DMA((5, 2)), pltpu.SemaphoreType.DMA((17,))]
+        + semaphores(4, 6) + dma(4) + dma(2) + dma(1) + dma(3) + dma(3) + dma(3) + dma(3)
+        + dma(4) + semaphores(2, 3)
+        + [pltpu.SemaphoreType.DMA((5, 2)), pltpu.SemaphoreType.DMA((34,))]
         + [pltpu.SemaphoreType.REGULAR, pltpu.SemaphoreType.REGULAR]
         + flat([of_part[0] for of_part in layout])
         + flat([of_part[1] for of_part in layout]),

time: 238 us -> 231 us (0.971)
  Pallas kernels: 237 us -> 230 us
    pallas_call x1, Pallas kernels: 129 us -> 122 us  [backward_all(): pl.pallas_call(partial(backward_all_kernel, (inner, pair, heads, lead, wh...]
where the time goes in v6:
time: 231 us
  Pallas kernels  230 us (100%)
    pallas_call x1, Pallas kernels, backward_all(): pl.pallas_call(partial(backward_all_kernel, (inner, pair, heads, lead, wh...  122 us
    pallas_call x1, Pallas kernels, forward_all(): pl.pallas_call(partial(forward_all_kernel, (inner, pair, heads, lead, who...  103 us
    pallas_call x1, Pallas kernels, finish_call(): pl.pallas_call(partial(finish_kernel, (inner, pair, heads, lead)), grid=(...  5.27 us

profile of v6, /device:TPU:0, one launch (start us, length us, event | category | flops | bytes accessed | tf_op | source)
XLA Modules:
  0.0 231.2 jit_solution(4228260541312244967)
XLA Ops:
  0.6 102.9 %forward_layers.1 = (f32[2,8,768]{2,1,0:T(8,128)}, bf16[2,2,4,2,64,1408]{5,4,3,2,1,0:T(8,128)(2,1)}, bf16[2,2,4,2,64,512]{5,4,3,2,1,0:T(8,128)(2,1)}, bf16[1024,...) custom-call(bf16[2,2,128,1024]{3,2,1,0:T(8,128)(2,1)} %bitcast.11, ...), custom_call_target="tpu_custom_call" | custom-call | tf_op jit(solution)/shard_map/forward_layers/pallas_call | solution.py:736
  103.6 122.2 %backward_layers.1 = (bf16[2,256,1024]{2,1,0:T(8,128)(2,1)}, bf16[2,256,1024]{2,1,0:T(8,128)(2,1)}, bf16[2,4,64,1024]{3,2,1,0:T(8,128)(2,1)}, bf16[2,256,1024]{2...) custom-call(bf16[1024,1024]{1,0:T(8,128)(2,1)} %get-tuple-element.47.errors_la, ...), custom_call_target="tpu_custom_call" | custom-call | tf_op jit(solution)/shard_map/backward_layers/pallas_call | solution.py:1427
  225.8 5.3 %outputs.1 = (f32[1,2,256,1024]{3,2,1,0:T(8,128)}, f32[1,2,256,1024]{3,2,1,0:T(8,128)}, f32[1,1024]{1,0:T(1,128)}, f32[1,64,2,512]{3,2,1,0:T(2,128)}, f32[1,16,2...) custom-call(bf16[2,256,1024]{2,1,0:T(8,128)(2,1)} %get-tuple-element, ...), custom_call_target="tpu_custom_call" | custom-call | tf_op jit(solution)/shard_map/outputs/pallas_call | solution.py:1546

commit v7 on v6

--- a/solution.py
+++ b/solution.py
@@ -655,7 +655,6 @@
 
             @pl.when(op == 1)
             def _():
-                e_ring.relay()
                 rings[1].relay()
 
             @pl.when((op >= 1) & (op < 5))
@@ -694,6 +693,10 @@
         @pl.when(op < 4)
         def _():
             sums_of(op).start()
+
+        @pl.when(op == 0)
+        def _():
+            e_ring.relay()
 
         @pl.when(op >= 4)
         def _():
@@ -1270,10 +1273,6 @@
                        part.at[op % 3], grad, mixed, few_grad.at[layer], state, later, pad, serve)
         sums_of(op).start()
 
-        @pl.when(op >= 1)
-        def _():
-            finish_sums(op - 1)
-
         @pl.when(op >= 6)
         def _():
             last_sums(op - 6).start()
@@ -1293,6 +1292,10 @@
         @pl.when(block == 0)
         def _():
             send_on(parts[1])
+
+        @pl.when(op >= 1)
+        def _():
+            finish_sums(op - 1)
 
         for index in range(total.shape[0] // ROWS):
             rows = slice(index * ROWS, (index + 1) * ROWS)

time: 231 us -> 229 us (level)
    pallas_call x1, Pallas kernels: 122 us -> 120 us  [backward_all(): pl.pallas_call(partial(backward_all_kernel, (inner, pair, heads, lead, wh...]
where the time goes in v7:
time: 229 us
  Pallas kernels  228 us (100%)
    pallas_call x1, Pallas kernels, backward_all(): pl.pallas_call(partial(backward_all_kernel, (inner, pair, heads, lead, wh...  120 us
    pallas_call x1, Pallas kernels, forward_all(): pl.pallas_call(partial(forward_all_kernel, (inner, pair, heads, lead, who...  103 us
    pallas_call x1, Pallas kernels, finish_call(): pl.pallas_call(partial(finish_kernel, (inner, pair, heads, lead)), grid=(...  5.27 us

profile of v7, /device:TPU:0, one launch (start us, length us, event | category | flops | bytes accessed | tf_op | source)
XLA Modules:
  0.0 228.8 jit_solution(4141810025637652831)
XLA Ops:
  0.6 103.0 %forward_layers.1 = (f32[2,8,768]{2,1,0:T(8,128)}, bf16[2,2,4,2,64,1408]{5,4,3,2,1,0:T(8,128)(2,1)}, bf16[2,2,4,2,64,512]{5,4,3,2,1,0:T(8,128)(2,1)}, bf16[1024,...) custom-call(bf16[2,2,128,1024]{3,2,1,0:T(8,128)(2,1)} %bitcast.11, ...), custom_call_target="tpu_custom_call" | custom-call | tf_op jit(solution)/shard_map/forward_layers/pallas_call | solution.py:739
  103.6 119.7 %backward_layers.1 = (bf16[2,256,1024]{2,1,0:T(8,128)(2,1)}, bf16[2,256,1024]{2,1,0:T(8,128)(2,1)}, bf16[2,4,64,1024]{3,2,1,0:T(8,128)(2,1)}, bf16[2,256,1024]{2...) custom-call(bf16[1024,1024]{1,0:T(8,128)(2,1)} %get-tuple-element.47.errors_la, ...), custom_call_target="tpu_custom_call" | custom-call | tf_op jit(solution)/shard_map/backward_layers/pallas_call | solution.py:1430
  223.3 5.3 %outputs.1 = (f32[1,2,256,1024]{3,2,1,0:T(8,128)}, f32[1,2,256,1024]{3,2,1,0:T(8,128)}, f32[1,1024]{1,0:T(1,128)}, f32[1,64,2,512]{3,2,1,0:T(2,128)}, f32[1,16,2...) custom-call(bf16[2,256,1024]{2,1,0:T(8,128)(2,1)} %get-tuple-element, ...), custom_call_target="tpu_custom_call" | custom-call | tf_op jit(solution)/shard_map/outputs/pallas_call | solution.py:1549
